TPU v7x, 128 devices: a whole 4x4x4 slice. The times are simulated.
128 devices in a mesh: traj: 8 (over x, core), tm: 16 (over y, z).
Axes of the slice: x: 4, y: 4, z: 4, core: 2. Of those that a mesh axis runs over, the one named last changes fastest.
Arguments:
- frames: bfloat16 [8, 4096, 4096], P('traj', 'tm'), may hold values from -60 to 60
- w_in: bfloat16 [4096, 512], replicated, may hold values from -0.0625 to 0.0625
- b_in: float32 [512], replicated, may hold values from -3 to 3
- w_conv: bfloat16 [3, 1024, 512], replicated, may hold values from -0.5 to 0.5
- b_conv: float32 [3, 512], replicated, may hold values from -3 to 3
Outputs:
- score: float32 [], replicated
- grad_w_in: float32 [4096, 512], replicated
- grad_b_in: float32 [512], replicated
- grad_w_conv: float32 [3, 1024, 512], replicated
- grad_b_conv: float32 [3, 512], replicated
All inputs are finite; a program needn't handle non-finite values.
Results may differ from a plain program's by a relative error of at most 0.012.
Values may be sent and summed in bfloat16 or wider, within the bound.
No kernel may reach another device: no remote copies, remote signals or barrier semaphores. Data moves between devices by JAX's collectives and lax.ppermute only.
A program may use at most 128 MiB of HBM per device.

v0:
```python
import jax
import jax.numpy as jnp
from jax import lax
from jax.sharding import PartitionSpec as P

NL = 3
NS_IT = 2
LAG = 16


RIDGE = 0.0001


def from_behind(value, axis, steps):
    count = lax.axis_size(axis)
    initial, last = (max(0, -steps), min(count, count - steps))
    return lax.ppermute(value, axis, [(source, source + steps) for source in range(initial, last)])


def matmul_hi(first_mat, second_mat):
    return jnp.dot(
        first_mat, second_mat, precision=lax.Precision.HIGHEST, preferred_element_type=jnp.float32
    )


def gram_hi(first_mat, second_mat):
    return lax.dot_general(
        first_mat,
        second_mat,
        (((0,), (0,)), ((), ())),
        precision=lax.Precision.HIGHEST,
        preferred_element_type=jnp.float32,
    )


def inv_sqrt(matrix):
    unit = jnp.eye(matrix.shape[0], dtype=jnp.float32)
    shifted = matrix + RIDGE * unit
    norm_scale = jnp.sqrt(jnp.sum(shifted * shifted))
    approx = shifted / norm_scale
    inverse = unit
    for sweep in range(NS_IT):
        mixing = 1.5 * unit - 0.5 * matmul_hi(inverse, approx)
        approx = matmul_hi(approx, mixing)
        inverse = matmul_hi(mixing, inverse)
    return inverse / jnp.sqrt(norm_scale)


def vamp_score(cov_early, cov_cross, cov_later):
    koopman = matmul_hi(matmul_hi(inv_sqrt(cov_early), cov_cross), inv_sqrt(cov_later))
    return 1.0 + jnp.sum(koopman * koopman)


def per_device(frames, w_in, b_in, w_conv, b_conv):
    frames = frames[0]
    row_count, feature_dim = frames.shape
    channels = w_in.shape[1]
    segment = lax.axis_index("tm")
    segments = lax.axis_size("tm")
    stored = []
    squash0 = jnp.tanh(jnp.dot(frames, w_in, preferred_element_type=jnp.float32) + b_in)
    hidden = squash0.astype(jnp.bfloat16)
    for layer_idx in range(NL):
        dilation = 2**layer_idx
        history = from_behind(hidden[row_count - dilation :], "tm", 1)
        joined = jnp.concatenate(
            [hidden, jnp.concatenate([history, hidden[: row_count - dilation]], axis=0)], axis=1
        )
        squashed = jnp.tanh(
            jnp.dot(joined, w_conv[layer_idx], preferred_element_type=jnp.float32)
            + b_conv[layer_idx]
        )
        stored.append((joined, squashed))
        hidden = (hidden.astype(jnp.float32) + squashed).astype(jnp.bfloat16)
    upcoming = from_behind(hidden[:LAG], "tm", -1)
    is_last = segment == segments - 1
    row_ids = jnp.arange(row_count)
    pair_mask = jnp.where(jnp.logical_and(is_last, row_ids >= row_count - LAG), 0.0, 1.0)[
        :, None
    ].astype(jnp.float32)
    early_rows = hidden.astype(jnp.float32) * pair_mask
    later_rows = jnp.concatenate([hidden[LAG:], upcoming], axis=0).astype(jnp.float32) * pair_mask
    pair_count = lax.axis_size("traj") * (row_count * segments - LAG)
    totals = lax.psum((jnp.sum(early_rows, axis=0), jnp.sum(later_rows, axis=0)), ("traj", "tm"))
    centred_early = (early_rows - totals[0] / pair_count) * pair_mask
    centred_later = (later_rows - totals[1] / pair_count) * pair_mask
    moments = lax.psum(
        (
            gram_hi(centred_early, centred_early),
            gram_hi(centred_early, centred_later),
            gram_hi(centred_later, centred_later),
        ),
        ("traj", "tm"),
    )
    cov_early = moments[0] / pair_count
    cov_cross = moments[1] / pair_count
    cov_later = moments[2] / pair_count
    score, pullback = jax.vjp(vamp_score, cov_early, cov_cross, cov_later)
    grad_early, grad_cross, grad_later = pullback(jnp.ones_like(score))
    dearly = (
        matmul_hi(centred_early, grad_early + grad_early.T) + matmul_hi(centred_later, grad_cross.T)
    ) / pair_count
    dlater = (
        matmul_hi(centred_early, grad_cross) + matmul_hi(centred_later, grad_later + grad_later.T)
    ) / pair_count
    arrived = from_behind(dlater[row_count - LAG :].astype(jnp.bfloat16), "tm", 1).astype(
        jnp.float32
    )
    hidden_grad = dearly + jnp.concatenate([arrived, dlater[: row_count - LAG]], axis=0)
    weight_grads = []
    bias_grads = []
    for layer_idx in reversed(range(NL)):
        dilation = 2**layer_idx
        joined, squashed = stored[layer_idx]
        pre_grad = (hidden_grad * (1.0 - squashed * squashed)).astype(jnp.bfloat16)
        weight_grads.insert(
            0,
            lax.dot_general(
                joined, pre_grad, (((0,), (0,)), ((), ())), preferred_element_type=jnp.float32
            ),
        )
        bias_grads.insert(0, jnp.sum(pre_grad.astype(jnp.float32), axis=0))
        input_grad = lax.dot_general(
            pre_grad,
            w_conv[layer_idx],
            (((1,), (1,)), ((), ())),
            preferred_element_type=jnp.float32,
        )
        carried = from_behind(input_grad[:dilation, channels:], "tm", -1)
        hidden_grad = (
            hidden_grad
            + input_grad[:, :channels]
            + jnp.concatenate([input_grad[dilation:, channels:], carried], axis=0)
        )
    pre_grad0 = (hidden_grad * (1.0 - squash0 * squash0)).astype(jnp.bfloat16)
    local_b_in = jnp.sum(pre_grad0.astype(jnp.float32), axis=0)
    stacked_w = jnp.stack(weight_grads)
    stacked_b = jnp.stack(bias_grads)
    local_w_in = lax.dot_general(
        frames, pre_grad0, (((0,), (0,)), ((), ())), preferred_element_type=jnp.float32
    )
    grad_w_in, grad_b_in, grad_w_conv, grad_b_conv = lax.psum(
        (local_w_in, local_b_in, stacked_w, stacked_b), ("traj", "tm")
    )
    return (score, grad_w_in, grad_b_in, grad_w_conv, grad_b_conv)


def solution(mesh):
    return jax.shard_map(
        per_device,
        mesh=mesh,
        in_specs=(P("traj", "tm", None), P(), P(), P(), P()),
        out_specs=(P(), P(), P(), P(), P()),
        check_vma=False,
    )
```

profile of v0, /device:TPU:1, one launch (start us, length us, event | category | flops | bytes accessed | tf_op | source)
XLA Modules:
  0.0 631.7 jit_solution(18159884056216987852)
XLA Ops:
  8.8 4.4 fusion.96
  13.2 4.4 collective-permute-start
  19.5 3.6 collective-permute-start.1
  25.1 3.6 collective-permute-start.2
  29.5 2.5 add_convert_fusion
  33.3 3.4 collective-permute-done.3
  36.9 75.7 %all-reduce.1 = (f32[512]{0:T(512)S(1)}, f32[512]{0:T(512)S(1)}) all-reduce(f32[512]{0:T(512)S(1)} %get-tuple-element.11, f32[512]{0:T(512)S(1)} %get-tuple-element.10), channel_id=1, replica_groups=mesh['traj'=8,'tm'=16] {'traj','tm'}, use_global_device_ids=true, to_apply=%region_5.6 | all-reduce | flops 1024 | bytes 8192 | tf_op jit(solution)/shard_map/psum | solution.py:84
  114.8 2.2 fusion.57
  119.6 150.5 %all-reduce.9.cloned.1.call-done = (f32[512,512]{1,0:T(8,128)}, f32[512,512]{1,0:T(8,128)}, f32[512,512]{1,0:T(8,128)}) async-done(((f32[512,512]{1,0:T(8,128)}, f32[512,512]{1,0:T(8,128)}, f32[512,512]{1,0:T(8,128)}), (f32[512,512]{1,0:T(8,128)}, f32[512,512]{1,0:T(8,128)}, f32[512,512]{1,0:T(8,128)})) %all-reduce.9.cloned.1.call-update) | async-done | bytes 3145744 | tf_op jit(solution)/shard_map/psum | solution.py:87
  272.9 2.5 select_subtract_fusion.3
  276.4 2.9 fusion.90
  282.2 2.5 select_subtract_fusion.1
  286.6 3.0 fusion.91
  289.6 3.2 select_subtract_fusion.2
  292.9 2.8 fusion.97
  295.7 2.3 select_subtract_fusion
  299.0 2.8 fusion.98
  301.9 3.5 fusion.42
  306.4 2.6 multiply_reduce_fusion.4
  310.0 2.9 fusion.38
  313.0 4.6 multiply_reduce_fusion.1
  317.5 3.1 fusion.66
  320.6 2.9 fusion.5
  323.5 4.4 fusion.63
  328.0 4.5 multiply_reduce_fusion.3
  332.6 2.8 fusion.64
  335.4 2.9 fusion.8
  338.4 3.1 fusion.61
  341.6 4.0 fusion.100
  348.5 3.5 fusion.4
  354.7 7.2 %multiply_reduce_fusion = (f32[]{:T(128)}, f32[512,512]{1,0:T(8,128)}) fusion(f32[]{:T(128)S(6)} %div.109, f32[512,512]{1,0:T(8,128)} %get-tuple-element.20, f32[512,512]{1,0:T(8,128)} %fusion.30, f32[512,512]{1,0:T(8,128)} %copy-done.20, f32[512,512]{1,0:T(8,128)} %copy-done.23), kind=kOutput, calls=%fused_computation.58 | convolution fusion | flops 1612709888 | bytes 5242888 | tf_op jit(solution)/shard_map/transpose(jvp())/dot_general | solution.py:21
  362.6 2.8 add_add_fusion
  365.4 2.5 copy.11
  367.9 3.1 fusion.13
  371.8 2.8 collective-permute-start.4
  374.7 3.2 fusion.99
  380.9 3.5 fusion.7
  387.1 7.1 %multiply_reduce_fusion.2 = (f32[]{:T(128)}, f32[512,512]{1,0:T(8,128)}) fusion(f32[]{:T(128)S(6)} %div.102, f32[512,512]{1,0:T(8,128)S(1)} %copy-done.4, f32[512,512]{1,0:T(8,128)} %fusion.32, f32[512,512]{1,0:T(8,128)} %copy-done.21, f32[512,512]{1,0:T(8,128)} %copy-done.22), kind=kOutput, calls=%fused_computation.60 | convolution fusion | flops 1612709888 | bytes 5242888 | tf_op jit(solution)/shard_map/transpose(jvp())/dot_general | solution.py:21
  398.0 2.5 fusion.20
  401.6 2.3 convert_reduce_fusion
  406.3 2.5 collective-permute-done.5
  411.4 2.5 collective-permute-done.6
  416.5 3.4 pad_maximum_fusion
  420.2 4.7 convolution_bitcast_fusion
  425.6 75.2 %all-reduce = (f32[512]{0:T(512)}, f32[3,512]{1,0:T(4,128)}) all-reduce(f32[512]{0:T(512)S(1)} %get-tuple-element.29, f32[3,512]{1,0:T(4,128)S(1)} %pad_maximum_fusion.2), channel_id=1, replica_groups=mesh['traj'=8,'tm'=16] {'traj','tm'}, use_global_device_ids=true, to_apply=%region_16.17 | all-reduce | flops 2048 | bytes 16384 | tf_op jit(solution)/shard_map/psum | solution.py:142
  500.8 107.6 %all-reduce.7.cloned.1.call-done = (f32[4096,512]{0,1:T(8,128)}, f32[3,1024,512]{2,1,0:T(8,128)}) async-done(((f32[4096,512]{0,1:T(8,128)}, f32[3,1024,512]{2,1,0:T(8,128)}), (f32[4096,512]{0,1:T(8,128)}, f32[3,1024,512]{2,1,0:T(8,128)})) %all-reduce.7.cloned.1.call-update) | async-done | bytes 14680080 | tf_op jit(solution)/shard_map/psum | solution.py:142
  608.4 8.9 %copy.12 = f32[4096,512]{1,0:T(8,128)} copy(f32[4096,512]{0,1:T(8,128)} %get-tuple-element.16) | data formatting | bytes 16777216
  617.3 6.2 copy.18
  (139 shorter events, 45.2 us)
Async XLA Ops:
  7.2 1.6 copy-start
  7.2 10.4 %copy-start.40 = (f32[3,512]{1,0:T(4,128)S(1)}, f32[3,512]{1,0:T(4,128)}, u32[]{:S(2)}) copy-start(f32[3,512]{1,0:T(4,128)} %param.9) | copy-start | bytes 18436
  7.2 262.9 %all-reduce.9.cloned.1.call-start = ((), (), s32[]{:S(2)}) async-start(), calls=%async_computation.1 | async-start | bytes 6291456 | tf_op jit(solution)/shard_map/psum | solution.py:87
  8.8 9.5 %copy-start.24 = (bf16[3,1024,512]{2,1,0:T(8,128)(2,1)S(1)}, bf16[3,1024,512]{2,1,0:T(8,128)(2,1)}, u32[]{:S(2)}) copy-start(bf16[3,1024,512]{2,1,0:T(8,128)(2,1)} %param.8) | copy-start | bytes 9437188
  13.2 12.0 %copy-start.29 = (bf16[256,512]{1,0:T(8,128)(2,1)}, bf16[256,512]{1,0:T(8,128)(2,1)S(1)}, u32[]{:S(2)}) copy-start(bf16[256,512]{1,0:T(8,128)(2,1)S(1)} %get-tuple-element.34) | copy-start | bytes 786436
  13.2 5.1 collective-permute-start
  19.5 5.6 copy-start.31
  19.5 4.3 collective-permute-start.1
  25.1 8.1 %copy-start.27 = (bf16[256,512]{1,0:T(8,128)(2,1)}, bf16[256,512]{1,0:T(8,128)(2,1)S(1)}, u32[]{:S(2)}) copy-start(bf16[256,512]{1,0:T(8,128)(2,1)S(1)} %get-tuple-element.38) | copy-start | bytes 786436
  25.1 4.3 collective-permute-start.2
  32.0 4.7 collective-permute-start.3
  33.3 86.0 %copy-start.7 = (bf16[240,512]{1,0:T(8,128)(2,1)}, bf16[240,512]{1,0:T(8,128)(2,1)S(1)}, u32[]{:S(2)}) copy-start(bf16[240,512]{1,0:T(8,128)(2,1)S(1)} %slice.110) | copy-start | bytes 737284
  119.3 489.1 %all-reduce.7.cloned.1.call-start = ((), (), s32[]{:S(2)}) async-start(), calls=%async_computation | async-start | bytes 29360128 | tf_op jit(solution)/shard_map/psum | solution.py:142
  272.9 3.5 copy-start.3
  282.1 4.4 copy-start.5
  284.6 1.9 copy-start.23
  289.6 6.1 copy-start.1
  289.6 6.1 copy-start.17
  292.9 5.2 copy-start.9
  298.0 1.0 copy-start.11
  301.9 4.5 copy-start.13
  309.0 1.0 copy-start.34
  313.0 4.6 copy-start.12
  317.5 3.1 copy-start.2
  328.0 4.6 copy-start.10
  341.6 4.0 copy-start.18
  341.6 4.0 copy-start.19
  341.6 4.0 copy-start.36
  345.6 2.9 copy-start.20
  345.6 2.9 copy-start.6
  371.8 29.8 %collective-permute-start.4 = (bf16[16,512]{1,0:T(8,128)(2,1)S(1)}, bf16[16,512]{1,0:T(8,128)(2,1)S(1)}, u32[]{:S(2)}, u32[]{:S(2)}) collective-permute-start(bf16[16,512]{1,0:T(8,128)(2,1)S(1)} %slice.161), channel_id=1, source_target_pairs={{0,1},{1,2},{2,3},{3,4},{4,5},{5,6},{6,7},{7,8},{8,9},{9,10},{10,1... | collective-permute-start | bytes 49160 | tf_op jit(solution)/shard_map/ppermute | solution.py:17
  374.7 3.3 copy-start.15
  374.7 3.3 copy-start.16
  374.7 3.3 copy-start.35
  378.0 2.9 copy-start.21
  378.0 2.9 copy-start.4
  398.0 3.6 copy-start.8
  398.0 3.6 copy-start.14
  398.0 6.0 copy-start.25
  401.6 4.2 copy-start.28
  403.9 4.9 copy-start.38
  404.4 4.4 collective-permute-start.5
  406.2 4.7 copy-start.32
  409.1 4.8 copy-start.37
  409.6 4.4 collective-permute-start.6
  411.4 4.6 copy-start.30
  414.7 5.3 collective-permute-start.7
  416.5 3.5 copy-start.39
  (3 other events, 2.8 us)
Sparse Core Ops, SparseCore 0:
  119.5 150.6 all-reduce.8
  425.1 183.2 all-reduce.6
where the time goes:
time: 638 us; the launch traced here: 632 us
  waiting for transfers between devices  269 us (42%)
  blocking collectives  151 us (24%)
  matrix products  132 us (21%)
  local copies, waits for them, and re-layouts  25.8 us (4%)
  between operations  21.3 us (3%)
  starting transfers between devices  19.8 us (3%)
  other arithmetic  13.2 us (2%)
    psum x1, waiting for transfers between devices, per_device(): lax.psum((gram_hi(centred_early, centred_early), gram_hi(centred_early, c...  150 us
    dot_general x36, matrix products, matmul_hi(): jnp.dot(first_mat, second_mat, precision=lax.Precision.HIGHEST, preferred...  108 us
    psum x1, waiting for transfers between devices, per_device(): lax.psum((local_w_in, local_b_in, stacked_w, stacked_b), ('traj', 'tm'))  108 us
    psum x1, blocking collectives, per_device(): lax.psum((jnp.sum(early_rows, axis=0), jnp.sum(later_rows, axis=0)), ('tr...  75.7 us
    psum x1, blocking collectives, per_device(): lax.psum((local_w_in, local_b_in, stacked_w, stacked_b), ('traj', 'tm'))  75.2 us
    unnamed x84, local copies, waits for them, and re-layouts  20.6 us
    ppermute x8, starting transfers between devices, from_behind(): lax.ppermute(value, axis, [(source, source + steps) for source in range(i...  19.5 us
  transfers between devices with their start and end apart: 10, of which 8 were waited for; matrix products, arithmetic and copies ran while one was open for 5% of the time, Pallas kernels for 0%

commit v1 on v0

v1 whole, which is shorter than its diff:
```python
import functools

import jax
import jax.numpy as jnp
from jax import lax
from jax.experimental import pallas as pl
from jax.experimental.pallas import tpu as pltpu
from jax.sharding import Mesh, PartitionSpec as P

NL = 3
LAG = 16
RIDGE = 0.0001
HALO = 32
LANES = 128
BF = jnp.bfloat16
F32 = jnp.float32
PEERS = ("x", "tm")
HI = lax.Precision.HIGHEST
C0, C1, C2, C3, C4 = 2.25, -2.4375, 1.6875, -0.5625, 0.0625

NN = (((1,), (0,)), ((), ()))
NT = (((1,), (1,)), ((), ()))
TN = (((0,), (0,)), ((), ()))


def dot(a, b, dims=NN, precision=None):
    return lax.dot_general(a, b, dims, precision=precision, preferred_element_type=F32)


def split(a):
    hi = a.astype(BF)
    return hi, (a - hi.astype(F32)).astype(BF)


def dot3(a, b, dims=NN):
    return dot(a[0], b[0], dims) + (dot(a[0], b[1], dims) + dot(a[1], b[0], dims))


def swap_core(value):
    return lax.ppermute(value, "c", [(0, 1), (1, 0)])


def shift_segment(value, steps):
    count = lax.axis_size("tm")
    first, last = max(0, -steps), min(count, count - steps)
    return lax.ppermute(value, "tm", [(i, i + steps) for i in range(first, last)])


def exchange(value):
    return lax.all_to_all(value, PEERS, 0, 0, tiled=True)


def call(kernel, outs, *args, scratch=(), flops=0, moved=0):
    specs = [
        pl.BlockSpec(memory_space=pltpu.SMEM if a.dtype == jnp.int32 else pltpu.VMEM) for a in args
    ]
    return pl.pallas_call(
        kernel,
        out_shape=outs,
        in_specs=specs,
        out_specs=[pl.BlockSpec(memory_space=pltpu.VMEM) for _ in outs],
        scratch_shapes=list(scratch),
        compiler_params=pltpu.CompilerParams(vmem_limit_bytes=50 * 2**20),
        cost_estimate=pl.CostEstimate(flops=flops, bytes_accessed=moved, transcendentals=0),
    )(*args)


def sds(shape, dtype):
    return jax.ShapeDtypeStruct(shape, dtype)


def forward_kernel(dims, info, before, own, after, w, b, hid, sq, mine, other, means, mom):
    rows, ch, length, peers, piece = dims
    core, segment = info[0], info[1]
    ext = rows + 2 * HALO
    nb = ch // LANES
    t = segment * rows - HALO + lax.broadcasted_iota(jnp.int32, (ext, 1), 0)
    h = jnp.concatenate(
        [before[...].astype(F32), own[...].astype(F32), after[...].astype(F32)], axis=0
    )
    for layer in range(NL):
        hb = h.astype(BF)
        hid[layer] = hb
        hist = pltpu.roll(h, 2**layer, 0).astype(BF)
        s = jnp.tanh(dot(hb, w[layer, :ch]) + dot(hist, w[layer, ch:]) + b[layer : layer + 1])
        sq[layer] = s
        h = jnp.where(t >= 0, (h + s).astype(BF).astype(F32), 0.0)
    hid[NL] = h.astype(BF)
    tp = segment * rows + lax.broadcasted_iota(jnp.int32, (rows, 1), 0)
    pair = jnp.where(tp < length - LAG, 1.0, 0.0).astype(F32)
    last = segment == length // rows - 1
    count = jnp.where(last, rows - LAG, rows).astype(F32)
    early = h[HALO : HALO + rows] * pair
    later = h[HALO + LAG : HALO + LAG + rows] * pair
    mean_e = jnp.sum(early, axis=0, keepdims=True) / count
    mean_l = jnp.sum(later, axis=0, keepdims=True) / count
    means[...] = jnp.concatenate([mean_e, mean_l, jnp.zeros((6, ch), F32)], axis=0)
    ce = split((early - mean_e) * pair)
    cl = split((later - mean_l) * pair)
    left_e = jnp.concatenate([ce[0], ce[0], ce[1]], axis=0)
    left_l = jnp.concatenate([cl[0], cl[0], cl[1]], axis=0)
    right_e = jnp.concatenate([ce[0], ce[1], ce[0]], axis=0)
    right_l = jnp.concatenate([cl[0], cl[1], cl[0]], axis=0)
    mom[0] = dot(left_e, right_e, TN)
    mom[1] = dot(left_e, right_l, TN)
    mom[2] = dot(left_l, right_l, TN)
    half = ch // 2

    def pack(i, carry):
        at = pl.multiple_of(core * half + i * piece, piece)
        to = pl.multiple_of((1 - core) * half + i * piece, piece)
        for m in range(3):
            for j in range(nb):
                cols = slice(j * LANES, (j + 1) * LANES)
                put = slice(m * piece, (m + 1) * piece)
                mine[i * nb + j, put, :] = mom[m, pl.ds(at, piece), cols]
                other[i * nb + j, put, :] = mom[m, pl.ds(to, piece), cols].astype(BF)
        return carry

    lax.fori_loop(0, peers // nb, pack, 0)


def pair_kernel(dims, info, mine, got, means, sib, packed, turned):
    rows, ch, length, peers, piece = dims
    core, segment = info[0], info[1]
    nb = ch // LANES
    half = ch // 2
    last = segment == length // rows - 1
    weight = 0.5 * jnp.where(last, rows - LAG, rows).astype(F32)
    gap = means[...] - sib[...]
    mid = 0.5 * (means[...] + sib[...])
    turned[...] = gap.T * weight
    hi, lo = split(mid)
    tail = []
    for part in (hi.astype(F32), lo.astype(F32)):
        for k in range(2):
            for j in range(nb):
                tail.append(part[k : k + 1, j * LANES : (j + 1) * LANES])
    tail = jnp.concatenate(tail, axis=0).astype(BF)

    def pack(i, carry):
        at = pl.multiple_of(core * half + i * piece, piece)
        col = turned[pl.ds(at, piece), :]
        for j in range(nb):
            cols = slice(j * LANES, (j + 1) * LANES)
            p = i * nb + j
            for m, (a, c) in enumerate(((0, 0), (0, 1), (1, 1))):
                put = slice(m * piece, (m + 1) * piece)
                value = mine[p, put, :] + got[p, put, :].astype(F32)
                value = value + col[:, a : a + 1] * gap[c : c + 1, cols]
                packed[p, put, :] = value.astype(BF)
            packed[p, 3 * piece :, :] = tail
        return carry

    lax.fori_loop(0, peers // nb, pack, 0)


def merge_kernel(dims, info, arrived, cov, mean_all, flat, dev, square):
    rows, ch, length, peers, piece = dims
    core, peer = info[0], info[2]
    nb = ch // LANES
    segments = length // rows
    total = 2 * (peers // segments) * (length - LAG)
    body = 3 * piece

    def add(p, acc):
        z = arrived[p, body:, :].astype(F32)
        flat[pl.ds(pl.multiple_of(p * 2 * nb, 2 * nb), 2 * nb), :] = z[: 2 * nb] + z[2 * nb :]
        return acc + arrived[p, :body, :].astype(F32)

    within = lax.fori_loop(0, peers, add, jnp.zeros((body, LANES), F32))
    seg = lax.rem(lax.broadcasted_iota(jnp.int32, (peers, 1), 0), segments)
    counts = 2.0 * jnp.where(seg == segments - 1, rows - LAG, rows).astype(F32)
    mean_all[...] = jnp.zeros_like(mean_all)
    for k in range(2):
        for j in range(nb):
            cols = slice(j * LANES, (j + 1) * LANES)
            v = flat[pl.ds(k * nb + j, peers, stride=2 * nb), :]
            mean = jnp.sum(v * counts, axis=0, keepdims=True) / total
            mean_all[k : k + 1, cols] = mean
            dev[k, :, cols] = v - mean
    start = core * (ch // 2) + (peer // nb) * piece
    block = pl.multiple_of((start // LANES) * LANES, LANES)
    inside = pl.multiple_of(lax.rem(start, LANES), piece)
    here = pl.multiple_of(lax.rem(peer, nb) * LANES, LANES)
    for m, (a, c) in enumerate(((0, 0), (0, 1), (1, 1))):
        left = dev[a, :, pl.ds(block, LANES)] * counts
        square[m] = dot(left, dev[c, :, pl.ds(here, LANES)], TN, HI)
    between = jnp.concatenate([square[m, pl.ds(inside, piece), :] for m in range(3)], axis=0)
    value = ((within + between) / total).astype(BF)
    cov[...] = jnp.broadcast_to(value[None], cov.shape)


def score_kernel(dims, info, half_cov, other_cov, grads, score, cov):
    rows, ch, length, peers, piece = dims
    core = info[0]
    nb = ch // LANES
    half = ch // 2

    def place(i, carry):
        at = pl.multiple_of(core * half + i * piece, piece)
        to = pl.multiple_of((1 - core) * half + i * piece, piece)
        for m in range(3):
            for j in range(nb):
                cols = slice(j * LANES, (j + 1) * LANES)
                put = slice(m * piece, (m + 1) * piece)
                cov[m, pl.ds(at, piece), cols] = half_cov[i * nb + j, put, :].astype(F32)
                cov[m, pl.ds(to, piece), cols] = other_cov[i * nb + j, put, :].astype(F32)
        return carry

    lax.fori_loop(0, peers // nb, place, 0)
    row = lax.broadcasted_iota(jnp.int32, (ch, ch), 0)
    col = lax.broadcasted_iota(jnp.int32, (ch, ch), 1)
    unit = jnp.where(row == col, 1.0, 0.0).astype(F32)

    def forward(matrix):
        shifted = matrix + RIDGE * unit
        square = jnp.sum(shifted * shifted, keepdims=True)
        inv_scale = lax.rsqrt(square)
        a = shifted * inv_scale
        ab = a.astype(BF)
        a2 = dot(ab, ab)
        a2b = a2.astype(BF)
        poly = C0 * unit + C1 * a + C2 * a2 + dot(a2b, (C3 * a + C4 * a2).astype(BF))
        root = jnp.sqrt(inv_scale)
        return a, ab, a2b, poly, inv_scale, root, split(poly * root)

    def backward(a, ab, a2b, poly, inv_scale, root, grad):
        dscale = -0.5 * jnp.sum(grad * poly, keepdims=True) * root * inv_scale
        g = grad * root
        gb = g.astype(BF)
        y = dot(gb, ab)
        x = dot(a2b, gb)
        xs = x + x.T
        h = C2 * g + (0.5 * C3) * (y + y.T) + C4 * xs
        z = dot(ab, h.astype(BF))
        da = C1 * g + (0.5 * C3) * xs + z + z.T
        dscale = dscale - jnp.sum(da * a, keepdims=True) * inv_scale
        return da * inv_scale + dscale * a

    fe = forward(cov[0])
    fl = forward(cov[2])
    re, rl = fe[6], fl[6]
    c = split(cov[1])
    u = split(dot3(re, c))
    v = split(dot3(c, rl))
    k = dot3(u, rl)
    score[...] = jnp.broadcast_to(1.0 + jnp.sum(k * k, keepdims=True), score.shape)
    k2 = split(2.0 * k)
    gc = dot3(split(dot3(re, k2)), rl)
    grads[ch : 2 * ch] = gc.T.astype(BF)
    grads[2 * ch : 3 * ch] = gc.astype(BF)
    gre = dot3(k2, v, NT)
    grads[:ch] = backward(*fe[:6], gre + gre.T).astype(BF)
    grl = dot3(u, k2, TN)
    grads[3 * ch :] = backward(*fl[:6], grl + grl.T).astype(BF)


def backward_kernel(dims, info, hid, sq, sq0, frames, w, grads, mean_all, mine, other):
    rows, ch, length, peers, piece = dims
    core, segment = info[0], info[1]
    segments = length // rows
    features = frames.shape[1]
    half = ch // 2
    nh = half // LANES
    total = 2 * (peers // segments) * (length - LAG)
    grows = rows + 16
    t = segment * rows + lax.broadcasted_iota(jnp.int32, (grows, 1), 0)
    has_early = t < length - LAG
    has_later = jnp.logical_and(t >= LAG, t < length)
    out = hid[NL].astype(F32)
    base = out[HALO : HALO + grows]
    mean_e, mean_l = mean_all[0:1], mean_all[1:2]
    zero = jnp.zeros((1, ch), F32)
    consts = []
    for early_on in (True, False):
        left_e, left_l = mean_e, mean_l
        for _ in range(3):
            top_e, top_l = left_e.astype(BF).astype(F32), left_l.astype(BF).astype(F32)
            parts = [top_e, top_l, zero, zero] if early_on else [zero, zero, top_e, top_l]
            consts.append(jnp.concatenate(parts, axis=1))
            left_e, left_l = left_e - top_e, left_l - top_l
    consts = jnp.concatenate(consts + [jnp.zeros((10, 4 * ch), F32)], axis=0)
    lhs = jnp.concatenate(
        [
            jnp.where(has_early, base, 0.0),
            jnp.where(has_early, out[HALO + LAG : HALO + LAG + grows], 0.0),
            jnp.where(has_later, out[HALO - LAG : HALO - LAG + grows], 0.0),
            jnp.where(has_later, base, 0.0),
        ],
        axis=1,
    )
    lhs = jnp.concatenate([lhs, consts], axis=0).astype(BF)
    grad = dot(lhs, grads[...])
    off_early = grad[grows : grows + 1] + grad[grows + 1 : grows + 2] + grad[grows + 2 : grows + 3]
    off_later = grad[grows + 3 : grows + 4] + grad[grows + 4 : grows + 5] + grad[grows + 5 : grows + 6]
    grad = grad[:grows] - jnp.where(has_early, off_early, 0.0) - jnp.where(has_later, off_later, 0.0)
    grad = grad / total
    biases = [None] * (NL + 1)
    first = core == 0

    def halves(value):
        lo, hi = value[:, :half], value[:, half:]
        return jnp.where(first, lo, hi), jnp.where(first, hi, lo)

    def store(left, value, p0, count, size, at):
        for part, ref in zip(halves(value), (mine, other)):
            res = dot(left, part.astype(BF), TN).astype(BF)
            for j in range(nh):
                piece_j = res[:, j * LANES : (j + 1) * LANES].reshape(count, size, LANES)
                ref[p0 : p0 + count, at + j * size : at + (j + 1) * size, :] = piece_j

    in_size = features // peers
    conv_size = 2 * ch // peers
    for layer in reversed(range(NL)):
        step = 2**layer
        s = sq[layer, HALO : HALO + grows, :]
        pre = jnp.where(t < length, grad * (1.0 - s * s), 0.0).astype(BF)
        own = pre[:rows].astype(F32)
        biases[layer + 1] = jnp.sum(own, axis=0, keepdims=True)
        h = hid[layer].astype(F32)
        hist = pltpu.roll(h, step, 0)[HALO : HALO + rows].astype(BF)
        at = nh * in_size + layer * nh * conv_size
        count = ch // conv_size
        store(hid[layer, HALO : HALO + rows, :], own, 0, count, conv_size, at)
        store(hist, own, count, count, conv_size, at)
        back = dot(pre, w[layer, ch:], NT)
        grad = grad + dot(pre, w[layer, :ch], NT) + pltpu.roll(back, grows - step, 0)
    s = sq0[...]
    own = (grad[:rows] * (1.0 - s * s)).astype(BF).astype(F32)
    biases[0] = jnp.sum(own, axis=0, keepdims=True)
    tile = min(features, 512)
    for k in range(features // tile):
        count = tile // in_size
        store(frames[:, k * tile : (k + 1) * tile], own, k * count, count, in_size, 0)
    bias = jnp.concatenate(biases, axis=0)
    for part, ref in zip(halves(bias), (mine, other)):
        hi, lo = split(part)
        tail = []
        for value in (hi.astype(F32), lo.astype(F32)):
            for j in range(nh):
                tail.append(value[:, j * LANES : (j + 1) * LANES])
        tail = jnp.concatenate(tail, axis=0).astype(BF)
        at = ref.shape[1] - tail.shape[0]
        ref[:, at:, :] = jnp.broadcast_to(tail[None], (peers,) + tail.shape)


def add_kernel(nbias, mine, got, packed):
    body = packed.shape[1] - 2 * nbias
    a, b = mine[...].astype(F32), got[...].astype(F32)
    value = a + b
    packed[:, :body, :] = value[:, :body].astype(BF)
    bias = value[0, body : body + nbias] + value[0, body + nbias :]
    hi = bias.astype(BF).astype(F32)
    tail = jnp.concatenate([hi, bias - hi], axis=0).astype(BF)
    packed[:, body:, :] = jnp.broadcast_to(tail[None], (packed.shape[0],) + tail.shape)


def sum_kernel(arrived, tails, full, bias):
    peers = arrived.shape[0]

    def add(p, acc):
        return acc + arrived[p].astype(F32)

    value = lax.fori_loop(0, peers, add, jnp.zeros(arrived.shape[1:], F32), unroll=4)
    full[...] = jnp.broadcast_to(value.astype(BF)[None], full.shape)

    @pl.when(pl.program_id(0) == 0)
    def _():
        def add_tail(p, acc):
            return acc + tails[p].astype(F32)

        t = lax.fori_loop(0, peers, add_tail, jnp.zeros(tails.shape[1:], F32))
        n = t.shape[0] // 2
        bias[...] = t[:n] + t[n:]


def unpack_kernel(sizes, info, mine, got, bias, bias_got, w_in, w_conv, b_all):
    in_size, conv_size, nh = sizes
    first = info[0] == 0
    count = mine.shape[0]
    lo = jnp.where(first, mine[...].astype(F32), got[...].astype(F32))
    hi = jnp.where(first, got[...].astype(F32), mine[...].astype(F32))
    for side, value in enumerate((lo, hi)):
        for j in range(nh):
            cols = slice((side * nh + j) * LANES, (side * nh + j + 1) * LANES)
            part = value[:, j * in_size : (j + 1) * in_size]
            w_in[:, cols] = part.reshape(count * in_size, LANES)
            for layer in range(NL):
                at = nh * in_size + (layer * nh + j) * conv_size
                part = value[:, at : at + conv_size]
                w_conv[layer, :, cols] = part.reshape(count * conv_size, LANES)

    @pl.when(pl.program_id(0) == 0)
    def _():
        lo = jnp.where(first, bias[...], bias_got[...])
        hi = jnp.where(first, bias_got[...], bias[...])
        n = NL + 1
        for side, value in enumerate((lo, hi)):
            for j in range(nh):
                cols = slice((side * nh + j) * LANES, (side * nh + j + 1) * LANES)
                b_all[:, cols] = value[j * n : (j + 1) * n]


def per_device(frames, w_in, b_in, w_conv, b_conv):
    frames = frames[0]
    rows, features = frames.shape
    ch = w_in.shape[1]
    core = lax.axis_index("c")
    segment = lax.axis_index("tm")
    segments = lax.axis_size("tm")
    peers = lax.axis_size("x") * segments
    length = rows * segments
    nb = ch // LANES
    nh = nb // 2
    piece = (ch // 2) * nb // peers
    dims = (rows, ch, length, peers, piece)
    info = jnp.stack([core, segment, lax.axis_index("x") * segments + segment]).astype(jnp.int32)
    ext = rows + 2 * HALO

    squash0 = jnp.tanh(jnp.dot(frames, w_in, preferred_element_type=F32) + b_in)
    own = squash0.astype(BF)
    before = shift_segment(own[rows - HALO :], 1)
    after = shift_segment(own[:HALO], -1)
    hid, sq, mine, other, means = call(
        functools.partial(forward_kernel, dims),
        [
            sds((NL + 1, ext, ch), BF),
            sds((NL, ext, ch), F32),
            sds((peers, 3 * piece, LANES), F32),
            sds((peers, 3 * piece, LANES), BF),
            sds((8, ch), F32),
        ],
        info, before, own, after, w_conv, b_conv,
        scratch=[pltpu.VMEM((3, ch, ch), F32)],
    )
    (packed,) = call(
        functools.partial(pair_kernel, dims),
        [sds((peers, 3 * piece + 4 * nb, LANES), BF)],
        info, mine, swap_core(other), means, swap_core(means),
        scratch=[pltpu.VMEM((ch, 8), F32)],
    )
    cov, mean_all = call(
        functools.partial(merge_kernel, dims),
        [sds((peers, 3 * piece, LANES), BF), sds((8, ch), F32)],
        info, exchange(packed),
        scratch=[
            pltpu.VMEM((peers * 2 * nb, LANES), F32),
            pltpu.VMEM((2, peers, ch), F32),
            pltpu.VMEM((3, LANES, LANES), F32),
        ],
    )
    cov = exchange(cov)
    grads, score = call(
        functools.partial(score_kernel, dims),
        [sds((4 * ch, ch), BF), sds((8, LANES), F32)],
        info, cov, swap_core(cov),
        scratch=[pltpu.VMEM((3, ch, ch), F32)],
    )
    in_size = features // peers
    conv_size = 2 * ch // peers
    body = nh * (in_size + NL * conv_size)
    nbias = (NL + 1) * nh
    wide = body + 2 * nbias
    mine, other = call(
        functools.partial(backward_kernel, dims),
        [sds((peers, wide, LANES), BF), sds((peers, wide, LANES), BF)],
        info, hid, sq, squash0, frames, w_conv, grads, mean_all,
    )
    group = 8
    params = pltpu.CompilerParams(vmem_limit_bytes=50 * 2**20)
    spec = pl.BlockSpec((group, wide, LANES), lambda i: (i, 0, 0))
    packed = pl.pallas_call(
        functools.partial(add_kernel, nbias),
        grid=(peers // group,),
        out_shape=sds((peers, wide, LANES), BF),
        in_specs=[spec, spec],
        out_specs=spec,
        compiler_params=params,
    )(mine, swap_core(other))
    arrived = exchange(packed)
    block = 32
    full, bias = pl.pallas_call(
        sum_kernel,
        grid=(body // block,),
        out_shape=[sds((peers, body, LANES), BF), sds((nbias, LANES), F32)],
        in_specs=[
            pl.BlockSpec((peers, block, LANES), lambda i: (0, i, 0)),
            pl.BlockSpec((peers, 2 * nbias, LANES), lambda i: (0, body // (2 * nbias), 0)),
        ],
        out_specs=[
            pl.BlockSpec((peers, block, LANES), lambda i: (0, i, 0)),
            pl.BlockSpec((nbias, LANES), lambda i: (0, 0)),
        ],
        compiler_params=params,
    )(arrived, arrived)
    bias_got = swap_core(bias)
    full = exchange(full)
    spec = pl.BlockSpec((group, body, LANES), lambda i: (i, 0, 0))
    small = pl.BlockSpec((nbias, LANES), lambda i: (0, 0))
    g_in, g_conv, g_bias = pl.pallas_call(
        functools.partial(unpack_kernel, (in_size, conv_size, nh)),
        grid=(peers // group,),
        out_shape=[sds((features, ch), F32), sds((NL, 2 * ch, ch), F32), sds((NL + 1, ch), F32)],
        in_specs=[pl.BlockSpec(memory_space=pltpu.SMEM), spec, spec, small, small],
        out_specs=[
            pl.BlockSpec((group * in_size, ch), lambda i: (i, 0)),
            pl.BlockSpec((NL, group * conv_size, ch), lambda i: (0, i, 0)),
            pl.BlockSpec((NL + 1, ch), lambda i: (0, 0)),
        ],
        compiler_params=params,
    )(info, full, swap_core(full), bias, bias_got)
    return score[0, 0], g_in, g_bias[0], g_conv, g_bias[1:]


def solution(mesh):
    devices = mesh.devices
    trajs, segments = devices.shape
    inner = Mesh(devices.reshape(trajs // 2, 2, segments), ("x", "c", "tm"))
    return jax.shard_map(
        per_device,
        mesh=inner,
        in_specs=(P(("x", "c"), "tm", None), P(), P(), P(), P()),
        out_specs=(P(), P(), P(), P(), P()),
        check_vma=False,
    )
```

time: 638 us -> 252 us (0.39)
  waiting for transfers between devices: 269 us -> 16.9 us
  matrix products: 132 us -> 4.13 us
  Pallas kernels: 0 us -> 54.2 us
  between operations: 21.3 us -> 0.75 us
  local copies, waits for them, and re-layouts: 25.8 us -> 6.74 us
  other arithmetic: 13.2 us -> 0.08 us
    psum x2 -> x0, waiting for transfers between devices: 258 us -> none  [the longest x1 150 us: per_device(): lax.psum((gram_hi(centred_early, centred_early), gram_hi(centred_early, c...]
    all_to_all x0 -> x4, blocking collectives: none -> 153 us  [exchange(): return lax.all_to_all(value, PEERS, 0, 0, tiled=True)]
    psum x2 -> x0, blocking collectives: 151 us -> none  [the longest x1 75.7 us: per_device(): lax.psum((jnp.sum(early_rows, axis=0), jnp.sum(later_rows, axis=0)), ('tr...]
    dot_general x50 -> x1, matrix products: 132 us -> 4.13 us  [per_device(): squash0 = jnp.tanh(jnp.dot(frames, w_in, preferred_element_type=F32) + b_in)]
    pallas_call x0 -> x8, Pallas kernels: none -> 54.2 us  [the longest x5 34.1 us: call(): pl.pallas_call(kernel, out_shape=outs, in_specs=specs, out_specs=[pl.Bloc...]
    unnamed x84 -> x10, local copies, waits for them, and re-layouts: 20.6 us -> 5.04 us
  transfers between devices with their start and end apart: 10 -> 8, of which waited for: 8 -> 5; matrix products, arithmetic and copies ran while one was open for 5% -> 0% of each run, Pallas kernels for 0% -> 0%
where the time goes in v1:
time: 252 us; the launch traced here: 251 us
  blocking collectives  153 us (61%)
  Pallas kernels  54.2 us (22%)
  waiting for transfers between devices  16.9 us (7%)
  starting transfers between devices  14.8 us (6%)
  local copies, waits for them, and re-layouts  6.74 us (3%)
  matrix products  4.13 us (2%)
    all_to_all x4, blocking collectives, exchange(): return lax.all_to_all(value, PEERS, 0, 0, tiled=True)  153 us
    pallas_call x5, Pallas kernels, call(): pl.pallas_call(kernel, out_shape=outs, in_specs=specs, out_specs=[pl.Bloc...  34.1 us
    ppermute x6, waiting for transfers between devices, swap_core(): return lax.ppermute(value, 'c', [(0, 1), (1, 0)])  16 us
    pallas_call x1, Pallas kernels, per_device(): pl.pallas_call(functools.partial(unpack_kernel, (in_size, conv_size, nh))...  8.91 us
    ppermute x6, starting transfers between devices, swap_core(): return lax.ppermute(value, 'c', [(0, 1), (1, 0)])  8.53 us
    ppermute x2, starting transfers between devices, shift_segment(): lax.ppermute(value, 'tm', [(i, i + steps) for i in range(first, last)])  6.29 us
    pallas_call x1, Pallas kernels, per_device(): pl.pallas_call(functools.partial(add_kernel, nbias), grid=(peers // group...  5.68 us
    pallas_call x1, Pallas kernels, per_device(): pl.pallas_call(sum_kernel, grid=(body // block,), out_shape=[sds((peers,...  5.47 us
  transfers between devices with their start and end apart: 8, of which 5 were waited for; matrix products, arithmetic and copies ran while one was open for 0% of the time, Pallas kernels for 0%

profile of v1, /device:TPU:1, one launch (start us, length us, event | category | flops | bytes accessed | tf_op | source)
XLA Modules:
  0.0 250.9 jit_solution(13973145591490475483)
XLA Ops:
  0.6 0.0 copy-start.2
  0.6 4.1 %fusion.3 = (bf16[256,512]{1,0:T(8,128)(2,1)S(1)}, f32[256,512]{1,0:T(8,128)S(1)}) fusion(f32[512]{0:T(512)} %param.7, bf16[4096,512]{1,0:T(8,128)(2,1)} %param.6, bf16[1,256,4096]{2,1,0:T(8,128)(2,1)} %param.5), kind=kOutput, calls=%fused_computation.5 | convolution fusion | flops 1074003968 | bytes 7079936 | tf_op jit(solution)/shard_map/dot_general | solution.py:421
  4.8 1.3 collective-permute-start.1
  6.1 5.0 %collective-permute-start = (bf16[32,512]{1,0:T(8,128)(2,1)S(1)}, bf16[32,512]{1,0:T(8,128)(2,1)S(1)}, u32[]{:S(2)}, u32[]{:S(2)}) collective-permute-start(bf16[32,512]{1,0:T(8,128)(2,1)S(1)} %get-tuple-element.38), channel_id=1, source_target_pairs={{0,1},{1,2},{2,3},{3,4},{4,5},{5,6},{6,7},{7,8},{8,9},{9,10},{10,1... | collective-permute-start | bytes 98312 | tf_op jit(solution)/shard_map/ppermute | solution.py:46
  11.1 0.1 pad_add_fusion.info
  11.2 0.0 collective-permute-done.1.after
  11.2 0.9 collective-permute-done.before
  12.1 0.0 copy-done.2
  12.1 6.5 %shard_map.92 = (bf16[4,320,512]{2,1,0:T(8,128)(2,1)S(1)}, f32[3,320,512]{2,1,0:T(8,128)}, f32[64,48,128]{2,1,0:T(8,128)S(1)}, bf16[64,48,128]{2,1,0:T(8,128)(2,1)S(1)}, f32[8,512]{1,0:T(8,128)S(1)}) custom-call(s32[3]{0:T(128)S(1)} %pad_add_fusion.info, bf16[32,512]{1,0:T(8,128)(2,1)S(1)} %collective-permute-done.before, ...), custom_call_target="tpu_custom_call" | custom-call | tf_op jit(solution)/shard_map/pallas_call | solution.py:57
  18.7 1.5 collective-permute-start.2
  20.2 0.0 collective-permute-start.3
  20.2 1.9 collective-permute-done.3.sib
  22.1 0.0 collective-permute-done.2.got
  22.1 2.0 shard_map.93
  24.1 0.0 copy-start.1
  24.1 31.0 %all_to_all.20.arrived = bf16[64,64,128]{2,1,0:T(8,128)(2,1)S(1)} all-to-all(bf16[64,64,128]{2,1,0:T(8,128)(2,1)S(1)} %shard_map.93), channel_id=1, replica_groups=mesh['x'=4,'c'=2,'tm'=16] {'x','tm'}, dimensions={0} | all-to-all | bytes 2097152 | tf_op jit(solution)/shard_map/all_to_all | solution.py:50
  55.1 1.5 shard_map.94
  56.5 19.0 %all_to_all.21.half_cov = bf16[64,48,128]{2,1,0:T(8,128)(2,1)S(1)} all-to-all(bf16[64,48,128]{2,1,0:T(8,128)(2,1)S(1)} %get-tuple-element.24), channel_id=1, replica_groups=mesh['x'=4,'c'=2,'tm'=16] {'x','tm'}, dimensions={0} | all-to-all | bytes 1572864 | tf_op jit(solution)/shard_map/all_to_all | solution.py:50
  75.6 3.1 %collective-permute-start.4 = (bf16[64,48,128]{2,1,0:T(8,128)(2,1)S(1)}, bf16[64,48,128]{2,1,0:T(8,128)(2,1)S(1)}, u32[]{:S(2)}, u32[]{:S(2)}) collective-permute-start(bf16[64,48,128]{2,1,0:T(8,128)(2,1)S(1)} %all_to_all.21.half_cov), channel_id=1, source_target_pairs={{0,16},{16,0},{1,17},{17,1},{2,18},{18,2},{3,19},{19,3},{4,20},{20... | collective-permute-start | bytes 2359304 | tf_op jit(solution)/shard_map/ppermute | solution.py:40
  78.7 1.9 collective-permute-done.4.other_cov
  80.6 12.6 %shard_map.95 = (bf16[2048,512]{1,0:T(8,128)(2,1)S(1)}, f32[8,128]{1,0:T(8,128)S(1)}) custom-call(s32[3]{0:T(128)S(1)} %pad_add_fusion.info, bf16[64,48,128]{2,1,0:T(8,128)(2,1)S(1)} %all_to_all.21.half_cov, bf16[64,48,128]{2,1,0:T(8,128)(2,1)S(1)} %collective-permute-done.4.other_cov), custom_call_target="tpu_custom_call" | custom-call | tf_op jit(solution)/shard_map/pallas_call | solution.py:57
  93.2 0.0 copy-start
  93.2 1.3 copy-done
  94.5 0.0 copy-done.1
  94.5 11.6 %shard_map.96 = (bf16[64,240,128]{2,1,0:T(8,128)(2,1)}, bf16[64,240,128]{2,1,0:T(8,128)(2,1)}) custom-call(s32[3]{0:T(128)S(1)} %pad_add_fusion.info, bf16[4,320,512]{2,1,0:T(8,128)(2,1)S(1)} %get-tuple-element.26.hid, f32[3,320,512]{2,1,0:T(8,128)S(1)} %copy-done.1, f32[256,512]{1,0:T(8,128)S(1)} %get-tuple-element.40.sq0, bf16[256,4096]{1,0:T(8,128)(2,1)} %bitcast.11, ...), custom_call_target="tpu_custom_call" | custom-call | tf_op jit(solution)/shard_map/pallas_call | solution.py:57
  106.1 0.4 collective-permute-start.5
  106.5 6.6 %collective-permute-done.5.got = bf16[64,240,128]{2,1,0:T(8,128)(2,1)S(1)} collective-permute-done((bf16[64,240,128]{2,1,0:T(8,128)(2,1)}, bf16[64,240,128]{2,1,0:T(8,128)(2,1)S(1)}, u32[]{:S(2)}, u32[]{:S(2)}) %collective-permute-start.5) | collective-permute-done | bytes 3932192 | tf_op jit(solution)/shard_map/ppermute | solution.py:40
  113.1 0.0 copy-start.3
  113.1 1.9 copy-done.3
  115.0 5.7 %shard_map.97 = bf16[64,240,128]{2,1,0:T(8,128)(2,1)S(1)} custom-call(bf16[64,240,128]{2,1,0:T(8,128)(2,1)} %get-tuple-element.30.mine, bf16[64,240,128]{2,1,0:T(8,128)(2,1)} %copy-done.3), custom_call_target="tpu_custom_call" | custom-call | tf_op jit(solution)/shard_map/pallas_call | solution.py:473
  120.7 52.3 %all_to_all.22.arrived.tails = bf16[64,240,128]{2,1,0:T(8,128)(2,1)} all-to-all(bf16[64,240,128]{2,1,0:T(8,128)(2,1)S(1)} %shard_map.97), channel_id=1, replica_groups=mesh['x'=4,'c'=2,'tm'=16] {'x','tm'}, dimensions={0} | all-to-all | bytes 7864320 | tf_op jit(solution)/shard_map/all_to_all | solution.py:50
  173.0 5.5 %shard_map.98 = (bf16[64,224,128]{2,1,0:T(8,128)(2,1)S(1)}, f32[8,128]{1,0:T(8,128)S(1)}) custom-call(bf16[64,240,128]{2,1,0:T(8,128)(2,1)} %all_to_all.22.arrived.tails, bf16[64,240,128]{2,1,0:T(8,128)(2,1)} %all_to_all.22.arrived.tails), custom_call_target="tpu_custom_call" | custom-call | tf_op jit(solution)/shard_map/pallas_call | solution.py:483
  178.5 51.1 %all_to_all.23.mine = bf16[64,224,128]{2,1,0:T(8,128)(2,1)S(1)} all-to-all(bf16[64,224,128]{2,1,0:T(8,128)(2,1)S(1)} %get-tuple-element.32), channel_id=1, replica_groups=mesh['x'=4,'c'=2,'tm'=16] {'x','tm'}, dimensions={0} | all-to-all | bytes 7340032 | tf_op jit(solution)/shard_map/all_to_all | solution.py:50
  229.5 3.5 %collective-permute-start.6 = (bf16[64,224,128]{2,1,0:T(8,128)(2,1)S(1)}, bf16[64,224,128]{2,1,0:T(8,128)(2,1)S(1)}, u32[]{:S(2)}, u32[]{:S(2)}) collective-permute-start(bf16[64,224,128]{2,1,0:T(8,128)(2,1)S(1)} %all_to_all.23.mine), channel_id=1, source_target_pairs={{0,16},{16,0},{1,17},{17,1},{2,18},{18,2},{3,19},{19,3},{4,20},{20... | collective-permute-start | bytes 11010056 | tf_op jit(solution)/shard_map/ppermute | solution.py:40
  233.0 0.0 collective-permute-start.7
  233.0 0.5 slice.17
  233.5 5.5 %collective-permute-done.7.bias_got = f32[8,128]{1,0:T(8,128)S(1)} collective-permute-done((f32[8,128]{1,0:T(8,128)S(1)}, f32[8,128]{1,0:T(8,128)S(1)}, u32[]{:S(2)}, u32[]{:S(2)}) %collective-permute-start.7) | collective-permute-done | bytes 4128 | tf_op jit(solution)/shard_map/ppermute | solution.py:40
  239.1 0.0 collective-permute-done.6.got
  239.1 0.0 copy-start.4
  239.1 1.8 copy-done.4
  240.8 8.9 %shard_map.99 = (f32[4096,512]{1,0:T(8,128)}, f32[3,1024,512]{2,1,0:T(8,128)}, f32[4,512]{1,0:T(4,128)S(1)}) custom-call(s32[3]{0:T(128)S(1)} %pad_add_fusion.info, bf16[64,224,128]{2,1,0:T(8,128)(2,1)S(1)} %all_to_all.23.mine, bf16[64,224,128]{2,1,0:T(8,128)(2,1)} %copy-done.4, f32[8,128]{1,0:T(8,128)S(1)} %get-tuple-element.33.bias, ...), custom_call_target="tpu_custom_call" | custom-call | tf_op jit(solution)/shard_map/pallas_call | solution.py:501
  249.7 0.6 slice.18
  250.3 0.6 slice.19
  (1 shorter events, 0.0 us)
Async XLA Ops:
  0.6 11.5 %copy-start.2 = (f32[3,512]{1,0:T(4,128)S(1)}, f32[3,512]{1,0:T(4,128)}, u32[]{:S(2)}) copy-start(f32[3,512]{1,0:T(4,128)} %b.1) | copy-start | bytes 18436
  4.8 6.4 %collective-permute-start.1 = (bf16[32,512]{1,0:T(8,128)(2,1)S(1)}, bf16[32,512]{1,0:T(8,128)(2,1)S(1)}, u32[]{:S(2)}, u32[]{:S(2)}) collective-permute-start(bf16[32,512]{1,0:T(8,128)(2,1)S(1)} %get-tuple-element.37), channel_id=1, source_target_pairs={{1,0},{2,1},{3,2},{4,3},{5,4},{6,5},{7,6},{8,7},{9,8},{10,9},{11,1... | collective-permute-start | bytes 98312 | tf_op jit(solution)/shard_map/ppermute | solution.py:46
  6.1 6.0 %collective-permute-start = (bf16[32,512]{1,0:T(8,128)(2,1)S(1)}, bf16[32,512]{1,0:T(8,128)(2,1)S(1)}, u32[]{:S(2)}, u32[]{:S(2)}) collective-permute-start(bf16[32,512]{1,0:T(8,128)(2,1)S(1)} %get-tuple-element.38), channel_id=1, source_target_pairs={{0,1},{1,2},{2,3},{3,4},{4,5},{5,6},{6,7},{7,8},{8,9},{9,10},{10,1... | collective-permute-start | bytes 98312 | tf_op jit(solution)/shard_map/ppermute | solution.py:46
  18.7 3.5 %collective-permute-start.2 = (bf16[64,48,128]{2,1,0:T(8,128)(2,1)S(1)}, bf16[64,48,128]{2,1,0:T(8,128)(2,1)S(1)}, u32[]{:S(2)}, u32[]{:S(2)}) collective-permute-start(bf16[64,48,128]{2,1,0:T(8,128)(2,1)S(1)} %get-tuple-element.22), channel_id=1, source_target_pairs={{0,16},{16,0},{1,17},{17,1},{2,18},{18,2},{3,19},{19,3},{4,20},{20... | collective-permute-start | bytes 2359304 | tf_op jit(solution)/shard_map/ppermute | solution.py:40
  20.2 1.9 collective-permute-start.3
  24.1 70.4 %copy-start.1 = (f32[3,320,512]{2,1,0:T(8,128)S(1)}, f32[3,320,512]{2,1,0:T(8,128)}, u32[]{:S(2)}) copy-start(f32[3,320,512]{2,1,0:T(8,128)} %get-tuple-element.27.sq) | copy-start | bytes 5898244
  75.6 5.1 %collective-permute-start.4 = (bf16[64,48,128]{2,1,0:T(8,128)(2,1)S(1)}, bf16[64,48,128]{2,1,0:T(8,128)(2,1)S(1)}, u32[]{:S(2)}, u32[]{:S(2)}) collective-permute-start(bf16[64,48,128]{2,1,0:T(8,128)(2,1)S(1)} %all_to_all.21.half_cov), channel_id=1, source_target_pairs={{0,16},{16,0},{1,17},{17,1},{2,18},{18,2},{3,19},{19,3},{4,20},{20... | collective-permute-start | bytes 2359304 | tf_op jit(solution)/shard_map/ppermute | solution.py:40
  93.2 1.3 copy-start
  106.1 7.0 %collective-permute-start.5 = (bf16[64,240,128]{2,1,0:T(8,128)(2,1)}, bf16[64,240,128]{2,1,0:T(8,128)(2,1)S(1)}, u32[]{:S(2)}, u32[]{:S(2)}) collective-permute-start(bf16[64,240,128]{2,1,0:T(8,128)(2,1)} %get-tuple-element.31), channel_id=1, source_target_pairs={{0,16},{16,0},{1,17},{17,1},{2,18},{18,2},{3,19},{19,3},{4,20},{20... | collective-permute-start | bytes 11796488 | tf_op jit(solution)/shard_map/ppermute | solution.py:40
  113.1 1.9 copy-start.3
  229.5 9.5 %collective-permute-start.6 = (bf16[64,224,128]{2,1,0:T(8,128)(2,1)S(1)}, bf16[64,224,128]{2,1,0:T(8,128)(2,1)S(1)}, u32[]{:S(2)}, u32[]{:S(2)}) collective-permute-start(bf16[64,224,128]{2,1,0:T(8,128)(2,1)S(1)} %all_to_all.23.mine), channel_id=1, source_target_pairs={{0,16},{16,0},{1,17},{17,1},{2,18},{18,2},{3,19},{19,3},{4,20},{20... | collective-permute-start | bytes 11010056 | tf_op jit(solution)/shard_map/ppermute | solution.py:40
  233.0 6.0 %collective-permute-start.7 = (f32[8,128]{1,0:T(8,128)S(1)}, f32[8,128]{1,0:T(8,128)S(1)}, u32[]{:S(2)}, u32[]{:S(2)}) collective-permute-start(f32[8,128]{1,0:T(8,128)S(1)} %get-tuple-element.33.bias), channel_id=1, source_target_pairs={{0,16},{16,0},{1,17},{17,1},{2,18},{18,2},{3,19},{19,3},{4,20},{20... | collective-permute-start | bytes 12296 | tf_op jit(solution)/shard_map/ppermute | solution.py:40
  239.1 1.8 copy-start.4

commit v2 on v1

--- a/solution.py
+++ b/solution.py
@@ -191,11 +191,20 @@
     cov[...] = jnp.broadcast_to(value[None], cov.shape)
 
 
-def score_kernel(dims, info, half_cov, other_cov, grads, score, cov):
+def step_kernel(
+    dims, info, half_cov, other_cov, mean_all, hid_hbm, sq_hbm, sq0_hbm, w_hbm,
+    score, mine, other, dpre, cov, grads, hid, sq, sq0, w, sems,
+):
     rows, ch, length, peers, piece = dims
     core = info[0]
     nb = ch // LANES
     half = ch // 2
+    loads = [
+        pltpu.make_async_copy(src, dst, sems.at[n])
+        for n, (src, dst) in enumerate(((hid_hbm, hid), (sq_hbm, sq), (sq0_hbm, sq0), (w_hbm, w)))
+    ]
+    for load in loads:
+        load.start()
 
     def place(i, carry):
         at = pl.multiple_of(core * half + i * piece, piece)
@@ -254,13 +263,15 @@
     grads[:ch] = backward(*fe[:6], gre + gre.T).astype(BF)
     grl = dot3(u, k2, TN)
     grads[3 * ch :] = backward(*fl[:6], grl + grl.T).astype(BF)
-
-
-def backward_kernel(dims, info, hid, sq, sq0, frames, w, grads, mean_all, mine, other):
+    for load in loads:
+        load.wait()
+    conv_backward(dims, info, hid, sq, sq0, w, grads, mean_all, mine, other, dpre)
+
+
+def conv_backward(dims, info, hid, sq, sq0, w, grads, mean_all, mine, other, dpre):
     rows, ch, length, peers, piece = dims
     core, segment = info[0], info[1]
     segments = length // rows
-    features = frames.shape[1]
     half = ch // 2
     nh = half // LANES
     total = 2 * (peers // segments) * (length - LAG)
@@ -310,7 +321,6 @@
                 piece_j = res[:, j * LANES : (j + 1) * LANES].reshape(count, size, LANES)
                 ref[p0 : p0 + count, at + j * size : at + (j + 1) * size, :] = piece_j
 
-    in_size = features // peers
     conv_size = 2 * ch // peers
     for layer in reversed(range(NL)):
         step = 2**layer
@@ -320,19 +330,16 @@
         biases[layer + 1] = jnp.sum(own, axis=0, keepdims=True)
         h = hid[layer].astype(F32)
         hist = pltpu.roll(h, step, 0)[HALO : HALO + rows].astype(BF)
-        at = nh * in_size + layer * nh * conv_size
+        at = layer * nh * conv_size
         count = ch // conv_size
         store(hid[layer, HALO : HALO + rows, :], own, 0, count, conv_size, at)
         store(hist, own, count, count, conv_size, at)
         back = dot(pre, w[layer, ch:], NT)
         grad = grad + dot(pre, w[layer, :ch], NT) + pltpu.roll(back, grows - step, 0)
     s = sq0[...]
-    own = (grad[:rows] * (1.0 - s * s)).astype(BF).astype(F32)
-    biases[0] = jnp.sum(own, axis=0, keepdims=True)
-    tile = min(features, 512)
-    for k in range(features // tile):
-        count = tile // in_size
-        store(frames[:, k * tile : (k + 1) * tile], own, k * count, count, in_size, 0)
+    own = (grad[:rows] * (1.0 - s * s)).astype(BF)
+    dpre[...] = own
+    biases[0] = jnp.sum(own.astype(F32), axis=0, keepdims=True)
     bias = jnp.concatenate(biases, axis=0)
     for part, ref in zip(halves(bias), (mine, other)):
         hi, lo = split(part)
@@ -345,15 +352,23 @@
         ref[:, at:, :] = jnp.broadcast_to(tail[None], (peers,) + tail.shape)
 
 
-def add_kernel(nbias, mine, got, packed):
-    body = packed.shape[1] - 2 * nbias
-    a, b = mine[...].astype(F32), got[...].astype(F32)
-    value = a + b
-    packed[:, :body, :] = value[:, :body].astype(BF)
+def pack_kernel(nbias, info, left, left_got, dpre, dpre_got, mine, got, packed):
+    count = packed.shape[0]
+    ch = dpre.shape[1]
+    size = left.shape[1] // count
+    lhs = jnp.concatenate([left[...], left_got[...]], axis=0)
+    res = dot(lhs, jnp.concatenate([dpre[...], dpre_got[...]], axis=0), TN).astype(BF)
+    for j in range(ch // LANES):
+        part = res[:, j * LANES : (j + 1) * LANES].reshape(count, size, LANES)
+        packed[:, j * size : (j + 1) * size, :] = part
+    at = size * (ch // LANES)
+    body = mine.shape[1] - 2 * nbias
+    value = mine[...].astype(F32) + got[...].astype(F32)
+    packed[:, at : at + body, :] = value[:, :body].astype(BF)
     bias = value[0, body : body + nbias] + value[0, body + nbias :]
     hi = bias.astype(BF).astype(F32)
     tail = jnp.concatenate([hi, bias - hi], axis=0).astype(BF)
-    packed[:, body:, :] = jnp.broadcast_to(tail[None], (packed.shape[0],) + tail.shape)
+    packed[:, at + body :, :] = jnp.broadcast_to(tail[None], (count,) + tail.shape)
 
 
 def sum_kernel(arrived, tails, full, bias):
@@ -375,31 +390,18 @@
         bias[...] = t[:n] + t[n:]
 
 
-def unpack_kernel(sizes, info, mine, got, bias, bias_got, w_in, w_conv, b_all):
-    in_size, conv_size, nh = sizes
-    first = info[0] == 0
-    count = mine.shape[0]
-    lo = jnp.where(first, mine[...].astype(F32), got[...].astype(F32))
-    hi = jnp.where(first, got[...].astype(F32), mine[...].astype(F32))
-    for side, value in enumerate((lo, hi)):
-        for j in range(nh):
-            cols = slice((side * nh + j) * LANES, (side * nh + j + 1) * LANES)
-            part = value[:, j * in_size : (j + 1) * in_size]
-            w_in[:, cols] = part.reshape(count * in_size, LANES)
-            for layer in range(NL):
-                at = nh * in_size + (layer * nh + j) * conv_size
-                part = value[:, at : at + conv_size]
-                w_conv[layer, :, cols] = part.reshape(count * conv_size, LANES)
-
-    @pl.when(pl.program_id(0) == 0)
-    def _():
-        lo = jnp.where(first, bias[...], bias_got[...])
-        hi = jnp.where(first, bias_got[...], bias[...])
-        n = NL + 1
-        for side, value in enumerate((lo, hi)):
-            for j in range(nh):
-                cols = slice((side * nh + j) * LANES, (side * nh + j + 1) * LANES)
-                b_all[:, cols] = value[j * n : (j + 1) * n]
+def unpack_kernel(sizes, info, chunks, *refs):
+    in_size, conv_size, nb = sizes
+    w_in, w_conv = refs[-2:]
+    count = chunks.shape[0]
+    for j in range(nb):
+        part = chunks[:, j * in_size : (j + 1) * in_size, :].astype(F32)
+        w_in[0, :, j * LANES : (j + 1) * LANES] = part.reshape(count * in_size, LANES)
+    for layer in range(NL):
+        for j in range(nb // 2):
+            at = nb * in_size + (layer * (nb // 2) + j) * conv_size
+            part = chunks[:, at : at + conv_size, :].astype(F32)
+            w_conv[layer, :, j * LANES : (j + 1) * LANES] = part.reshape(count * conv_size, LANES)
 
 
 def per_device(frames, w_in, b_in, w_conv, b_conv):
@@ -417,6 +419,9 @@
     dims = (rows, ch, length, peers, piece)
     info = jnp.stack([core, segment, lax.axis_index("x") * segments + segment]).astype(jnp.int32)
     ext = rows + 2 * HALO
+    frames_got = swap_core(
+        lax.dynamic_slice_in_dim(frames, (1 - core) * (features // 2), features // 2, 1)
+    )
 
     squash0 = jnp.tanh(jnp.dot(frames, w_in, preferred_element_type=F32) + b_in)
     own = squash0.astype(BF)
@@ -451,33 +456,61 @@
         ],
     )
     cov = exchange(cov)
-    grads, score = call(
-        functools.partial(score_kernel, dims),
-        [sds((4 * ch, ch), BF), sds((8, LANES), F32)],
-        info, cov, swap_core(cov),
-        scratch=[pltpu.VMEM((3, ch, ch), F32)],
-    )
-    in_size = features // peers
+    half_features = features // 2
+    in_size = half_features // peers
     conv_size = 2 * ch // peers
-    body = nh * (in_size + NL * conv_size)
     nbias = (NL + 1) * nh
+    conv_wide = NL * nh * conv_size + 2 * nbias
+    body = nb * in_size + NL * nh * conv_size
     wide = body + 2 * nbias
-    mine, other = call(
-        functools.partial(backward_kernel, dims),
-        [sds((peers, wide, LANES), BF), sds((peers, wide, LANES), BF)],
-        info, hid, sq, squash0, frames, w_conv, grads, mean_all,
-    )
-    group = 8
+    vmem = pl.BlockSpec(memory_space=pltpu.VMEM)
+    smem = pl.BlockSpec(memory_space=pltpu.SMEM)
+    hbm = pl.BlockSpec(memory_space=pl.ANY)
     params = pltpu.CompilerParams(vmem_limit_bytes=50 * 2**20)
-    spec = pl.BlockSpec((group, wide, LANES), lambda i: (i, 0, 0))
+    score, mine, other, dpre = pl.pallas_call(
+        functools.partial(step_kernel, dims),
+        out_shape=[
+            sds((8, LANES), F32),
+            sds((peers, conv_wide, LANES), BF),
+            sds((peers, conv_wide, LANES), BF),
+            sds((rows, ch), BF),
+        ],
+        in_specs=[smem, vmem, vmem, vmem, hbm, hbm, hbm, hbm],
+        out_specs=[vmem] * 4,
+        scratch_shapes=[
+            pltpu.VMEM((3, ch, ch), F32),
+            pltpu.VMEM((4 * ch, ch), BF),
+            pltpu.VMEM(hid.shape, BF),
+            pltpu.VMEM(sq.shape, F32),
+            pltpu.VMEM(squash0.shape, F32),
+            pltpu.VMEM(w_conv.shape, BF),
+            pltpu.SemaphoreType.DMA((4,)),
+        ],
+        compiler_params=params,
+    )(info, cov, swap_core(cov), mean_all, hid, sq, squash0, w_conv)
+    steps = 4
+    group = peers // steps
+    tile = group * in_size
+    whole = pl.BlockSpec((rows, ch), lambda i, at: (0, 0))
+    conv_spec = pl.BlockSpec((group, conv_wide, LANES), lambda i, at: (i, 0, 0))
     packed = pl.pallas_call(
-        functools.partial(add_kernel, nbias),
-        grid=(peers // group,),
+        functools.partial(pack_kernel, nbias),
+        grid_spec=pltpu.PrefetchScalarGridSpec(
+            num_scalar_prefetch=1,
+            grid=(steps,),
+            in_specs=[
+                pl.BlockSpec((rows, tile), lambda i, at: (0, at[0] * steps + i)),
+                pl.BlockSpec((rows, tile), lambda i, at: (0, i)),
+                whole,
+                whole,
+                conv_spec,
+                conv_spec,
+            ],
+            out_specs=pl.BlockSpec((group, wide, LANES), lambda i, at: (i, 0, 0)),
+        ),
         out_shape=sds((peers, wide, LANES), BF),
-        in_specs=[spec, spec],
-        out_specs=spec,
         compiler_params=params,
-    )(mine, swap_core(other))
+    )(info, frames, frames_got, dpre, swap_core(dpre), mine, swap_core(other))
     arrived = exchange(packed)
     block = 32
     full, bias = pl.pallas_call(
@@ -496,21 +529,34 @@
     )(arrived, arrived)
     bias_got = swap_core(bias)
     full = exchange(full)
-    spec = pl.BlockSpec((group, body, LANES), lambda i: (i, 0, 0))
-    small = pl.BlockSpec((nbias, LANES), lambda i: (0, 0))
-    g_in, g_conv, g_bias = pl.pallas_call(
-        functools.partial(unpack_kernel, (in_size, conv_size, nh)),
-        grid=(peers // group,),
-        out_shape=[sds((features, ch), F32), sds((NL, 2 * ch, ch), F32), sds((NL + 1, ch), F32)],
-        in_specs=[pl.BlockSpec(memory_space=pltpu.SMEM), spec, spec, small, small],
-        out_specs=[
-            pl.BlockSpec((group * in_size, ch), lambda i: (i, 0)),
-            pl.BlockSpec((NL, group * conv_size, ch), lambda i: (0, i, 0)),
-            pl.BlockSpec((NL + 1, ch), lambda i: (0, 0)),
-        ],
-        compiler_params=params,
-    )(info, full, swap_core(full), bias, bias_got)
-    return score[0, 0], g_in, g_bias[0], g_conv, g_bias[1:]
+    steps = 8
+    group = peers // steps
+
+    def unpack(chunks, at, earlier):
+        return pl.pallas_call(
+            functools.partial(unpack_kernel, (in_size, conv_size, nb)),
+            grid_spec=pltpu.PrefetchScalarGridSpec(
+                num_scalar_prefetch=1,
+                grid=(steps,),
+                in_specs=[pl.BlockSpec((group, body, LANES), lambda i, at: (i, 0, 0))]
+                + [hbm] * len(earlier),
+                out_specs=[
+                    pl.BlockSpec((1, group * in_size, ch), lambda i, at: (at[0], i, 0)),
+                    pl.BlockSpec((NL, group * conv_size, ch // 2), lambda i, at: (0, i, at[0])),
+                ],
+            ),
+            out_shape=[sds((2, half_features, ch), F32), sds((NL, 2 * ch, ch), F32)],
+            input_output_aliases={2 + n: n for n in range(len(earlier))},
+            compiler_params=params,
+            cost_estimate=pl.CostEstimate(flops=0, bytes_accessed=12 * 2**20, transcendentals=0),
+        )(at, chunks, *earlier)
+
+    got = swap_core(full)
+    partial = unpack(full, info[:1], [])
+    g_in, g_conv = unpack(got, 1 - info[:1], partial)
+    both = jnp.where(core == 0, jnp.stack([bias, bias_got]), jnp.stack([bias_got, bias]))
+    g_bias = both.reshape(2, nh, NL + 1, LANES).transpose(2, 0, 1, 3).reshape(NL + 1, ch)
+    return score[0, 0], g_in.reshape(features, ch), g_bias[0], g_conv, g_bias[1:]
 
 
 def solution(mesh):

time: 252 us -> 246 us (0.976)
  local copies, waits for them, and re-layouts: 6.74 us -> 3.28 us
    pallas_call x5 -> x3, Pallas kernels: 34.1 us -> 10 us  [call(): pl.pallas_call(kernel, out_shape=outs, in_specs=specs, out_specs=[pl.Bloc...]
    pallas_call x2 -> x4, Pallas kernels: 14.6 us -> 38.3 us  [the longest x1 18.3 us: per_device(): pl.pallas_call(functools.partial(step_kernel, dims), out_shape=[sds((8, L...]
    unnamed x10 -> x6, local copies, waits for them, and re-layouts: 5.04 us -> 1.51 us
    ppermute x2, waiting for transfers between devices: 0.92 us -> 3.46 us  [shift_segment(): lax.ppermute(value, 'tm', [(i, i + steps) for i in range(first, last)])]
    ppermute x6 -> x8, waiting for transfers between devices: 16 us -> 13.7 us  [swap_core(): return lax.ppermute(value, 'c', [(0, 1), (1, 0)])]
    ppermute x6 -> x8, starting transfers between devices: 8.53 us -> 9.87 us  [swap_core(): return lax.ppermute(value, 'c', [(0, 1), (1, 0)])]
  transfers between devices with their start and end apart: 8 -> 10, of which waited for: 5 -> 6; matrix products, arithmetic and copies ran while one was open for 0% -> 1% of each run, Pallas kernels for 0% -> 3%
where the time goes in v2:
time: 246 us
  blocking collectives  151 us (61%)
  Pallas kernels  53.8 us (22%)
  waiting for transfers between devices  17.2 us (7%)
  starting transfers between devices  15.5 us (6%)
  matrix products  4.13 us (2%)
  local copies, waits for them, and re-layouts  3.28 us (1%)
    all_to_all x4, blocking collectives, exchange(): return lax.all_to_all(value, PEERS, 0, 0, tiled=True)  151 us
    pallas_call x1, Pallas kernels, per_device(): pl.pallas_call(functools.partial(step_kernel, dims), out_shape=[sds((8, L...  18.3 us
    pallas_call x2, Pallas kernels, unpack(): pl.pallas_call(functools.partial(unpack_kernel, (in_size, conv_size, nb))...  14 us
    ppermute x8, waiting for transfers between devices, swap_core(): return lax.ppermute(value, 'c', [(0, 1), (1, 0)])  13.7 us
    pallas_call x3, Pallas kernels, call(): pl.pallas_call(kernel, out_shape=outs, in_specs=specs, out_specs=[pl.Bloc...  10 us
    ppermute x8, starting transfers between devices, swap_core(): return lax.ppermute(value, 'c', [(0, 1), (1, 0)])  9.87 us
    pallas_call x1, Pallas kernels, per_device(): pl.pallas_call(functools.partial(pack_kernel, nbias), grid_spec=pltpu.Pre...  5.96 us
    ppermute x2, starting transfers between devices, shift_segment(): lax.ppermute(value, 'tm', [(i, i + steps) for i in range(first, last)])  5.66 us
  transfers between devices with their start and end apart: 10, of which 6 were waited for; matrix products, arithmetic and copies ran while one was open for 1% of the time, Pallas kernels for 3%

profile of v2, /device:TPU:1, one launch (start us, length us, event | category | flops | bytes accessed | tf_op | source)
XLA Modules:
  0.0 245.6 jit_solution(7513942499970686496)
XLA Ops:
  0.6 0.0 copy-start.1
  0.6 4.1 %fusion.4 = (bf16[256,512]{1,0:T(8,128)(2,1)S(1)}, f32[256,512]{1,0:T(8,128)S(1)}) fusion(f32[512]{0:T(512)} %param.7, bf16[4096,512]{1,0:T(8,128)(2,1)} %param.6, bf16[1,256,4096]{2,1,0:T(8,128)(2,1)} %param.5), kind=kOutput, calls=%fused_computation.8 | convolution fusion | flops 1074003968 | bytes 7079936 | tf_op jit(solution)/shard_map/dot_general | solution.py:426
  4.8 4.4 %collective-permute-start = (bf16[32,512]{1,0:T(8,128)(2,1)S(1)}, bf16[32,512]{1,0:T(8,128)(2,1)S(1)}, u32[]{:S(2)}, u32[]{:S(2)}) collective-permute-start(bf16[32,512]{1,0:T(8,128)(2,1)S(1)} %get-tuple-element.40), channel_id=1, source_target_pairs={{0,1},{1,2},{2,3},{3,4},{4,5},{5,6},{6,7},{7,8},{8,9},{9,10},{10,1... | collective-permute-start | bytes 98312 | tf_op jit(solution)/shard_map/ppermute | solution.py:46
  9.2 1.3 collective-permute-start.1
  10.5 0.1 pad_add_fusion.info
  10.6 0.0 collective-permute-done.before
  10.6 3.5 %collective-permute-done.1.after = bf16[32,512]{1,0:T(8,128)(2,1)S(1)} collective-permute-done((bf16[32,512]{1,0:T(8,128)(2,1)S(1)}, bf16[32,512]{1,0:T(8,128)(2,1)S(1)}, u32[]{:S(2)}, u32[]{:S(2)}) %collective-permute-start.1) | collective-permute-done | bytes 32800 | tf_op jit(solution)/shard_map/ppermute | solution.py:46
  14.0 0.0 copy-done.1
  14.0 6.6 %shard_map.92 = (bf16[4,320,512]{2,1,0:T(8,128)(2,1)S(1)}, f32[3,320,512]{2,1,0:T(8,128)}, f32[64,48,128]{2,1,0:T(8,128)S(1)}, bf16[64,48,128]{2,1,0:T(8,128)(2,1)S(1)}, f32[8,512]{1,0:T(8,128)S(1)}) custom-call(s32[3]{0:T(128)S(1)} %pad_add_fusion.info, bf16[32,512]{1,0:T(8,128)(2,1)S(1)} %collective-permute-done.before, ...), custom_call_target="tpu_custom_call" | custom-call | tf_op jit(solution)/shard_map/pallas_call | solution.py:57
  20.6 1.9 collective-permute-start.2
  22.5 0.0 collective-permute-start.3
  22.5 1.9 collective-permute-done.3.sib
  24.4 0.0 collective-permute-done.2.got
  24.4 2.0 shard_map.93
  26.4 28.0 %all_to_all.20.arrived = bf16[64,64,128]{2,1,0:T(8,128)(2,1)S(1)} all-to-all(bf16[64,64,128]{2,1,0:T(8,128)(2,1)S(1)} %shard_map.93), channel_id=1, replica_groups=mesh['x'=4,'c'=2,'tm'=16] {'x','tm'}, dimensions={0} | all-to-all | bytes 2097152 | tf_op jit(solution)/shard_map/all_to_all | solution.py:50
  54.4 1.5 shard_map.94
  55.9 19.0 %all_to_all.21.half_cov = bf16[64,48,128]{2,1,0:T(8,128)(2,1)S(1)} all-to-all(bf16[64,48,128]{2,1,0:T(8,128)(2,1)S(1)} %get-tuple-element.25), channel_id=1, replica_groups=mesh['x'=4,'c'=2,'tm'=16] {'x','tm'}, dimensions={0} | all-to-all | bytes 1572864 | tf_op jit(solution)/shard_map/all_to_all | solution.py:50
  74.9 3.1 %collective-permute-start.4 = (bf16[64,48,128]{2,1,0:T(8,128)(2,1)S(1)}, bf16[64,48,128]{2,1,0:T(8,128)(2,1)S(1)}, u32[]{:S(2)}, u32[]{:S(2)}) collective-permute-start(bf16[64,48,128]{2,1,0:T(8,128)(2,1)S(1)} %all_to_all.21.half_cov), channel_id=1, source_target_pairs={{0,16},{16,0},{1,17},{17,1},{2,18},{18,2},{3,19},{19,3},{4,20},{20... | collective-permute-start | bytes 2359304 | tf_op jit(solution)/shard_map/ppermute | solution.py:40
  78.0 1.9 collective-permute-done.4.other_cov
  79.9 0.0 copy-start.2
  80.0 18.3 %shard_map.95 = (f32[8,128]{1,0:T(8,128)S(1)}, bf16[64,112,128]{2,1,0:T(8,128)(2,1)}, bf16[64,112,128]{2,1,0:T(8,128)(2,1)}, bf16[256,512]{1,0:T(8,128)(2,1)S(1)}) custom-call(s32[3]{0:T(128)S(1)} %pad_add_fusion.info, bf16[64,48,128]{2,1,0:T(8,128)(2,1)S(1)} %all_to_all.21.half_cov, bf16[64,48,128]{2,1,0:T(8,128)(2,1)S(1)} %collective-permute-done.4.other_cov, ...), custom_call_target="tpu_custom_call" | custom-call | tf_op jit(solution)/shard_map/pallas_call | solution.py:470
  98.3 0.5 collective-permute-start.7
  98.7 0.0 copy-done.2
  98.7 0.1 dynamic-slice_bitcast_fusion
  98.8 0.2 collective-permute-start.5
  99.0 0.4 collective-permute-start.6
  99.4 4.2 %collective-permute-done.5.left_got = bf16[256,2048]{1,0:T(8,128)(2,1)S(1)} collective-permute-done((bf16[256,2048]{1,0:T(8,128)(2,1)S(1)}, bf16[256,2048]{1,0:T(8,128)(2,1)S(1)}, u32[]{:S(2)}, u32[]{:S(2)}) %collective-permute-start.5) | collective-permute-done | bytes 1048608 | tf_op jit(solution)/shard_map/ppermute | solution.py:40
  103.7 0.4 collective-permute-done.6.dpre_got
  104.0 0.0 collective-permute-done.7.got
  104.0 0.0 copy-start
  104.0 1.5 copy-done
  105.5 6.0 %shard_map.96 = bf16[64,240,128]{2,1,0:T(8,128)(2,1)} custom-call(s32[3]{0:T(128)S(1)} %pad_add_fusion.info, bf16[256,4096]{1,0:T(8,128)(2,1)} %bitcast.21, bf16[256,2048]{1,0:T(8,128)(2,1)S(1)} %collective-permute-done.5.left_got, bf16[256,512]{1,0:T(8,128)(2,1)S(1)} %get-tuple-element.30.dpre, bf16[256,512]{1,0:T(8,128)(2,1)S(1)} %collective-permute-done.6.dpre_got, ...), custom_call_target="tpu_custom_call" | custom-call | tf_op jit(solution)/shard_map/pallas_call | solution.py:496
  111.5 53.2 %all_to_all.22.arrived.tails = bf16[64,240,128]{2,1,0:T(8,128)(2,1)} all-to-all(bf16[64,240,128]{2,1,0:T(8,128)(2,1)} %shard_map.96), channel_id=1, replica_groups=mesh['x'=4,'c'=2,'tm'=16] {'x','tm'}, dimensions={0} | all-to-all | bytes 7864320 | tf_op jit(solution)/shard_map/all_to_all | solution.py:50
  164.7 5.5 %shard_map.97 = (bf16[64,224,128]{2,1,0:T(8,128)(2,1)S(1)}, f32[8,128]{1,0:T(8,128)S(1)}) custom-call(bf16[64,240,128]{2,1,0:T(8,128)(2,1)} %all_to_all.22.arrived.tails, bf16[64,240,128]{2,1,0:T(8,128)(2,1)} %all_to_all.22.arrived.tails), custom_call_target="tpu_custom_call" | custom-call | tf_op jit(solution)/shard_map/pallas_call | solution.py:516
  170.2 50.7 %all_to_all.23.chunks = bf16[64,224,128]{2,1,0:T(8,128)(2,1)} all-to-all(bf16[64,224,128]{2,1,0:T(8,128)(2,1)S(1)} %get-tuple-element.33), channel_id=1, replica_groups=mesh['x'=4,'c'=2,'tm'=16] {'x','tm'}, dimensions={0} | all-to-all | bytes 7340032 | tf_op jit(solution)/shard_map/all_to_all | solution.py:50
  220.8 3.8 %collective-permute-start.8 = (bf16[64,224,128]{2,1,0:T(8,128)(2,1)}, bf16[64,224,128]{2,1,0:T(8,128)(2,1)}, u32[]{:S(2)}, u32[]{:S(2)}) collective-permute-start(bf16[64,224,128]{2,1,0:T(8,128)(2,1)} %all_to_all.23.chunks), channel_id=1, source_target_pairs={{0,16},{16,0},{1,17},{17,1},{2,18},{18,2},{3,19},{19,3},{4,20},{20... | collective-permute-start | bytes 11010056 | tf_op jit(solution)/shard_map/ppermute | solution.py:40
  224.6 0.0 collective-permute-start.9
  224.6 0.5 slice.21
  225.1 5.2 %collective-permute-done.9 = f32[8,128]{1,0:T(8,128)S(1)} collective-permute-done((f32[8,128]{1,0:T(8,128)S(1)}, f32[8,128]{1,0:T(8,128)S(1)}, u32[]{:S(2)}, u32[]{:S(2)}) %collective-permute-start.9) | collective-permute-done | bytes 4128 | tf_op jit(solution)/shard_map/ppermute | solution.py:40
  230.3 0.6 slice.27
  230.9 0.6 slice.28
  231.5 7.0 %shard_map.98 = (f32[2,2048,512]{2,1,0:T(8,128)}, f32[3,1024,512]{2,1,0:T(8,128)}) custom-call(s32[1]{0:T(128)} %bitcast.info, bf16[64,224,128]{2,1,0:T(8,128)(2,1)} %all_to_all.23.chunks), custom_call_target="tpu_custom_call" | custom-call | bytes 12582912 | tf_op jit(solution)/shard_map/pallas_call | solution.py:536
  238.5 0.0 collective-permute-done.8.chunks
  238.5 7.0 %shard_map.99 = (f32[2,2048,512]{2,1,0:T(8,128)}, f32[3,1024,512]{2,1,0:T(8,128)}) custom-call(s32[1]{0:T(128)S(6)} %sub.6.info, bf16[64,224,128]{2,1,0:T(8,128)(2,1)} %collective-permute-done.8.chunks, f32[2,2048,512]{2,1,0:T(8,128)} %get-tuple-element.34.refs_0_, ...), custom_call_target="tpu_custom_call", output_to_operand_aliasing={{0}: (2, {}), {1}: (3, {})} | custom-call | bytes 12582912 | tf_op jit(solution)/shard_map/pallas_call | solution.py:536
  (2 shorter events, 0.0 us)
Async XLA Ops:
  0.6 13.4 %copy-start.1 = (f32[3,512]{1,0:T(4,128)S(1)}, f32[3,512]{1,0:T(4,128)}, u32[]{:S(2)}) copy-start(f32[3,512]{1,0:T(4,128)} %b.1) | copy-start | bytes 18436
  4.8 5.8 %collective-permute-start = (bf16[32,512]{1,0:T(8,128)(2,1)S(1)}, bf16[32,512]{1,0:T(8,128)(2,1)S(1)}, u32[]{:S(2)}, u32[]{:S(2)}) collective-permute-start(bf16[32,512]{1,0:T(8,128)(2,1)S(1)} %get-tuple-element.40), channel_id=1, source_target_pairs={{0,1},{1,2},{2,3},{3,4},{4,5},{5,6},{6,7},{7,8},{8,9},{9,10},{10,1... | collective-permute-start | bytes 98312 | tf_op jit(solution)/shard_map/ppermute | solution.py:46
  9.2 4.8 %collective-permute-start.1 = (bf16[32,512]{1,0:T(8,128)(2,1)S(1)}, bf16[32,512]{1,0:T(8,128)(2,1)S(1)}, u32[]{:S(2)}, u32[]{:S(2)}) collective-permute-start(bf16[32,512]{1,0:T(8,128)(2,1)S(1)} %get-tuple-element.39), channel_id=1, source_target_pairs={{1,0},{2,1},{3,2},{4,3},{5,4},{6,5},{7,6},{8,7},{9,8},{10,9},{11,1... | collective-permute-start | bytes 98312 | tf_op jit(solution)/shard_map/ppermute | solution.py:46
  20.6 3.8 %collective-permute-start.2 = (bf16[64,48,128]{2,1,0:T(8,128)(2,1)S(1)}, bf16[64,48,128]{2,1,0:T(8,128)(2,1)S(1)}, u32[]{:S(2)}, u32[]{:S(2)}) collective-permute-start(bf16[64,48,128]{2,1,0:T(8,128)(2,1)S(1)} %get-tuple-element.23), channel_id=1, source_target_pairs={{0,16},{16,0},{1,17},{17,1},{2,18},{18,2},{3,19},{19,3},{4,20},{20... | collective-permute-start | bytes 2359304 | tf_op jit(solution)/shard_map/ppermute | solution.py:40
  22.5 1.9 collective-permute-start.3
  74.9 5.1 %collective-permute-start.4 = (bf16[64,48,128]{2,1,0:T(8,128)(2,1)S(1)}, bf16[64,48,128]{2,1,0:T(8,128)(2,1)S(1)}, u32[]{:S(2)}, u32[]{:S(2)}) collective-permute-start(bf16[64,48,128]{2,1,0:T(8,128)(2,1)S(1)} %all_to_all.21.half_cov), channel_id=1, source_target_pairs={{0,16},{16,0},{1,17},{17,1},{2,18},{18,2},{3,19},{19,3},{4,20},{20... | collective-permute-start | bytes 2359304 | tf_op jit(solution)/shard_map/ppermute | solution.py:40
  79.9 18.8 %copy-start.2 = (bf16[1,256,4096]{2,1,0:T(8,128)(2,1)S(1)}, bf16[1,256,4096]{2,1,0:T(8,128)(2,1)}, u32[]{:S(2)}) copy-start(bf16[1,256,4096]{2,1,0:T(8,128)(2,1)} %param.5) | copy-start | bytes 6291460
  98.3 5.7 %collective-permute-start.7 = (bf16[64,112,128]{2,1,0:T(8,128)(2,1)}, bf16[64,112,128]{2,1,0:T(8,128)(2,1)}, u32[]{:S(2)}, u32[]{:S(2)}) collective-permute-start(bf16[64,112,128]{2,1,0:T(8,128)(2,1)} %get-tuple-element.32), channel_id=1, source_target_pairs={{0,16},{16,0},{1,17},{17,1},{2,18},{18,2},{3,19},{19,3},{4,20},{20... | collective-permute-start | bytes 5505032 | tf_op jit(solution)/shard_map/ppermute | solution.py:40
  98.8 4.8 %collective-permute-start.5 = (bf16[256,2048]{1,0:T(8,128)(2,1)S(1)}, bf16[256,2048]{1,0:T(8,128)(2,1)S(1)}, u32[]{:S(2)}, u32[]{:S(2)}) collective-permute-start(bf16[256,2048]{1,0:T(8,128)(2,1)S(1)} %dynamic-slice_bitcast_fusion), channel_id=1, source_target_pairs={{0,16},{16,0},{1,17},{17,1},{2,18},{18,2},{3,19},{19,3},{4,20},{20... | collective-permute-start | bytes 3145736 | tf_op jit(solution)/shard_map/ppermute | solution.py:40
  99.0 5.0 %collective-permute-start.6 = (bf16[256,512]{1,0:T(8,128)(2,1)S(1)}, bf16[256,512]{1,0:T(8,128)(2,1)S(1)}, u32[]{:S(2)}, u32[]{:S(2)}) collective-permute-start(bf16[256,512]{1,0:T(8,128)(2,1)S(1)} %get-tuple-element.30.dpre), channel_id=1, source_target_pairs={{0,16},{16,0},{1,17},{17,1},{2,18},{18,2},{3,19},{19,3},{4,20},{20... | collective-permute-start | bytes 786440 | tf_op jit(solution)/shard_map/ppermute | solution.py:40
  104.0 1.5 copy-start
  220.8 17.7 %collective-permute-start.8 = (bf16[64,224,128]{2,1,0:T(8,128)(2,1)}, bf16[64,224,128]{2,1,0:T(8,128)(2,1)}, u32[]{:S(2)}, u32[]{:S(2)}) collective-permute-start(bf16[64,224,128]{2,1,0:T(8,128)(2,1)} %all_to_all.23.chunks), channel_id=1, source_target_pairs={{0,16},{16,0},{1,17},{17,1},{2,18},{18,2},{3,19},{19,3},{4,20},{20... | collective-permute-start | bytes 11010056 | tf_op jit(solution)/shard_map/ppermute | solution.py:40
  224.6 5.7 %collective-permute-start.9 = (f32[8,128]{1,0:T(8,128)S(1)}, f32[8,128]{1,0:T(8,128)S(1)}, u32[]{:S(2)}, u32[]{:S(2)}) collective-permute-start(f32[8,128]{1,0:T(8,128)S(1)} %get-tuple-element.37), channel_id=1, source_target_pairs={{0,16},{16,0},{1,17},{17,1},{2,18},{18,2},{3,19},{19,3},{4,20},{20... | collective-permute-start | bytes 12296 | tf_op jit(solution)/shard_map/ppermute | solution.py:40

commit v3 on v2

--- a/solution.py
+++ b/solution.py
@@ -50,7 +50,7 @@
     return lax.all_to_all(value, PEERS, 0, 0, tiled=True)
 
 
-def call(kernel, outs, *args, scratch=(), flops=0, moved=0):
+def call(kernel, outs, *args, scratch=(), vmem=16):
     specs = [
         pl.BlockSpec(memory_space=pltpu.SMEM if a.dtype == jnp.int32 else pltpu.VMEM) for a in args
     ]
@@ -60,8 +60,7 @@
         in_specs=specs,
         out_specs=[pl.BlockSpec(memory_space=pltpu.VMEM) for _ in outs],
         scratch_shapes=list(scratch),
-        compiler_params=pltpu.CompilerParams(vmem_limit_bytes=50 * 2**20),
-        cost_estimate=pl.CostEstimate(flops=flops, bytes_accessed=moved, transcendentals=0),
+        compiler_params=pltpu.CompilerParams(vmem_limit_bytes=vmem * 2**20),
     )(*args)
 
 
@@ -252,16 +251,16 @@
     re, rl = fe[6], fl[6]
     c = split(cov[1])
     u = split(dot3(re, c))
-    v = split(dot3(c, rl))
+    v = dot(c[0], rl[0]).astype(BF)
     k = dot3(u, rl)
     score[...] = jnp.broadcast_to(1.0 + jnp.sum(k * k, keepdims=True), score.shape)
     k2 = split(2.0 * k)
     gc = dot3(split(dot3(re, k2)), rl)
     grads[ch : 2 * ch] = gc.T.astype(BF)
     grads[2 * ch : 3 * ch] = gc.astype(BF)
-    gre = dot3(k2, v, NT)
+    gre = dot(k2[0], v, NT)
     grads[:ch] = backward(*fe[:6], gre + gre.T).astype(BF)
-    grl = dot3(u, k2, TN)
+    grl = dot(u[0], k2[0], TN)
     grads[3 * ch :] = backward(*fl[:6], grl + grl.T).astype(BF)
     for load in loads:
         load.wait()
@@ -390,9 +389,13 @@
         bias[...] = t[:n] + t[n:]
 
 
-def unpack_kernel(sizes, info, chunks, *refs):
+def unpack_kernel(sizes, nbiases, info, chunks, *refs):
     in_size, conv_size, nb = sizes
-    w_in, w_conv = refs[-2:]
+    if nbiases:
+        bias, bias_got = refs[:2]
+        w_in, w_conv, b_in, b_conv = refs[-4:]
+    else:
+        w_in, w_conv = refs[-2:]
     count = chunks.shape[0]
     for j in range(nb):
         part = chunks[:, j * in_size : (j + 1) * in_size, :].astype(F32)
@@ -402,6 +405,21 @@
             at = nb * in_size + (layer * (nb // 2) + j) * conv_size
             part = chunks[:, at : at + conv_size, :].astype(F32)
             w_conv[layer, :, j * LANES : (j + 1) * LANES] = part.reshape(count * conv_size, LANES)
+    if nbiases:
+
+        @pl.when(pl.program_id(0) == 0)
+        def _():
+            swapped = info[0] == 0
+            n = NL + 1
+            rows = []
+            for side in range(2):
+                keep = bias_got[...] if side == 0 else bias[...]
+                swap = bias[...] if side == 0 else bias_got[...]
+                value = jnp.where(swapped, keep, swap)
+                rows += [value[j * n : (j + 1) * n] for j in range(nb // 2)]
+            full = jnp.concatenate(rows, axis=1)
+            b_in[...] = full[0]
+            b_conv[...] = full[1:]
 
 
 def per_device(frames, w_in, b_in, w_conv, b_conv):
@@ -427,6 +445,7 @@
     own = squash0.astype(BF)
     before = shift_segment(own[rows - HALO :], 1)
     after = shift_segment(own[:HALO], -1)
+    before, after, frames_got = lax.optimization_barrier((before, after, frames_got))
     hid, sq, mine, other, means = call(
         functools.partial(forward_kernel, dims),
         [
@@ -438,6 +457,7 @@
         ],
         info, before, own, after, w_conv, b_conv,
         scratch=[pltpu.VMEM((3, ch, ch), F32)],
+        vmem=36,
     )
     (packed,) = call(
         functools.partial(pair_kernel, dims),
@@ -467,6 +487,7 @@
     smem = pl.BlockSpec(memory_space=pltpu.SMEM)
     hbm = pl.BlockSpec(memory_space=pl.ANY)
     params = pltpu.CompilerParams(vmem_limit_bytes=50 * 2**20)
+    small_params = pltpu.CompilerParams(vmem_limit_bytes=16 * 2**20)
     score, mine, other, dpre = pl.pallas_call(
         functools.partial(step_kernel, dims),
         out_shape=[
@@ -509,7 +530,7 @@
             out_specs=pl.BlockSpec((group, wide, LANES), lambda i, at: (i, 0, 0)),
         ),
         out_shape=sds((peers, wide, LANES), BF),
-        compiler_params=params,
+        compiler_params=small_params,
     )(info, frames, frames_got, dpre, swap_core(dpre), mine, swap_core(other))
     arrived = exchange(packed)
     block = 32
@@ -525,38 +546,40 @@
             pl.BlockSpec((peers, block, LANES), lambda i: (0, i, 0)),
             pl.BlockSpec((nbias, LANES), lambda i: (0, 0)),
         ],
-        compiler_params=params,
+        compiler_params=small_params,
     )(arrived, arrived)
     bias_got = swap_core(bias)
     full = exchange(full)
     steps = 8
     group = peers // steps
 
-    def unpack(chunks, at, earlier):
+    def unpack(chunks, at, biases, earlier):
+        spare = [sds((ch,), F32), sds((NL, ch), F32)] if biases else []
         return pl.pallas_call(
-            functools.partial(unpack_kernel, (in_size, conv_size, nb)),
+            functools.partial(unpack_kernel, (in_size, conv_size, nb), len(biases)),
             grid_spec=pltpu.PrefetchScalarGridSpec(
                 num_scalar_prefetch=1,
                 grid=(steps,),
                 in_specs=[pl.BlockSpec((group, body, LANES), lambda i, at: (i, 0, 0))]
+                + [pl.BlockSpec(b.shape, lambda i, at: (0, 0)) for b in biases]
                 + [hbm] * len(earlier),
                 out_specs=[
                     pl.BlockSpec((1, group * in_size, ch), lambda i, at: (at[0], i, 0)),
                     pl.BlockSpec((NL, group * conv_size, ch // 2), lambda i, at: (0, i, at[0])),
-                ],
+                ]
+                + [pl.BlockSpec(b.shape, lambda i, at, n=len(b.shape): (0,) * n) for b in spare],
             ),
-            out_shape=[sds((2, half_features, ch), F32), sds((NL, 2 * ch, ch), F32)],
-            input_output_aliases={2 + n: n for n in range(len(earlier))},
-            compiler_params=params,
+            out_shape=[sds((2, half_features, ch), F32), sds((NL, 2 * ch, ch), F32)] + spare,
+            input_output_aliases={2 + len(biases) + n: n for n in range(len(earlier))},
+            compiler_params=small_params,
             cost_estimate=pl.CostEstimate(flops=0, bytes_accessed=12 * 2**20, transcendentals=0),
-        )(at, chunks, *earlier)
+        )(at, chunks, *biases, *earlier)
 
     got = swap_core(full)
-    partial = unpack(full, info[:1], [])
-    g_in, g_conv = unpack(got, 1 - info[:1], partial)
-    both = jnp.where(core == 0, jnp.stack([bias, bias_got]), jnp.stack([bias_got, bias]))
-    g_bias = both.reshape(2, nh, NL + 1, LANES).transpose(2, 0, 1, 3).reshape(NL + 1, ch)
-    return score[0, 0], g_in.reshape(features, ch), g_bias[0], g_conv, g_bias[1:]
+    partial = unpack(full, info[:1], [], [])
+    got, bias_got = lax.optimization_barrier((got, bias_got))
+    g_in, g_conv, g_b_in, g_b_conv = unpack(got, 1 - info[:1], [bias, bias_got], partial)
+    return score[0, 0], g_in.reshape(features, ch), g_b_in, g_conv, g_b_conv
 
 
 def solution(mesh):

time: 246 us -> 227 us (0.923)
  Pallas kernels: 53.8 us -> 39.1 us
  waiting for transfers between devices: 17.2 us -> 9.47 us
    pallas_call x2, Pallas kernels: 14 us -> 8.52 us  [unpack(): pl.pallas_call(functools.partial(unpack_kernel, (in_size, conv_size, nb),...]
    ppermute x8, waiting for transfers between devices: 13.7 us -> 8.55 us  [swap_core(): return lax.ppermute(value, 'c', [(0, 1), (1, 0)])]
    pallas_call x1, Pallas kernels: 5.47 us -> 2.68 us  [per_device(): pl.pallas_call(sum_kernel, grid=(body // block,), out_shape=[sds((peers,...]
    pallas_call x3, Pallas kernels: 10 us -> 7.36 us  [call(): pl.pallas_call(kernel, out_shape=outs, in_specs=specs, out_specs=[pl.Bloc...]
    ppermute x2, waiting for transfers between devices: 3.46 us -> 0.92 us  [shift_segment(): lax.ppermute(value, 'tm', [(i, i + steps) for i in range(first, last)])]
  transfers between devices with their start and end apart: 10 -> 10, of which waited for: 6 -> 5; matrix products, arithmetic and copies ran while one was open for 1% -> 2% of each run, Pallas kernels for 3% -> 2%
where the time goes in v3:
time: 227 us
  blocking collectives  152 us (67%)
  Pallas kernels  39.1 us (17%)
  starting transfers between devices  15.6 us (7%)
  waiting for transfers between devices  9.47 us (4%)
  matrix products  4.92 us (2%)
  local copies, waits for them, and re-layouts  4.35 us (2%)
    all_to_all x4, blocking collectives, exchange(): return lax.all_to_all(value, PEERS, 0, 0, tiled=True)  152 us
    pallas_call x1, Pallas kernels, per_device(): pl.pallas_call(functools.partial(step_kernel, dims), out_shape=[sds((8, L...  16.2 us
    ppermute x8, starting transfers between devices, swap_core(): return lax.ppermute(value, 'c', [(0, 1), (1, 0)])  9.84 us
    ppermute x8, waiting for transfers between devices, swap_core(): return lax.ppermute(value, 'c', [(0, 1), (1, 0)])  8.55 us
    pallas_call x2, Pallas kernels, unpack(): pl.pallas_call(functools.partial(unpack_kernel, (in_size, conv_size, nb),...  8.52 us
    pallas_call x3, Pallas kernels, call(): pl.pallas_call(kernel, out_shape=outs, in_specs=specs, out_specs=[pl.Bloc...  7.36 us
    ppermute x2, starting transfers between devices, shift_segment(): lax.ppermute(value, 'tm', [(i, i + steps) for i in range(first, last)])  5.8 us
    dot_general x1, matrix products, per_device(): squash0 = jnp.tanh(jnp.dot(frames, w_in, preferred_element_type=F32) + b_in)  4.92 us
  transfers between devices with their start and end apart: 10, of which 5 were waited for; matrix products, arithmetic and copies ran while one was open for 2% of the time, Pallas kernels for 2%

profile of v3, /device:TPU:1, one launch (start us, length us, event | category | flops | bytes accessed | tf_op | source)
XLA Modules:
  0.0 226.8 jit_solution(14280674382856652480)
XLA Ops:
  0.6 2.3 %dynamic-slice_bitcast_fusion = bf16[256,2048]{1,0:T(8,128)(2,1)} fusion(bf16[1,256,4096]{2,1,0:T(8,128)(2,1)} %param.5, s32[]{:T(128)S(6)} %select_n.3), kind=kLoop, calls=%fused_computation.2 | loop fusion | bytes 2097156 | tf_op jit(solution)/shard_map/dynamic_slice | solution.py:441
  2.9 0.0 copy-start
  2.9 0.0 copy-start.5
  3.0 1.4 collective-permute-start.2
  4.4 4.9 %fusion.3 = (bf16[256,512]{1,0:T(8,128)(2,1)S(1)}, f32[256,512]{1,0:T(8,128)}) fusion(f32[512]{0:T(512)} %param.7, bf16[4096,512]{1,0:T(8,128)(2,1)} %param.6, bf16[1,256,4096]{2,1,0:T(8,128)(2,1)} %param.5), kind=kOutput, calls=%fused_computation.6 | convolution fusion | flops 1074003968 | bytes 7079936 | tf_op jit(solution)/shard_map/dot_general | solution.py:444
  9.3 1.3 collective-permute-start.1
  10.6 4.5 %collective-permute-start = (bf16[32,512]{1,0:T(8,128)(2,1)S(1)}, bf16[32,512]{1,0:T(8,128)(2,1)S(1)}, u32[]{:S(2)}, u32[]{:S(2)}) collective-permute-start(bf16[32,512]{1,0:T(8,128)(2,1)S(1)} %get-tuple-element.54), channel_id=1, source_target_pairs={{0,1},{1,2},{2,3},{3,4},{4,5},{5,6},{6,7},{7,8},{8,9},{9,10},{10,1... | collective-permute-start | bytes 98312 | tf_op jit(solution)/shard_map/ppermute | solution.py:46
  15.1 0.1 pad_add_fusion.info
  15.2 0.0 collective-permute-done.1.after
  15.2 0.9 collective-permute-done.before
  16.1 0.0 collective-permute-done.2.left_got
  16.1 0.0 copy-done
  16.1 0.0 copy-done.5
  16.1 3.9 %shard_map.92 = (bf16[4,320,512]{2,1,0:T(8,128)(2,1)S(1)}, f32[3,320,512]{2,1,0:T(8,128)S(1)}, f32[64,48,128]{2,1,0:T(8,128)S(1)}, bf16[64,48,128]{2,1,0:T(8,128)(2,1)S(1)}, f32[8,512]{1,0:T(8,128)S(1)}) custom-call(s32[3]{0:T(128)S(1)} %pad_add_fusion.info, bf16[32,512]{1,0:T(8,128)(2,1)S(1)} %collective-permute-done.before, ...), custom_call_target="tpu_custom_call" | custom-call | tf_op jit(solution)/shard_map/pallas_call | solution.py:57
  20.1 0.0 copy-start.2
  20.1 0.8 collective-permute-start.3
  20.9 0.1 collective-permute-start.4
  21.0 1.8 collective-permute-done.4.sib
  22.9 0.0 collective-permute-done.3.got
  22.9 0.0 copy-start.4
  22.9 2.0 shard_map.93
  24.8 30.8 %all_to_all.20.arrived = bf16[64,64,128]{2,1,0:T(8,128)(2,1)S(1)} all-to-all(bf16[64,64,128]{2,1,0:T(8,128)(2,1)S(1)} %shard_map.93), channel_id=1, replica_groups=mesh['x'=4,'c'=2,'tm'=16] {'x','tm'}, dimensions={0} | all-to-all | bytes 2097152 | tf_op jit(solution)/shard_map/all_to_all | solution.py:50
  55.7 1.5 shard_map.94
  57.1 19.0 %all_to_all.21.half_cov = bf16[64,48,128]{2,1,0:T(8,128)(2,1)S(1)} all-to-all(bf16[64,48,128]{2,1,0:T(8,128)(2,1)S(1)} %get-tuple-element.34), channel_id=1, replica_groups=mesh['x'=4,'c'=2,'tm'=16] {'x','tm'}, dimensions={0} | all-to-all | bytes 1572864 | tf_op jit(solution)/shard_map/all_to_all | solution.py:50
  76.1 0.0 copy-done.2
  76.2 3.1 %collective-permute-start.5 = (bf16[64,48,128]{2,1,0:T(8,128)(2,1)S(1)}, bf16[64,48,128]{2,1,0:T(8,128)(2,1)S(1)}, u32[]{:S(2)}, u32[]{:S(2)}) collective-permute-start(bf16[64,48,128]{2,1,0:T(8,128)(2,1)S(1)} %all_to_all.21.half_cov), channel_id=1, source_target_pairs={{0,16},{16,0},{1,17},{17,1},{2,18},{18,2},{3,19},{19,3},{4,20},{20... | collective-permute-start | bytes 2359304 | tf_op jit(solution)/shard_map/ppermute | solution.py:40
  79.3 1.9 collective-permute-done.5.other_cov
  81.2 0.0 copy-done.4
  81.2 0.0 copy-start.1
  81.2 16.2 %shard_map.95 = (f32[8,128]{1,0:T(8,128)S(1)}, bf16[64,112,128]{2,1,0:T(8,128)(2,1)}, bf16[64,112,128]{2,1,0:T(8,128)(2,1)}, bf16[256,512]{1,0:T(8,128)(2,1)S(1)}) custom-call(s32[3]{0:T(128)S(1)} %pad_add_fusion.info, bf16[64,48,128]{2,1,0:T(8,128)(2,1)S(1)} %all_to_all.21.half_cov, bf16[64,48,128]{2,1,0:T(8,128)(2,1)S(1)} %collective-permute-done.5.other_cov, ...), custom_call_target="tpu_custom_call" | custom-call | tf_op jit(solution)/shard_map/pallas_call | solution.py:491
  97.4 0.5 collective-permute-start.7
  97.8 0.3 collective-permute-start.6
  98.1 3.5 %collective-permute-done.6.dpre_got = bf16[256,512]{1,0:T(8,128)(2,1)S(1)} collective-permute-done((bf16[256,512]{1,0:T(8,128)(2,1)S(1)}, bf16[256,512]{1,0:T(8,128)(2,1)S(1)}, u32[]{:S(2)}, u32[]{:S(2)}) %collective-permute-start.6) | collective-permute-done | bytes 262176 | tf_op jit(solution)/shard_map/ppermute | solution.py:40
  101.6 0.0 collective-permute-done.7.got
  101.6 0.0 copy-done.1
  101.6 0.0 copy-start.3
  101.6 1.5 copy-done.3
  103.1 4.4 %shard_map.96 = bf16[64,240,128]{2,1,0:T(8,128)(2,1)S(1)} custom-call(s32[3]{0:T(128)S(1)} %pad_add_fusion.info, bf16[256,4096]{1,0:T(8,128)(2,1)S(1)} %bitcast.13, bf16[256,2048]{1,0:T(8,128)(2,1)} %collective-permute-done.2.left_got, bf16[256,512]{1,0:T(8,128)(2,1)S(1)} %get-tuple-element.40.dpre, bf16[256,512]{1,0:T(8,128)(2,1)S(1)} %collective-permute-done.6.dpre_got, ...), custom_call_target="tpu_custom_call" | custom-call | tf_op jit(solution)/shard_map/pallas_call | solution.py:517
  107.5 51.7 %all_to_all.22.arrived.tails = bf16[64,240,128]{2,1,0:T(8,128)(2,1)S(1)} all-to-all(bf16[64,240,128]{2,1,0:T(8,128)(2,1)S(1)} %shard_map.96), channel_id=1, replica_groups=mesh['x'=4,'c'=2,'tm'=16] {'x','tm'}, dimensions={0} | all-to-all | bytes 7864320 | tf_op jit(solution)/shard_map/all_to_all | solution.py:50
  159.2 2.7 %shard_map.97 = (bf16[64,224,128]{2,1,0:T(8,128)(2,1)S(1)}, f32[8,128]{1,0:T(8,128)S(1)}) custom-call(bf16[64,240,128]{2,1,0:T(8,128)(2,1)S(1)} %all_to_all.22.arrived.tails, bf16[64,240,128]{2,1,0:T(8,128)(2,1)S(1)} %all_to_all.22.arrived.tails), custom_call_target="tpu_custom_call" | custom-call | tf_op jit(solution)/shard_map/pallas_call | solution.py:537
  161.9 51.0 %all_to_all.23.chunks = bf16[64,224,128]{2,1,0:T(8,128)(2,1)S(1)} all-to-all(bf16[64,224,128]{2,1,0:T(8,128)(2,1)S(1)} %get-tuple-element.43), channel_id=1, replica_groups=mesh['x'=4,'c'=2,'tm'=16] {'x','tm'}, dimensions={0} | all-to-all | bytes 7340032 | tf_op jit(solution)/shard_map/all_to_all | solution.py:50
  212.8 3.6 %collective-permute-start.8 = (bf16[64,224,128]{2,1,0:T(8,128)(2,1)S(1)}, bf16[64,224,128]{2,1,0:T(8,128)(2,1)S(1)}, u32[]{:S(2)}, u32[]{:S(2)}) collective-permute-start(bf16[64,224,128]{2,1,0:T(8,128)(2,1)S(1)} %all_to_all.23.chunks), channel_id=1, source_target_pairs={{0,16},{16,0},{1,17},{17,1},{2,18},{18,2},{3,19},{19,3},{4,20},{20... | collective-permute-start | bytes 11010056 | tf_op jit(solution)/shard_map/ppermute | solution.py:40
  216.4 0.0 collective-permute-start.9
  216.4 0.5 slice.11
  216.9 4.2 %shard_map.98 = (f32[2,2048,512]{2,1,0:T(8,128)}, f32[3,1024,512]{2,1,0:T(8,128)}) custom-call(s32[1]{0:T(128)} %bitcast.info, bf16[64,224,128]{2,1,0:T(8,128)(2,1)S(1)} %all_to_all.23.chunks), custom_call_target="tpu_custom_call" | custom-call | bytes 12582912 | tf_op jit(solution)/shard_map/pallas_call | solution.py:558
  221.1 1.3 collective-permute-done.9.refs_1_
  222.4 0.0 collective-permute-done.8.chunks
  222.5 4.3 %shard_map.99 = (f32[2,2048,512]{2,1,0:T(8,128)}, f32[3,1024,512]{2,1,0:T(8,128)}, f32[512]{0:T(512)}, f32[3,512]{1,0:T(4,128)}) custom-call(s32[1]{0:T(128)S(6)} %sub.7.info, bf16[64,224,128]{2,1,0:T(8,128)(2,1)S(1)} %collective-permute-done.8.chunks, f32[8,128]{1,0:T(8,128)S(1)} %get-tuple-element.44.refs_0_, ...), custom_call_target="tpu_custom_call", output_to_operand_aliasing={{0}: (4, {}), {1}: (5, {})} | custom-call | bytes 12582912 | tf_op jit(solution)/shard_map/pallas_call | solution.py:558
  (1 shorter events, 0.0 us)
Async XLA Ops:
  2.9 13.2 %copy-start = (bf16[3,1024,512]{2,1,0:T(8,128)(2,1)S(1)}, bf16[3,1024,512]{2,1,0:T(8,128)(2,1)}, u32[]{:S(2)}) copy-start(bf16[3,1024,512]{2,1,0:T(8,128)(2,1)} %w_hbm.1) | copy-start | bytes 9437188
  2.9 13.2 %copy-start.5 = (f32[3,512]{1,0:T(4,128)S(1)}, f32[3,512]{1,0:T(4,128)}, u32[]{:S(2)}) copy-start(f32[3,512]{1,0:T(4,128)} %b.1) | copy-start | bytes 18436
  3.0 13.2 %collective-permute-start.2 = (bf16[256,2048]{1,0:T(8,128)(2,1)}, bf16[256,2048]{1,0:T(8,128)(2,1)}, u32[]{:S(2)}, u32[]{:S(2)}) collective-permute-start(bf16[256,2048]{1,0:T(8,128)(2,1)} %dynamic-slice_bitcast_fusion), channel_id=1, source_target_pairs={{0,16},{16,0},{1,17},{17,1},{2,18},{18,2},{3,19},{19,3},{4,20},{20... | collective-permute-start | bytes 3145736 | tf_op jit(solution)/shard_map/ppermute | solution.py:40
  9.3 5.9 %collective-permute-start.1 = (bf16[32,512]{1,0:T(8,128)(2,1)S(1)}, bf16[32,512]{1,0:T(8,128)(2,1)S(1)}, u32[]{:S(2)}, u32[]{:S(2)}) collective-permute-start(bf16[32,512]{1,0:T(8,128)(2,1)S(1)} %get-tuple-element.53), channel_id=1, source_target_pairs={{1,0},{2,1},{3,2},{4,3},{5,4},{6,5},{7,6},{8,7},{9,8},{10,9},{11,1... | collective-permute-start | bytes 98312 | tf_op jit(solution)/shard_map/ppermute | solution.py:46
  10.6 5.5 %collective-permute-start = (bf16[32,512]{1,0:T(8,128)(2,1)S(1)}, bf16[32,512]{1,0:T(8,128)(2,1)S(1)}, u32[]{:S(2)}, u32[]{:S(2)}) collective-permute-start(bf16[32,512]{1,0:T(8,128)(2,1)S(1)} %get-tuple-element.54), channel_id=1, source_target_pairs={{0,1},{1,2},{2,3},{3,4},{4,5},{5,6},{6,7},{7,8},{8,9},{9,10},{10,1... | collective-permute-start | bytes 98312 | tf_op jit(solution)/shard_map/ppermute | solution.py:46
  20.1 56.1 %copy-start.2 = (f32[3,320,512]{2,1,0:T(8,128)}, f32[3,320,512]{2,1,0:T(8,128)S(1)}, u32[]{:S(2)}) copy-start(f32[3,320,512]{2,1,0:T(8,128)S(1)} %get-tuple-element.37.sq_hbm) | copy-start | bytes 5898244
  20.1 2.8 %collective-permute-start.3 = (bf16[64,48,128]{2,1,0:T(8,128)(2,1)S(1)}, bf16[64,48,128]{2,1,0:T(8,128)(2,1)S(1)}, u32[]{:S(2)}, u32[]{:S(2)}) collective-permute-start(bf16[64,48,128]{2,1,0:T(8,128)(2,1)S(1)} %get-tuple-element.32), channel_id=1, source_target_pairs={{0,16},{16,0},{1,17},{17,1},{2,18},{18,2},{3,19},{19,3},{4,20},{20... | collective-permute-start | bytes 2359304 | tf_op jit(solution)/shard_map/ppermute | solution.py:40
  20.9 1.9 collective-permute-start.4
  22.9 58.4 %copy-start.4 = (f32[256,512]{1,0:T(8,128)S(1)}, f32[256,512]{1,0:T(8,128)}, u32[]{:S(2)}) copy-start(f32[256,512]{1,0:T(8,128)} %get-tuple-element.56.sq0_hbm) | copy-start | bytes 1572868
  76.2 5.1 %collective-permute-start.5 = (bf16[64,48,128]{2,1,0:T(8,128)(2,1)S(1)}, bf16[64,48,128]{2,1,0:T(8,128)(2,1)S(1)}, u32[]{:S(2)}, u32[]{:S(2)}) collective-permute-start(bf16[64,48,128]{2,1,0:T(8,128)(2,1)S(1)} %all_to_all.21.half_cov), channel_id=1, source_target_pairs={{0,16},{16,0},{1,17},{17,1},{2,18},{18,2},{3,19},{19,3},{4,20},{20... | collective-permute-start | bytes 2359304 | tf_op jit(solution)/shard_map/ppermute | solution.py:40
  81.2 20.4 %copy-start.1 = (bf16[1,256,4096]{2,1,0:T(8,128)(2,1)S(1)}, bf16[1,256,4096]{2,1,0:T(8,128)(2,1)}, u32[]{:S(2)}) copy-start(bf16[1,256,4096]{2,1,0:T(8,128)(2,1)} %param.5) | copy-start | bytes 6291460
  97.4 4.2 %collective-permute-start.7 = (bf16[64,112,128]{2,1,0:T(8,128)(2,1)}, bf16[64,112,128]{2,1,0:T(8,128)(2,1)S(1)}, u32[]{:S(2)}, u32[]{:S(2)}) collective-permute-start(bf16[64,112,128]{2,1,0:T(8,128)(2,1)} %get-tuple-element.42), channel_id=1, source_target_pairs={{0,16},{16,0},{1,17},{17,1},{2,18},{18,2},{3,19},{19,3},{4,20},{20... | collective-permute-start | bytes 5505032 | tf_op jit(solution)/shard_map/ppermute | solution.py:40
  97.8 3.8 %collective-permute-start.6 = (bf16[256,512]{1,0:T(8,128)(2,1)S(1)}, bf16[256,512]{1,0:T(8,128)(2,1)S(1)}, u32[]{:S(2)}, u32[]{:S(2)}) collective-permute-start(bf16[256,512]{1,0:T(8,128)(2,1)S(1)} %get-tuple-element.40.dpre), channel_id=1, source_target_pairs={{0,16},{16,0},{1,17},{17,1},{2,18},{18,2},{3,19},{19,3},{4,20},{20... | collective-permute-start | bytes 786440 | tf_op jit(solution)/shard_map/ppermute | solution.py:40
  101.6 1.5 copy-start.3
  212.8 9.6 %collective-permute-start.8 = (bf16[64,224,128]{2,1,0:T(8,128)(2,1)S(1)}, bf16[64,224,128]{2,1,0:T(8,128)(2,1)S(1)}, u32[]{:S(2)}, u32[]{:S(2)}) collective-permute-start(bf16[64,224,128]{2,1,0:T(8,128)(2,1)S(1)} %all_to_all.23.chunks), channel_id=1, source_target_pairs={{0,16},{16,0},{1,17},{17,1},{2,18},{18,2},{3,19},{19,3},{4,20},{20... | collective-permute-start | bytes 11010056 | tf_op jit(solution)/shard_map/ppermute | solution.py:40
  216.4 6.0 %collective-permute-start.9 = (f32[8,128]{1,0:T(8,128)S(1)}, f32[8,128]{1,0:T(8,128)S(1)}, u32[]{:S(2)}, u32[]{:S(2)}) collective-permute-start(f32[8,128]{1,0:T(8,128)S(1)} %get-tuple-element.44.refs_0_), channel_id=1, source_target_pairs={{0,16},{16,0},{1,17},{17,1},{2,18},{18,2},{3,19},{19,3},{4,20},{20... | collective-permute-start | bytes 12296 | tf_op jit(solution)/shard_map/ppermute | solution.py:40

commit v4 on v3

--- a/solution.py
+++ b/solution.py
@@ -229,11 +229,12 @@
         ab = a.astype(BF)
         a2 = dot(ab, ab)
         a2b = a2.astype(BF)
-        poly = C0 * unit + C1 * a + C2 * a2 + dot(a2b, (C3 * a + C4 * a2).astype(BF))
+        rest = C1 * a + C2 * a2 + dot(a2b, (C3 * a + C4 * a2).astype(BF))
         root = jnp.sqrt(inv_scale)
-        return a, ab, a2b, poly, inv_scale, root, split(poly * root)
-
-    def backward(a, ab, a2b, poly, inv_scale, root, grad):
+        return a, ab, a2b, rest, inv_scale, root, C0 * root, (rest * root).astype(BF)
+
+    def backward(a, ab, a2b, rest, inv_scale, root, grad):
+        poly = C0 * unit + rest
         dscale = -0.5 * jnp.sum(grad * poly, keepdims=True) * root * inv_scale
         g = grad * root
         gb = g.astype(BF)
@@ -248,19 +249,24 @@
 
     fe = forward(cov[0])
     fl = forward(cov[2])
-    re, rl = fe[6], fl[6]
-    c = split(cov[1])
-    u = split(dot3(re, c))
-    v = dot(c[0], rl[0]).astype(BF)
-    k = dot3(u, rl)
+    alpha, re = fe[6:]
+    beta, rl = fl[6:]
+    c = cov[1]
+    cb = c.astype(BF)
+    u = alpha * c + dot(re, cb)
+    ub = u.astype(BF)
+    vb = (beta * c + dot(cb, rl)).astype(BF)
+    k = beta * u + dot(ub, rl)
     score[...] = jnp.broadcast_to(1.0 + jnp.sum(k * k, keepdims=True), score.shape)
-    k2 = split(2.0 * k)
-    gc = dot3(split(dot3(re, k2)), rl)
+    k2 = 2.0 * k
+    kb = k2.astype(BF)
+    rk = alpha * k2 + dot(re, kb)
+    gc = beta * rk + dot(rk.astype(BF), rl)
     grads[ch : 2 * ch] = gc.T.astype(BF)
     grads[2 * ch : 3 * ch] = gc.astype(BF)
-    gre = dot(k2[0], v, NT)
+    gre = dot(kb, vb, NT)
     grads[:ch] = backward(*fe[:6], gre + gre.T).astype(BF)
-    grl = dot(u[0], k2[0], TN)
+    grl = dot(ub, kb, TN)
     grads[3 * ch :] = backward(*fl[:6], grl + grl.T).astype(BF)
     for load in loads:
         load.wait()
@@ -437,15 +443,12 @@
     dims = (rows, ch, length, peers, piece)
     info = jnp.stack([core, segment, lax.axis_index("x") * segments + segment]).astype(jnp.int32)
     ext = rows + 2 * HALO
-    frames_got = swap_core(
-        lax.dynamic_slice_in_dim(frames, (1 - core) * (features // 2), features // 2, 1)
-    )
+    frames_got = swap_core(frames)
 
     squash0 = jnp.tanh(jnp.dot(frames, w_in, preferred_element_type=F32) + b_in)
     own = squash0.astype(BF)
     before = shift_segment(own[rows - HALO :], 1)
     after = shift_segment(own[:HALO], -1)
-    before, after, frames_got = lax.optimization_barrier((before, after, frames_got))
     hid, sq, mine, other, means = call(
         functools.partial(forward_kernel, dims),
         [
@@ -459,10 +462,13 @@
         scratch=[pltpu.VMEM((3, ch, ch), F32)],
         vmem=36,
     )
+    got, sib, frames_got = lax.optimization_barrier(
+        (swap_core(other), swap_core(means), frames_got)
+    )
     (packed,) = call(
         functools.partial(pair_kernel, dims),
         [sds((peers, 3 * piece + 4 * nb, LANES), BF)],
-        info, mine, swap_core(other), means, swap_core(means),
+        info, mine, got, means, sib,
         scratch=[pltpu.VMEM((ch, 8), F32)],
     )
     cov, mean_all = call(
@@ -486,7 +492,7 @@
     vmem = pl.BlockSpec(memory_space=pltpu.VMEM)
     smem = pl.BlockSpec(memory_space=pltpu.SMEM)
     hbm = pl.BlockSpec(memory_space=pl.ANY)
-    params = pltpu.CompilerParams(vmem_limit_bytes=50 * 2**20)
+    params = pltpu.CompilerParams(vmem_limit_bytes=40 * 2**20)
     small_params = pltpu.CompilerParams(vmem_limit_bytes=16 * 2**20)
     score, mine, other, dpre = pl.pallas_call(
         functools.partial(step_kernel, dims),
@@ -521,7 +527,7 @@
             grid=(steps,),
             in_specs=[
                 pl.BlockSpec((rows, tile), lambda i, at: (0, at[0] * steps + i)),
-                pl.BlockSpec((rows, tile), lambda i, at: (0, i)),
+                pl.BlockSpec((rows, tile), lambda i, at: (0, at[0] * steps + i)),
                 whole,
                 whole,
                 conv_spec,

time: 227 us -> 220 us (0.969)
  local copies, waits for them, and re-layouts: 4.35 us -> 0.53 us
  Pallas kernels: 39.1 us -> 35.6 us
    pallas_call x1, Pallas kernels: 16.2 us -> 12.7 us  [per_device(): pl.pallas_call(functools.partial(step_kernel, dims), out_shape=[sds((8, L...]
    dynamic_slice x1 -> x0, local copies, waits for them, and re-layouts: 2.31 us -> none  [per_device(): lax.dynamic_slice_in_dim(frames, (1 - core) * (features // 2), features /...]
  transfers between devices with their start and end apart: 10 -> 10, of which waited for: 5 -> 5; matrix products, arithmetic and copies ran while one was open for 2% -> 3% of each run, Pallas kernels for 2% -> 4%
where the time goes in v4:
time: 220 us
  blocking collectives  152 us (69%)
  Pallas kernels  35.6 us (16%)
  starting transfers between devices  15.6 us (7%)
  waiting for transfers between devices  9.65 us (4%)
  matrix products  4.92 us (2%)
    all_to_all x4, blocking collectives, exchange(): return lax.all_to_all(value, PEERS, 0, 0, tiled=True)  152 us
    pallas_call x1, Pallas kernels, per_device(): pl.pallas_call(functools.partial(step_kernel, dims), out_shape=[sds((8, L...  12.7 us
    ppermute x8, starting transfers between devices, swap_core(): return lax.ppermute(value, 'c', [(0, 1), (1, 0)])  9.86 us
    ppermute x8, waiting for transfers between devices, swap_core(): return lax.ppermute(value, 'c', [(0, 1), (1, 0)])  8.73 us
    pallas_call x2, Pallas kernels, unpack(): pl.pallas_call(functools.partial(unpack_kernel, (in_size, conv_size, nb),...  8.52 us
    pallas_call x3, Pallas kernels, call(): pl.pallas_call(kernel, out_shape=outs, in_specs=specs, out_specs=[pl.Bloc...  7.36 us
    ppermute x2, starting transfers between devices, shift_segment(): lax.ppermute(value, 'tm', [(i, i + steps) for i in range(first, last)])  5.71 us
    dot_general x1, matrix products, per_device(): squash0 = jnp.tanh(jnp.dot(frames, w_in, preferred_element_type=F32) + b_in)  4.92 us
  transfers between devices with their start and end apart: 10, of which 5 were waited for; matrix products, arithmetic and copies ran while one was open for 3% of the time, Pallas kernels for 4%

profile of v4, /device:TPU:1, one launch (start us, length us, event | category | flops | bytes accessed | tf_op | source)
XLA Modules:
  0.0 219.5 jit_solution(10343190091943256303)
XLA Ops:
  0.6 0.0 copy-start
  0.6 0.0 copy-start.3
  0.7 1.5 collective-permute-start.4
  2.2 4.9 %fusion.3 = (bf16[256,512]{1,0:T(8,128)(2,1)S(1)}, f32[256,512]{1,0:T(8,128)}) fusion(f32[512]{0:T(512)} %param.7, bf16[4096,512]{1,0:T(8,128)(2,1)} %param.6, bf16[1,256,4096]{2,1,0:T(8,128)(2,1)} %param.5), kind=kOutput, calls=%fused_computation.5 | convolution fusion | flops 1074003968 | bytes 7079936 | tf_op jit(solution)/shard_map/dot_general | solution.py:448
  7.1 1.3 collective-permute-start.1
  8.4 4.4 %collective-permute-start = (bf16[32,512]{1,0:T(8,128)(2,1)S(1)}, bf16[32,512]{1,0:T(8,128)(2,1)S(1)}, u32[]{:S(2)}, u32[]{:S(2)}) collective-permute-start(bf16[32,512]{1,0:T(8,128)(2,1)S(1)} %get-tuple-element.54), channel_id=1, source_target_pairs={{0,1},{1,2},{2,3},{3,4},{4,5},{5,6},{6,7},{7,8},{8,9},{9,10},{10,1... | collective-permute-start | bytes 98312 | tf_op jit(solution)/shard_map/ppermute | solution.py:46
  12.8 0.1 pad_add_fusion.info
  12.9 0.0 collective-permute-done.1.after
  12.9 0.9 collective-permute-done.before
  13.8 0.0 copy-done
  13.8 0.0 copy-done.3
  13.8 3.9 %shard_map.92 = (bf16[4,320,512]{2,1,0:T(8,128)(2,1)S(1)}, f32[3,320,512]{2,1,0:T(8,128)S(1)}, f32[64,48,128]{2,1,0:T(8,128)S(1)}, bf16[64,48,128]{2,1,0:T(8,128)(2,1)S(1)}, f32[8,512]{1,0:T(8,128)S(1)}) custom-call(s32[3]{0:T(128)S(1)} %pad_add_fusion.info, bf16[32,512]{1,0:T(8,128)(2,1)S(1)} %collective-permute-done.before, ...), custom_call_target="tpu_custom_call" | custom-call | tf_op jit(solution)/shard_map/pallas_call | solution.py:57
  17.7 0.9 collective-permute-start.2
  18.7 0.1 collective-permute-start.3
  18.8 1.8 collective-permute-done.3.sib
  20.6 0.0 collective-permute-done.2.got
  20.6 0.0 collective-permute-done.4.left_got
  20.6 0.0 copy-start.2
  20.6 2.0 shard_map.93
  22.6 30.8 %all_to_all.20.arrived = bf16[64,64,128]{2,1,0:T(8,128)(2,1)S(1)} all-to-all(bf16[64,64,128]{2,1,0:T(8,128)(2,1)S(1)} %shard_map.93), channel_id=1, replica_groups=mesh['x'=4,'c'=2,'tm'=16] {'x','tm'}, dimensions={0} | all-to-all | bytes 2097152 | tf_op jit(solution)/shard_map/all_to_all | solution.py:50
  53.4 1.5 shard_map.94
  54.9 19.0 %all_to_all.21.half_cov = bf16[64,48,128]{2,1,0:T(8,128)(2,1)S(1)} all-to-all(bf16[64,48,128]{2,1,0:T(8,128)(2,1)S(1)} %get-tuple-element.34), channel_id=1, replica_groups=mesh['x'=4,'c'=2,'tm'=16] {'x','tm'}, dimensions={0} | all-to-all | bytes 1572864 | tf_op jit(solution)/shard_map/all_to_all | solution.py:50
  73.9 3.1 %collective-permute-start.5 = (bf16[64,48,128]{2,1,0:T(8,128)(2,1)S(1)}, bf16[64,48,128]{2,1,0:T(8,128)(2,1)S(1)}, u32[]{:S(2)}, u32[]{:S(2)}) collective-permute-start(bf16[64,48,128]{2,1,0:T(8,128)(2,1)S(1)} %all_to_all.21.half_cov), channel_id=1, source_target_pairs={{0,16},{16,0},{1,17},{17,1},{2,18},{18,2},{3,19},{19,3},{4,20},{20... | collective-permute-start | bytes 2359304 | tf_op jit(solution)/shard_map/ppermute | solution.py:40
  77.1 1.9 collective-permute-done.5.other_cov
  79.0 0.0 copy-done.2
  79.0 0.0 copy-start.1
  79.0 12.7 %shard_map.95 = (f32[8,128]{1,0:T(8,128)S(1)}, bf16[64,112,128]{2,1,0:T(8,128)(2,1)S(1)}, bf16[64,112,128]{2,1,0:T(8,128)(2,1)S(1)}, bf16[256,512]{1,0:T(8,128)(2,1)S(1)}) custom-call(s32[3]{0:T(128)S(1)} %pad_add_fusion.info, bf16[64,48,128]{2,1,0:T(8,128)(2,1)S(1)} %all_to_all.21.half_cov, bf16[64,48,128]{2,1,0:T(8,128)(2,1)S(1)} %collective-permute-done.5.other_cov, ...), custom_call_target="tpu_custom_call" | custom-call | tf_op jit(solution)/shard_map/pallas_call | solution.py:497
  91.6 0.4 collective-permute-start.7
  92.1 0.1 collective-permute-start.6
  92.2 3.6 %collective-permute-done.6.dpre_got = bf16[256,512]{1,0:T(8,128)(2,1)S(1)} collective-permute-done((bf16[256,512]{1,0:T(8,128)(2,1)S(1)}, bf16[256,512]{1,0:T(8,128)(2,1)S(1)}, u32[]{:S(2)}, u32[]{:S(2)}) %collective-permute-start.6) | collective-permute-done | bytes 262176 | tf_op jit(solution)/shard_map/ppermute | solution.py:40
  95.9 0.0 collective-permute-done.7.got
  95.9 0.0 copy-done.1
  95.9 4.4 %shard_map.96 = bf16[64,240,128]{2,1,0:T(8,128)(2,1)S(1)} custom-call(s32[3]{0:T(128)S(1)} %pad_add_fusion.info, bf16[256,4096]{1,0:T(8,128)(2,1)S(1)} %bitcast.12, bf16[256,4096]{1,0:T(8,128)(2,1)} %collective-permute-done.4.left_got, bf16[256,512]{1,0:T(8,128)(2,1)S(1)} %get-tuple-element.40.dpre, bf16[256,512]{1,0:T(8,128)(2,1)S(1)} %collective-permute-done.6.dpre_got, ...), custom_call_target="tpu_custom_call" | custom-call | tf_op jit(solution)/shard_map/pallas_call | solution.py:523
  100.3 51.6 %all_to_all.22.arrived.tails = bf16[64,240,128]{2,1,0:T(8,128)(2,1)S(1)} all-to-all(bf16[64,240,128]{2,1,0:T(8,128)(2,1)S(1)} %shard_map.96), channel_id=1, replica_groups=mesh['x'=4,'c'=2,'tm'=16] {'x','tm'}, dimensions={0} | all-to-all | bytes 7864320 | tf_op jit(solution)/shard_map/all_to_all | solution.py:50
  151.9 2.7 %shard_map.97 = (bf16[64,224,128]{2,1,0:T(8,128)(2,1)S(1)}, f32[8,128]{1,0:T(8,128)S(1)}) custom-call(bf16[64,240,128]{2,1,0:T(8,128)(2,1)S(1)} %all_to_all.22.arrived.tails, bf16[64,240,128]{2,1,0:T(8,128)(2,1)S(1)} %all_to_all.22.arrived.tails), custom_call_target="tpu_custom_call" | custom-call | tf_op jit(solution)/shard_map/pallas_call | solution.py:543
  154.6 51.0 %all_to_all.23.chunks = bf16[64,224,128]{2,1,0:T(8,128)(2,1)S(1)} all-to-all(bf16[64,224,128]{2,1,0:T(8,128)(2,1)S(1)} %get-tuple-element.43), channel_id=1, replica_groups=mesh['x'=4,'c'=2,'tm'=16] {'x','tm'}, dimensions={0} | all-to-all | bytes 7340032 | tf_op jit(solution)/shard_map/all_to_all | solution.py:50
  205.5 3.6 %collective-permute-start.8 = (bf16[64,224,128]{2,1,0:T(8,128)(2,1)S(1)}, bf16[64,224,128]{2,1,0:T(8,128)(2,1)S(1)}, u32[]{:S(2)}, u32[]{:S(2)}) collective-permute-start(bf16[64,224,128]{2,1,0:T(8,128)(2,1)S(1)} %all_to_all.23.chunks), channel_id=1, source_target_pairs={{0,16},{16,0},{1,17},{17,1},{2,18},{18,2},{3,19},{19,3},{4,20},{20... | collective-permute-start | bytes 11010056 | tf_op jit(solution)/shard_map/ppermute | solution.py:40
  209.1 0.0 collective-permute-start.9
  209.1 0.5 slice.11
  209.7 4.2 %shard_map.98 = (f32[2,2048,512]{2,1,0:T(8,128)}, f32[3,1024,512]{2,1,0:T(8,128)}) custom-call(s32[1]{0:T(128)} %bitcast.info, bf16[64,224,128]{2,1,0:T(8,128)(2,1)S(1)} %all_to_all.23.chunks), custom_call_target="tpu_custom_call" | custom-call | bytes 12582912 | tf_op jit(solution)/shard_map/pallas_call | solution.py:564
  213.9 1.3 collective-permute-done.9.refs_1_
  215.2 0.0 collective-permute-done.8.chunks
  215.2 4.3 %shard_map.99 = (f32[2,2048,512]{2,1,0:T(8,128)}, f32[3,1024,512]{2,1,0:T(8,128)}, f32[512]{0:T(512)}, f32[3,512]{1,0:T(4,128)}) custom-call(s32[1]{0:T(128)S(6)} %sub.3.info, bf16[64,224,128]{2,1,0:T(8,128)(2,1)S(1)} %collective-permute-done.8.chunks, f32[8,128]{1,0:T(8,128)S(1)} %get-tuple-element.44.refs_0_, ...), custom_call_target="tpu_custom_call", output_to_operand_aliasing={{0}: (4, {}), {1}: (5, {})} | custom-call | bytes 12582912 | tf_op jit(solution)/shard_map/pallas_call | solution.py:564
  (1 shorter events, 0.0 us)
Async XLA Ops:
  0.6 13.2 %copy-start = (bf16[3,1024,512]{2,1,0:T(8,128)(2,1)S(1)}, bf16[3,1024,512]{2,1,0:T(8,128)(2,1)}, u32[]{:S(2)}) copy-start(bf16[3,1024,512]{2,1,0:T(8,128)(2,1)} %w_hbm.1) | copy-start | bytes 9437188
  0.6 13.2 %copy-start.3 = (f32[3,512]{1,0:T(4,128)S(1)}, f32[3,512]{1,0:T(4,128)}, u32[]{:S(2)}) copy-start(f32[3,512]{1,0:T(4,128)} %b.1) | copy-start | bytes 18436
  0.7 20.0 %collective-permute-start.4 = (bf16[256,4096]{1,0:T(8,128)(2,1)}, bf16[256,4096]{1,0:T(8,128)(2,1)}, u32[]{:S(2)}, u32[]{:S(2)}) collective-permute-start(bf16[256,4096]{1,0:T(8,128)(2,1)} %bitcast.11), channel_id=1, source_target_pairs={{0,16},{16,0},{1,17},{17,1},{2,18},{18,2},{3,19},{19,3},{4,20},{20... | collective-permute-start | bytes 6291464 | tf_op jit(solution)/shard_map/ppermute | solution.py:40
  7.1 5.8 %collective-permute-start.1 = (bf16[32,512]{1,0:T(8,128)(2,1)S(1)}, bf16[32,512]{1,0:T(8,128)(2,1)S(1)}, u32[]{:S(2)}, u32[]{:S(2)}) collective-permute-start(bf16[32,512]{1,0:T(8,128)(2,1)S(1)} %get-tuple-element.53), channel_id=1, source_target_pairs={{1,0},{2,1},{3,2},{4,3},{5,4},{6,5},{7,6},{8,7},{9,8},{10,9},{11,1... | collective-permute-start | bytes 98312 | tf_op jit(solution)/shard_map/ppermute | solution.py:46
  8.4 5.4 %collective-permute-start = (bf16[32,512]{1,0:T(8,128)(2,1)S(1)}, bf16[32,512]{1,0:T(8,128)(2,1)S(1)}, u32[]{:S(2)}, u32[]{:S(2)}) collective-permute-start(bf16[32,512]{1,0:T(8,128)(2,1)S(1)} %get-tuple-element.54), channel_id=1, source_target_pairs={{0,1},{1,2},{2,3},{3,4},{4,5},{5,6},{6,7},{7,8},{8,9},{9,10},{10,1... | collective-permute-start | bytes 98312 | tf_op jit(solution)/shard_map/ppermute | solution.py:46
  17.7 2.9 %collective-permute-start.2 = (bf16[64,48,128]{2,1,0:T(8,128)(2,1)S(1)}, bf16[64,48,128]{2,1,0:T(8,128)(2,1)S(1)}, u32[]{:S(2)}, u32[]{:S(2)}) collective-permute-start(bf16[64,48,128]{2,1,0:T(8,128)(2,1)S(1)} %get-tuple-element.30), channel_id=1, source_target_pairs={{0,16},{16,0},{1,17},{17,1},{2,18},{18,2},{3,19},{19,3},{4,20},{20... | collective-permute-start | bytes 2359304 | tf_op jit(solution)/shard_map/ppermute | solution.py:40
  18.7 1.9 collective-permute-start.3
  20.6 58.3 %copy-start.2 = (f32[256,512]{1,0:T(8,128)S(1)}, f32[256,512]{1,0:T(8,128)}, u32[]{:S(2)}) copy-start(f32[256,512]{1,0:T(8,128)} %get-tuple-element.56.sq0_hbm) | copy-start | bytes 1572868
  73.9 5.1 %collective-permute-start.5 = (bf16[64,48,128]{2,1,0:T(8,128)(2,1)S(1)}, bf16[64,48,128]{2,1,0:T(8,128)(2,1)S(1)}, u32[]{:S(2)}, u32[]{:S(2)}) collective-permute-start(bf16[64,48,128]{2,1,0:T(8,128)(2,1)S(1)} %all_to_all.21.half_cov), channel_id=1, source_target_pairs={{0,16},{16,0},{1,17},{17,1},{2,18},{18,2},{3,19},{19,3},{4,20},{20... | collective-permute-start | bytes 2359304 | tf_op jit(solution)/shard_map/ppermute | solution.py:40
  79.0 16.9 %copy-start.1 = (bf16[1,256,4096]{2,1,0:T(8,128)(2,1)S(1)}, bf16[1,256,4096]{2,1,0:T(8,128)(2,1)}, u32[]{:S(2)}) copy-start(bf16[1,256,4096]{2,1,0:T(8,128)(2,1)} %param.5) | copy-start | bytes 6291460
  91.6 4.2 %collective-permute-start.7 = (bf16[64,112,128]{2,1,0:T(8,128)(2,1)S(1)}, bf16[64,112,128]{2,1,0:T(8,128)(2,1)S(1)}, u32[]{:S(2)}, u32[]{:S(2)}) collective-permute-start(bf16[64,112,128]{2,1,0:T(8,128)(2,1)S(1)} %get-tuple-element.42), channel_id=1, source_target_pairs={{0,16},{16,0},{1,17},{17,1},{2,18},{18,2},{3,19},{19,3},{4,20},{20... | collective-permute-start | bytes 5505032 | tf_op jit(solution)/shard_map/ppermute | solution.py:40
  92.1 3.8 %collective-permute-start.6 = (bf16[256,512]{1,0:T(8,128)(2,1)S(1)}, bf16[256,512]{1,0:T(8,128)(2,1)S(1)}, u32[]{:S(2)}, u32[]{:S(2)}) collective-permute-start(bf16[256,512]{1,0:T(8,128)(2,1)S(1)} %get-tuple-element.40.dpre), channel_id=1, source_target_pairs={{0,16},{16,0},{1,17},{17,1},{2,18},{18,2},{3,19},{19,3},{4,20},{20... | collective-permute-start | bytes 786440 | tf_op jit(solution)/shard_map/ppermute | solution.py:40
  205.5 9.6 %collective-permute-start.8 = (bf16[64,224,128]{2,1,0:T(8,128)(2,1)S(1)}, bf16[64,224,128]{2,1,0:T(8,128)(2,1)S(1)}, u32[]{:S(2)}, u32[]{:S(2)}) collective-permute-start(bf16[64,224,128]{2,1,0:T(8,128)(2,1)S(1)} %all_to_all.23.chunks), channel_id=1, source_target_pairs={{0,16},{16,0},{1,17},{17,1},{2,18},{18,2},{3,19},{19,3},{4,20},{20... | collective-permute-start | bytes 11010056 | tf_op jit(solution)/shard_map/ppermute | solution.py:40
  209.1 6.0 %collective-permute-start.9 = (f32[8,128]{1,0:T(8,128)S(1)}, f32[8,128]{1,0:T(8,128)S(1)}, u32[]{:S(2)}, u32[]{:S(2)}) collective-permute-start(f32[8,128]{1,0:T(8,128)S(1)} %get-tuple-element.44.refs_0_), channel_id=1, source_target_pairs={{0,16},{16,0},{1,17},{17,1},{2,18},{18,2},{3,19},{19,3},{4,20},{20... | collective-permute-start | bytes 12296 | tf_op jit(solution)/shard_map/ppermute | solution.py:40

commit v5 on v4

--- a/solution.py
+++ b/solution.py
@@ -357,12 +357,15 @@
         ref[:, at:, :] = jnp.broadcast_to(tail[None], (peers,) + tail.shape)
 
 
-def pack_kernel(nbias, info, left, left_got, dpre, dpre_got, mine, got, packed):
+def product_kernel(info, left, dpre, res):
+    res[...] = dot(left[...], dpre[...], TN)
+
+
+def pack_kernel(nbias, info, earlier, left_got, dpre_got, mine, got, packed):
     count = packed.shape[0]
-    ch = dpre.shape[1]
-    size = left.shape[1] // count
-    lhs = jnp.concatenate([left[...], left_got[...]], axis=0)
-    res = dot(lhs, jnp.concatenate([dpre[...], dpre_got[...]], axis=0), TN).astype(BF)
+    ch = dpre_got.shape[1]
+    size = left_got.shape[1] // count
+    res = (earlier[...] + dot(left_got[...], dpre_got[...], TN)).astype(BF)
     for j in range(ch // LANES):
         part = res[:, j * LANES : (j + 1) * LANES].reshape(count, size, LANES)
         packed[:, j * size : (j + 1) * size, :] = part
@@ -445,10 +448,12 @@
     ext = rows + 2 * HALO
     frames_got = swap_core(frames)
 
+    edges = jnp.concatenate([frames[:HALO], frames[rows - HALO :]], axis=0)
+    edges = jnp.tanh(jnp.dot(edges, w_in, preferred_element_type=F32) + b_in).astype(BF)
+    before = shift_segment(edges[HALO:], 1)
+    after = shift_segment(edges[:HALO], -1)
     squash0 = jnp.tanh(jnp.dot(frames, w_in, preferred_element_type=F32) + b_in)
     own = squash0.astype(BF)
-    before = shift_segment(own[rows - HALO :], 1)
-    after = shift_segment(own[:HALO], -1)
     hid, sq, mine, other, means = call(
         functools.partial(forward_kernel, dims),
         [
@@ -520,24 +525,34 @@
     tile = group * in_size
     whole = pl.BlockSpec((rows, ch), lambda i, at: (0, 0))
     conv_spec = pl.BlockSpec((group, conv_wide, LANES), lambda i, at: (i, 0, 0))
+    left_spec = pl.BlockSpec((rows, tile), lambda i, at: (0, at[0] * steps + i))
+    res_spec = pl.BlockSpec((tile, ch), lambda i, at: (i, 0))
+    dpre_got, got = swap_core(dpre), swap_core(other)
+    earlier = pl.pallas_call(
+        product_kernel,
+        grid_spec=pltpu.PrefetchScalarGridSpec(
+            num_scalar_prefetch=1,
+            grid=(steps,),
+            in_specs=[left_spec, whole],
+            out_specs=res_spec,
+        ),
+        out_shape=sds((half_features, ch), F32),
+        compiler_params=small_params,
+        cost_estimate=pl.CostEstimate(
+            flops=2 * rows * half_features * ch, bytes_accessed=6 * 2**20, transcendentals=0
+        ),
+    )(info, frames, dpre)
     packed = pl.pallas_call(
         functools.partial(pack_kernel, nbias),
         grid_spec=pltpu.PrefetchScalarGridSpec(
             num_scalar_prefetch=1,
             grid=(steps,),
-            in_specs=[
-                pl.BlockSpec((rows, tile), lambda i, at: (0, at[0] * steps + i)),
-                pl.BlockSpec((rows, tile), lambda i, at: (0, at[0] * steps + i)),
-                whole,
-                whole,
-                conv_spec,
-                conv_spec,
-            ],
+            in_specs=[res_spec, left_spec, whole, conv_spec, conv_spec],
             out_specs=pl.BlockSpec((group, wide, LANES), lambda i, at: (i, 0, 0)),
         ),
         out_shape=sds((peers, wide, LANES), BF),
         compiler_params=small_params,
-    )(info, frames, frames_got, dpre, swap_core(dpre), mine, swap_core(other))
+    )(info, earlier, frames_got, dpre_got, mine, got)
     arrived = exchange(packed)
     block = 32
     full, bias = pl.pallas_call(

time: 220 us -> 220 us (level)
  waiting for transfers between devices: 9.65 us -> 6.74 us
    dot_general x0 -> x1, matrix products: none -> 3.04 us  [per_device(): jnp.dot(edges, w_in, preferred_element_type=F32) + b_in]
  transfers between devices with their start and end apart: 10 -> 10, of which waited for: 5 -> 4; matrix products, arithmetic and copies ran while one was open for 3% -> 4% of each run, Pallas kernels for 4% -> 5%
where the time goes in v5:
time: 220 us; the launch traced here: 219 us
  blocking collectives  152 us (69%)
  Pallas kernels  37.1 us (17%)
  starting transfers between devices  15 us (7%)
  waiting for transfers between devices  6.74 us (3%)
  matrix products  6.64 us (3%)
    all_to_all x4, blocking collectives, exchange(): return lax.all_to_all(value, PEERS, 0, 0, tiled=True)  152 us
    pallas_call x1, Pallas kernels, per_device(): pl.pallas_call(functools.partial(step_kernel, dims), out_shape=[sds((8, L...  12.6 us
    ppermute x8, starting transfers between devices, swap_core(): return lax.ppermute(value, 'c', [(0, 1), (1, 0)])  9.46 us
    pallas_call x2, Pallas kernels, unpack(): pl.pallas_call(functools.partial(unpack_kernel, (in_size, conv_size, nb),...  8.52 us
    pallas_call x3, Pallas kernels, call(): pl.pallas_call(kernel, out_shape=outs, in_specs=specs, out_specs=[pl.Bloc...  7.4 us
    ppermute x8, waiting for transfers between devices, swap_core(): return lax.ppermute(value, 'c', [(0, 1), (1, 0)])  6.74 us
    ppermute x2, starting transfers between devices, shift_segment(): lax.ppermute(value, 'tm', [(i, i + steps) for i in range(first, last)])  5.55 us
  transfers between devices with their start and end apart: 10, of which 4 were waited for; matrix products, arithmetic and copies ran while one was open for 4% of the time, Pallas kernels for 5%

profile of v5, /device:TPU:1, one launch (start us, length us, event | category | flops | bytes accessed | tf_op | source)
XLA Modules:
  0.0 219.5 jit_solution(2399449328434233770)
XLA Ops:
  0.6 0.0 copy-start.1
  0.6 0.0 copy-start.3
  0.7 1.5 collective-permute-start.4
  2.2 1.1 slice_bitcast_fusion.1
  3.2 3.0 %fusion.2 = bf16[64,512]{1,0:T(8,128)(2,1)S(1)} fusion(bf16[4096,512]{1,0:T(8,128)(2,1)} %param.6, bf16[32,4096]{1,0:T(8,128)(2,1)S(1)} %get-tuple-element.54, bf16[32,4096]{1,0:T(8,128)(2,1)S(1)} %get-tuple-element.53, f32[512]{0:T(512)} %param.7), kind=kOutput, calls=%fused_computation.4 | convolution fusion | flops 269549568 | bytes 4786176 | tf_op jit(solution)/shard_map/dot_general | solution.py:452
  6.3 1.3 collective-permute-start.1
  7.6 4.3 %collective-permute-start = (bf16[32,512]{1,0:T(8,128)(2,1)S(1)}, bf16[32,512]{1,0:T(8,128)(2,1)S(1)}, u32[]{:S(2)}, u32[]{:S(2)}) collective-permute-start(bf16[32,512]{1,0:T(8,128)(2,1)S(1)} %get-tuple-element.56), channel_id=1, source_target_pairs={{0,1},{1,2},{2,3},{3,4},{4,5},{5,6},{6,7},{7,8},{8,9},{9,10},{10,1... | collective-permute-start | bytes 98312 | tf_op jit(solution)/shard_map/ppermute | solution.py:46
  11.9 0.0 copy-done.1
  11.9 0.0 copy-done.3
  11.9 0.0 copy-start
  11.9 0.0 copy-start.2
  11.9 3.6 %fusion.9 = (bf16[256,512]{1,0:T(8,128)(2,1)S(1)}, f32[256,512]{1,0:T(8,128)S(1)}) fusion(f32[512]{0:T(512)S(1)} %copy-done.3, bf16[4096,512]{1,0:T(8,128)(2,1)} %param.6, bf16[1,256,4096]{2,1,0:T(8,128)(2,1)S(1)} %copy-done.1), kind=kOutput, calls=%fused_computation.14 | convolution fusion | flops 1074003968 | bytes 7079936 | tf_op jit(solution)/shard_map/dot_general | solution.py:455
  15.5 0.1 pad_add_fusion.info
  15.6 0.0 collective-permute-done.1.after
  15.6 0.0 collective-permute-done.before
  15.6 0.0 copy-done
  15.6 0.0 copy-done.2
  15.6 4.0 %shard_map.92 = (bf16[4,320,512]{2,1,0:T(8,128)(2,1)S(1)}, f32[3,320,512]{2,1,0:T(8,128)S(1)}, f32[64,48,128]{2,1,0:T(8,128)S(1)}, bf16[64,48,128]{2,1,0:T(8,128)(2,1)S(1)}, f32[8,512]{1,0:T(8,128)S(1)}) custom-call(s32[3]{0:T(128)S(1)} %pad_add_fusion.info, bf16[32,512]{1,0:T(8,128)(2,1)S(1)} %collective-permute-done.before, ...), custom_call_target="tpu_custom_call" | custom-call | tf_op jit(solution)/shard_map/pallas_call | solution.py:57
  19.6 0.5 collective-permute-start.2
  20.1 0.1 collective-permute-start.3
  20.2 1.8 collective-permute-done.3.sib
  22.1 0.0 collective-permute-done.2.got
  22.1 0.0 collective-permute-done.4.left_got
  22.1 2.0 shard_map.93
  24.0 30.0 %all_to_all.20.arrived = bf16[64,64,128]{2,1,0:T(8,128)(2,1)S(1)} all-to-all(bf16[64,64,128]{2,1,0:T(8,128)(2,1)S(1)} %shard_map.93), channel_id=1, replica_groups=mesh['x'=4,'c'=2,'tm'=16] {'x','tm'}, dimensions={0} | all-to-all | bytes 2097152 | tf_op jit(solution)/shard_map/all_to_all | solution.py:50
  54.0 1.5 shard_map.94
  55.5 19.0 %all_to_all.21.half_cov = bf16[64,48,128]{2,1,0:T(8,128)(2,1)S(1)} all-to-all(bf16[64,48,128]{2,1,0:T(8,128)(2,1)S(1)} %get-tuple-element.34), channel_id=1, replica_groups=mesh['x'=4,'c'=2,'tm'=16] {'x','tm'}, dimensions={0} | all-to-all | bytes 1572864 | tf_op jit(solution)/shard_map/all_to_all | solution.py:50
  74.5 3.1 %collective-permute-start.5 = (bf16[64,48,128]{2,1,0:T(8,128)(2,1)S(1)}, bf16[64,48,128]{2,1,0:T(8,128)(2,1)S(1)}, u32[]{:S(2)}, u32[]{:S(2)}) collective-permute-start(bf16[64,48,128]{2,1,0:T(8,128)(2,1)S(1)} %all_to_all.21.half_cov), channel_id=1, source_target_pairs={{0,16},{16,0},{1,17},{17,1},{2,18},{18,2},{3,19},{19,3},{4,20},{20... | collective-permute-start | bytes 2359304 | tf_op jit(solution)/shard_map/ppermute | solution.py:40
  77.6 1.9 collective-permute-done.5.other_cov
  79.6 12.6 %shard_map.95 = (f32[8,128]{1,0:T(8,128)S(1)}, bf16[64,112,128]{2,1,0:T(8,128)(2,1)S(1)}, bf16[64,112,128]{2,1,0:T(8,128)(2,1)S(1)}, bf16[256,512]{1,0:T(8,128)(2,1)S(1)}) custom-call(s32[3]{0:T(128)S(1)} %pad_add_fusion.info, bf16[64,48,128]{2,1,0:T(8,128)(2,1)S(1)} %all_to_all.21.half_cov, bf16[64,48,128]{2,1,0:T(8,128)(2,1)S(1)} %collective-permute-done.5.other_cov, ...), custom_call_target="tpu_custom_call" | custom-call | tf_op jit(solution)/shard_map/pallas_call | solution.py:502
  92.2 0.5 collective-permute-start.7
  92.6 0.1 collective-permute-start.6
  92.8 2.0 shard_map.96.earlier
  94.8 1.7 collective-permute-done.6.dpre_got
  96.4 0.0 collective-permute-done.7.got
  96.4 3.8 %shard_map.97 = bf16[64,240,128]{2,1,0:T(8,128)(2,1)S(1)} custom-call(s32[3]{0:T(128)S(1)} %pad_add_fusion.info, f32[2048,512]{1,0:T(8,128)S(1)} %shard_map.96.earlier, bf16[256,4096]{1,0:T(8,128)(2,1)} %collective-permute-done.4.left_got, bf16[256,512]{1,0:T(8,128)(2,1)S(1)} %collective-permute-done.6.dpre_got, ...), custom_call_target="tpu_custom_call" | custom-call | tf_op jit(solution)/shard_map/pallas_call | solution.py:545
  100.3 51.6 %all_to_all.22.arrived.tails = bf16[64,240,128]{2,1,0:T(8,128)(2,1)S(1)} all-to-all(bf16[64,240,128]{2,1,0:T(8,128)(2,1)S(1)} %shard_map.97), channel_id=1, replica_groups=mesh['x'=4,'c'=2,'tm'=16] {'x','tm'}, dimensions={0} | all-to-all | bytes 7864320 | tf_op jit(solution)/shard_map/all_to_all | solution.py:50
  151.9 2.7 %shard_map.98 = (bf16[64,224,128]{2,1,0:T(8,128)(2,1)S(1)}, f32[8,128]{1,0:T(8,128)S(1)}) custom-call(bf16[64,240,128]{2,1,0:T(8,128)(2,1)S(1)} %all_to_all.22.arrived.tails, bf16[64,240,128]{2,1,0:T(8,128)(2,1)S(1)} %all_to_all.22.arrived.tails), custom_call_target="tpu_custom_call" | custom-call | tf_op jit(solution)/shard_map/pallas_call | solution.py:558
  154.6 51.0 %all_to_all.23.chunks = bf16[64,224,128]{2,1,0:T(8,128)(2,1)S(1)} all-to-all(bf16[64,224,128]{2,1,0:T(8,128)(2,1)S(1)} %get-tuple-element.43), channel_id=1, replica_groups=mesh['x'=4,'c'=2,'tm'=16] {'x','tm'}, dimensions={0} | all-to-all | bytes 7340032 | tf_op jit(solution)/shard_map/all_to_all | solution.py:50
  205.5 3.6 %collective-permute-start.8 = (bf16[64,224,128]{2,1,0:T(8,128)(2,1)S(1)}, bf16[64,224,128]{2,1,0:T(8,128)(2,1)S(1)}, u32[]{:S(2)}, u32[]{:S(2)}) collective-permute-start(bf16[64,224,128]{2,1,0:T(8,128)(2,1)S(1)} %all_to_all.23.chunks), channel_id=1, source_target_pairs={{0,16},{16,0},{1,17},{17,1},{2,18},{18,2},{3,19},{19,3},{4,20},{20... | collective-permute-start | bytes 11010056 | tf_op jit(solution)/shard_map/ppermute | solution.py:40
  209.1 0.0 collective-permute-start.9
  209.1 0.5 slice.27
  209.7 4.2 %shard_map.99 = (f32[2,2048,512]{2,1,0:T(8,128)}, f32[3,1024,512]{2,1,0:T(8,128)}) custom-call(s32[1]{0:T(128)} %bitcast.info, bf16[64,224,128]{2,1,0:T(8,128)(2,1)S(1)} %all_to_all.23.chunks), custom_call_target="tpu_custom_call" | custom-call | bytes 12582912 | tf_op jit(solution)/shard_map/pallas_call | solution.py:579
  213.9 1.3 collective-permute-done.9.refs_1_
  215.2 0.0 collective-permute-done.8.chunks
  215.2 4.3 %shard_map.100 = (f32[2,2048,512]{2,1,0:T(8,128)}, f32[3,1024,512]{2,1,0:T(8,128)}, f32[512]{0:T(512)}, f32[3,512]{1,0:T(4,128)}) custom-call(s32[1]{0:T(128)S(6)} %sub.3.info, bf16[64,224,128]{2,1,0:T(8,128)(2,1)S(1)} %collective-permute-done.8.chunks, f32[8,128]{1,0:T(8,128)S(1)} %get-tuple-element.44.refs_0_, ...), custom_call_target="tpu_custom_call", output_to_operand_aliasing={{0}: (4, {}), {1}: (5, {})} | custom-call | bytes 12582912 | tf_op jit(solution)/shard_map/pallas_call | solution.py:579
  (1 shorter events, 0.0 us)
Async XLA Ops:
  0.6 11.2 %copy-start.1 = (bf16[1,256,4096]{2,1,0:T(8,128)(2,1)S(1)}, bf16[1,256,4096]{2,1,0:T(8,128)(2,1)}, u32[]{:S(2)}) copy-start(bf16[1,256,4096]{2,1,0:T(8,128)(2,1)} %param.5) | copy-start | bytes 6291460
  0.6 11.2 %copy-start.3 = (f32[512]{0:T(512)S(1)}, f32[512]{0:T(512)}, u32[]{:S(2)}) copy-start(f32[512]{0:T(512)} %param.7) | copy-start | bytes 6148
  0.7 21.4 %collective-permute-start.4 = (bf16[256,4096]{1,0:T(8,128)(2,1)}, bf16[256,4096]{1,0:T(8,128)(2,1)}, u32[]{:S(2)}, u32[]{:S(2)}) collective-permute-start(bf16[256,4096]{1,0:T(8,128)(2,1)} %bitcast.16), channel_id=1, source_target_pairs={{0,16},{16,0},{1,17},{17,1},{2,18},{18,2},{3,19},{19,3},{4,20},{20... | collective-permute-start | bytes 6291464 | tf_op jit(solution)/shard_map/ppermute | solution.py:40
  6.3 9.3 %collective-permute-start.1 = (bf16[32,512]{1,0:T(8,128)(2,1)S(1)}, bf16[32,512]{1,0:T(8,128)(2,1)S(1)}, u32[]{:S(2)}, u32[]{:S(2)}) collective-permute-start(bf16[32,512]{1,0:T(8,128)(2,1)S(1)} %get-tuple-element.55), channel_id=1, source_target_pairs={{1,0},{2,1},{3,2},{4,3},{5,4},{6,5},{7,6},{8,7},{9,8},{10,9},{11,1... | collective-permute-start | bytes 98312 | tf_op jit(solution)/shard_map/ppermute | solution.py:46
  7.6 8.0 %collective-permute-start = (bf16[32,512]{1,0:T(8,128)(2,1)S(1)}, bf16[32,512]{1,0:T(8,128)(2,1)S(1)}, u32[]{:S(2)}, u32[]{:S(2)}) collective-permute-start(bf16[32,512]{1,0:T(8,128)(2,1)S(1)} %get-tuple-element.56), channel_id=1, source_target_pairs={{0,1},{1,2},{2,3},{3,4},{4,5},{5,6},{6,7},{7,8},{8,9},{9,10},{10,1... | collective-permute-start | bytes 98312 | tf_op jit(solution)/shard_map/ppermute | solution.py:46
  11.9 3.7 %copy-start = (bf16[3,1024,512]{2,1,0:T(8,128)(2,1)S(1)}, bf16[3,1024,512]{2,1,0:T(8,128)(2,1)}, u32[]{:S(2)}) copy-start(bf16[3,1024,512]{2,1,0:T(8,128)(2,1)} %w_hbm.1) | copy-start | bytes 9437188
  11.9 3.7 %copy-start.2 = (f32[3,512]{1,0:T(4,128)S(1)}, f32[3,512]{1,0:T(4,128)}, u32[]{:S(2)}) copy-start(f32[3,512]{1,0:T(4,128)} %b.1) | copy-start | bytes 18436
  19.6 2.5 %collective-permute-start.2 = (bf16[64,48,128]{2,1,0:T(8,128)(2,1)S(1)}, bf16[64,48,128]{2,1,0:T(8,128)(2,1)S(1)}, u32[]{:S(2)}, u32[]{:S(2)}) collective-permute-start(bf16[64,48,128]{2,1,0:T(8,128)(2,1)S(1)} %get-tuple-element.30), channel_id=1, source_target_pairs={{0,16},{16,0},{1,17},{17,1},{2,18},{18,2},{3,19},{19,3},{4,20},{20... | collective-permute-start | bytes 2359304 | tf_op jit(solution)/shard_map/ppermute | solution.py:40
  20.1 1.9 collective-permute-start.3
  74.5 5.1 %collective-permute-start.5 = (bf16[64,48,128]{2,1,0:T(8,128)(2,1)S(1)}, bf16[64,48,128]{2,1,0:T(8,128)(2,1)S(1)}, u32[]{:S(2)}, u32[]{:S(2)}) collective-permute-start(bf16[64,48,128]{2,1,0:T(8,128)(2,1)S(1)} %all_to_all.21.half_cov), channel_id=1, source_target_pairs={{0,16},{16,0},{1,17},{17,1},{2,18},{18,2},{3,19},{19,3},{4,20},{20... | collective-permute-start | bytes 2359304 | tf_op jit(solution)/shard_map/ppermute | solution.py:40
  92.2 4.2 %collective-permute-start.7 = (bf16[64,112,128]{2,1,0:T(8,128)(2,1)S(1)}, bf16[64,112,128]{2,1,0:T(8,128)(2,1)S(1)}, u32[]{:S(2)}, u32[]{:S(2)}) collective-permute-start(bf16[64,112,128]{2,1,0:T(8,128)(2,1)S(1)} %get-tuple-element.42), channel_id=1, source_target_pairs={{0,16},{16,0},{1,17},{17,1},{2,18},{18,2},{3,19},{19,3},{4,20},{20... | collective-permute-start | bytes 5505032 | tf_op jit(solution)/shard_map/ppermute | solution.py:40
  92.6 3.8 %collective-permute-start.6 = (bf16[256,512]{1,0:T(8,128)(2,1)S(1)}, bf16[256,512]{1,0:T(8,128)(2,1)S(1)}, u32[]{:S(2)}, u32[]{:S(2)}) collective-permute-start(bf16[256,512]{1,0:T(8,128)(2,1)S(1)} %get-tuple-element.39.dpre), channel_id=1, source_target_pairs={{0,16},{16,0},{1,17},{17,1},{2,18},{18,2},{3,19},{19,3},{4,20},{20... | collective-permute-start | bytes 786440 | tf_op jit(solution)/shard_map/ppermute | solution.py:40
  205.5 9.6 %collective-permute-start.8 = (bf16[64,224,128]{2,1,0:T(8,128)(2,1)S(1)}, bf16[64,224,128]{2,1,0:T(8,128)(2,1)S(1)}, u32[]{:S(2)}, u32[]{:S(2)}) collective-permute-start(bf16[64,224,128]{2,1,0:T(8,128)(2,1)S(1)} %all_to_all.23.chunks), channel_id=1, source_target_pairs={{0,16},{16,0},{1,17},{17,1},{2,18},{18,2},{3,19},{19,3},{4,20},{20... | collective-permute-start | bytes 11010056 | tf_op jit(solution)/shard_map/ppermute | solution.py:40
  209.1 6.0 %collective-permute-start.9 = (f32[8,128]{1,0:T(8,128)S(1)}, f32[8,128]{1,0:T(8,128)S(1)}, u32[]{:S(2)}, u32[]{:S(2)}) collective-permute-start(f32[8,128]{1,0:T(8,128)S(1)} %get-tuple-element.44.refs_0_), channel_id=1, source_target_pairs={{0,16},{16,0},{1,17},{17,1},{2,18},{18,2},{3,19},{19,3},{4,20},{20... | collective-permute-start | bytes 12296 | tf_op jit(solution)/shard_map/ppermute | solution.py:40

commit v6 on v5

--- a/solution.py
+++ b/solution.py
@@ -361,74 +361,77 @@
     res[...] = dot(left[...], dpre[...], TN)
 
 
-def pack_kernel(nbias, info, earlier, left_got, dpre_got, mine, got, packed):
+def pack_kernel(info, earlier, left_got, dpre_got, packed):
     count = packed.shape[0]
-    ch = dpre_got.shape[1]
     size = left_got.shape[1] // count
     res = (earlier[...] + dot(left_got[...], dpre_got[...], TN)).astype(BF)
-    for j in range(ch // LANES):
+    for j in range(res.shape[1] // LANES):
         part = res[:, j * LANES : (j + 1) * LANES].reshape(count, size, LANES)
         packed[:, j * size : (j + 1) * size, :] = part
-    at = size * (ch // LANES)
+
+
+def add_kernel(nbias, mine, got, packed):
     body = mine.shape[1] - 2 * nbias
     value = mine[...].astype(F32) + got[...].astype(F32)
-    packed[:, at : at + body, :] = value[:, :body].astype(BF)
+    packed[:, :body, :] = value[:, :body].astype(BF)
     bias = value[0, body : body + nbias] + value[0, body + nbias :]
     hi = bias.astype(BF).astype(F32)
     tail = jnp.concatenate([hi, bias - hi], axis=0).astype(BF)
-    packed[:, at + body :, :] = jnp.broadcast_to(tail[None], (count,) + tail.shape)
-
-
-def sum_kernel(arrived, tails, full, bias):
-    peers = arrived.shape[0]
-
+    packed[:, body:, :] = jnp.broadcast_to(tail[None], (mine.shape[0],) + tail.shape)
+
+
+def total_of(arrived):
     def add(p, acc):
         return acc + arrived[p].astype(F32)
 
-    value = lax.fori_loop(0, peers, add, jnp.zeros(arrived.shape[1:], F32), unroll=4)
-    full[...] = jnp.broadcast_to(value.astype(BF)[None], full.shape)
+    return lax.fori_loop(0, arrived.shape[0], add, jnp.zeros(arrived.shape[1:], F32), unroll=4)
+
+
+def sum_conv_kernel(nbias, arrived, chunk, bias):
+    value = total_of(arrived)
+    body = chunk.shape[0]
+    chunk[...] = value[:body].astype(BF)
+    bias[...] = value[body : body + nbias] + value[body + nbias :]
+
+
+def sum_in_kernel(arrived, full):
+    full[...] = jnp.broadcast_to(total_of(arrived).astype(BF)[None], full.shape)
+
+
+def unpack_in_kernel(info, chunks, *refs):
+    w_in = refs[-1]
+    count, wide = chunks.shape[:2]
+    nb = w_in.shape[2] // LANES
+    size = wide // nb
+    for j in range(nb):
+        part = chunks[:, j * size : (j + 1) * size, :].astype(F32)
+        w_in[0, :, j * LANES : (j + 1) * LANES] = part.reshape(count * size, LANES)
+
+
+def unpack_conv_kernel(info, low, high, bias, bias_got, w_conv, b_in, b_conv):
+    count = low.shape[0]
+    nh = w_conv.shape[2] // LANES // 2
+    size = low.shape[1] // (NL * nh)
+    for side, chunks in enumerate((low, high)):
+        for layer in range(NL):
+            for j in range(nh):
+                at = (layer * nh + j) * size
+                col = (side * nh + j) * LANES
+                part = chunks[:, at : at + size, :].astype(F32)
+                w_conv[layer, :, col : col + LANES] = part.reshape(count * size, LANES)
 
     @pl.when(pl.program_id(0) == 0)
     def _():
-        def add_tail(p, acc):
-            return acc + tails[p].astype(F32)
-
-        t = lax.fori_loop(0, peers, add_tail, jnp.zeros(tails.shape[1:], F32))
-        n = t.shape[0] // 2
-        bias[...] = t[:n] + t[n:]
-
-
-def unpack_kernel(sizes, nbiases, info, chunks, *refs):
-    in_size, conv_size, nb = sizes
-    if nbiases:
-        bias, bias_got = refs[:2]
-        w_in, w_conv, b_in, b_conv = refs[-4:]
-    else:
-        w_in, w_conv = refs[-2:]
-    count = chunks.shape[0]
-    for j in range(nb):
-        part = chunks[:, j * in_size : (j + 1) * in_size, :].astype(F32)
-        w_in[0, :, j * LANES : (j + 1) * LANES] = part.reshape(count * in_size, LANES)
-    for layer in range(NL):
-        for j in range(nb // 2):
-            at = nb * in_size + (layer * (nb // 2) + j) * conv_size
-            part = chunks[:, at : at + conv_size, :].astype(F32)
-            w_conv[layer, :, j * LANES : (j + 1) * LANES] = part.reshape(count * conv_size, LANES)
-    if nbiases:
-
-        @pl.when(pl.program_id(0) == 0)
-        def _():
-            swapped = info[0] == 0
-            n = NL + 1
-            rows = []
-            for side in range(2):
-                keep = bias_got[...] if side == 0 else bias[...]
-                swap = bias[...] if side == 0 else bias_got[...]
-                value = jnp.where(swapped, keep, swap)
-                rows += [value[j * n : (j + 1) * n] for j in range(nb // 2)]
-            full = jnp.concatenate(rows, axis=1)
-            b_in[...] = full[0]
-            b_conv[...] = full[1:]
+        first = info[0] == 0
+        n = NL + 1
+        parts = []
+        for side in range(2):
+            mine_side = first if side == 0 else jnp.logical_not(first)
+            value = jnp.where(mine_side, bias[...], bias_got[...])
+            parts += [value[j * n : (j + 1) * n] for j in range(nh)]
+        full = jnp.concatenate(parts, axis=1)
+        b_in[...] = full[0]
+        b_conv[...] = full[1:]
 
 
 def per_device(frames, w_in, b_in, w_conv, b_conv):
@@ -448,12 +451,10 @@
     ext = rows + 2 * HALO
     frames_got = swap_core(frames)
 
-    edges = jnp.concatenate([frames[:HALO], frames[rows - HALO :]], axis=0)
-    edges = jnp.tanh(jnp.dot(edges, w_in, preferred_element_type=F32) + b_in).astype(BF)
-    before = shift_segment(edges[HALO:], 1)
-    after = shift_segment(edges[:HALO], -1)
     squash0 = jnp.tanh(jnp.dot(frames, w_in, preferred_element_type=F32) + b_in)
     own = squash0.astype(BF)
+    before = shift_segment(own[rows - HALO :], 1)
+    after = shift_segment(own[:HALO], -1)
     hid, sq, mine, other, means = call(
         functools.partial(forward_kernel, dims),
         [
@@ -492,8 +493,6 @@
     conv_size = 2 * ch // peers
     nbias = (NL + 1) * nh
     conv_wide = NL * nh * conv_size + 2 * nbias
-    body = nb * in_size + NL * nh * conv_size
-    wide = body + 2 * nbias
     vmem = pl.BlockSpec(memory_space=pltpu.VMEM)
     smem = pl.BlockSpec(memory_space=pltpu.SMEM)
     hbm = pl.BlockSpec(memory_space=pl.ANY)
@@ -542,64 +541,92 @@
             flops=2 * rows * half_features * ch, bytes_accessed=6 * 2**20, transcendentals=0
         ),
     )(info, frames, dpre)
+    conv_packed = pl.pallas_call(
+        functools.partial(add_kernel, nbias),
+        grid=(steps,),
+        in_specs=[pl.BlockSpec((group, conv_wide, LANES), lambda i: (i, 0, 0))] * 2,
+        out_specs=pl.BlockSpec((group, conv_wide, LANES), lambda i: (i, 0, 0)),
+        out_shape=sds((peers, conv_wide, LANES), BF),
+        compiler_params=small_params,
+    )(mine, got)
+    in_wide = nb * in_size
     packed = pl.pallas_call(
-        functools.partial(pack_kernel, nbias),
+        pack_kernel,
         grid_spec=pltpu.PrefetchScalarGridSpec(
             num_scalar_prefetch=1,
             grid=(steps,),
-            in_specs=[res_spec, left_spec, whole, conv_spec, conv_spec],
-            out_specs=pl.BlockSpec((group, wide, LANES), lambda i, at: (i, 0, 0)),
+            in_specs=[res_spec, left_spec, whole],
+            out_specs=pl.BlockSpec((group, in_wide, LANES), lambda i, at: (i, 0, 0)),
         ),
-        out_shape=sds((peers, wide, LANES), BF),
+        out_shape=sds((peers, in_wide, LANES), BF),
         compiler_params=small_params,
-    )(info, earlier, frames_got, dpre_got, mine, got)
-    arrived = exchange(packed)
+    )(info, earlier, frames_got, dpre_got)
+    conv_body = conv_wide - 2 * nbias
+    chunk, bias = pl.pallas_call(
+        functools.partial(sum_conv_kernel, nbias),
+        in_specs=[vmem],
+        out_specs=[vmem, vmem],
+        out_shape=[sds((conv_body, LANES), BF), sds((nbias, LANES), F32)],
+        compiler_params=small_params,
+    )(exchange(conv_packed))
+    packed, chunk, bias = lax.optimization_barrier((packed, chunk, bias))
+    conv_all = lax.all_gather(chunk[None], ("c",) + PEERS, axis=0, tiled=True)
+    bias_got = swap_core(bias)
     block = 32
-    full, bias = pl.pallas_call(
-        sum_kernel,
-        grid=(body // block,),
-        out_shape=[sds((peers, body, LANES), BF), sds((nbias, LANES), F32)],
-        in_specs=[
-            pl.BlockSpec((peers, block, LANES), lambda i: (0, i, 0)),
-            pl.BlockSpec((peers, 2 * nbias, LANES), lambda i: (0, body // (2 * nbias), 0)),
-        ],
-        out_specs=[
-            pl.BlockSpec((peers, block, LANES), lambda i: (0, i, 0)),
-            pl.BlockSpec((nbias, LANES), lambda i: (0, 0)),
-        ],
+    full = pl.pallas_call(
+        sum_in_kernel,
+        grid=(in_wide // block,),
+        out_shape=sds((peers, in_wide, LANES), BF),
+        in_specs=[pl.BlockSpec((peers, block, LANES), lambda i: (0, i, 0))],
+        out_specs=pl.BlockSpec((peers, block, LANES), lambda i: (0, i, 0)),
         compiler_params=small_params,
-    )(arrived, arrived)
-    bias_got = swap_core(bias)
+    )(exchange(packed))
     full = exchange(full)
     steps = 8
     group = peers // steps
 
-    def unpack(chunks, at, biases, earlier):
-        spare = [sds((ch,), F32), sds((NL, ch), F32)] if biases else []
+    def unpack(chunks, at, earlier):
         return pl.pallas_call(
-            functools.partial(unpack_kernel, (in_size, conv_size, nb), len(biases)),
+            unpack_in_kernel,
             grid_spec=pltpu.PrefetchScalarGridSpec(
                 num_scalar_prefetch=1,
                 grid=(steps,),
-                in_specs=[pl.BlockSpec((group, body, LANES), lambda i, at: (i, 0, 0))]
-                + [pl.BlockSpec(b.shape, lambda i, at: (0, 0)) for b in biases]
+                in_specs=[pl.BlockSpec((group, in_wide, LANES), lambda i, at: (i, 0, 0))]
                 + [hbm] * len(earlier),
-                out_specs=[
-                    pl.BlockSpec((1, group * in_size, ch), lambda i, at: (at[0], i, 0)),
-                    pl.BlockSpec((NL, group * conv_size, ch // 2), lambda i, at: (0, i, at[0])),
-                ]
-                + [pl.BlockSpec(b.shape, lambda i, at, n=len(b.shape): (0,) * n) for b in spare],
+                out_specs=pl.BlockSpec((1, group * in_size, ch), lambda i, at: (at[0], i, 0)),
             ),
-            out_shape=[sds((2, half_features, ch), F32), sds((NL, 2 * ch, ch), F32)] + spare,
-            input_output_aliases={2 + len(biases) + n: n for n in range(len(earlier))},
+            out_shape=sds((2, half_features, ch), F32),
+            input_output_aliases={2 + n: 0 for n in range(len(earlier))},
             compiler_params=small_params,
-            cost_estimate=pl.CostEstimate(flops=0, bytes_accessed=12 * 2**20, transcendentals=0),
-        )(at, chunks, *biases, *earlier)
+            cost_estimate=pl.CostEstimate(flops=0, bytes_accessed=6 * 2**20, transcendentals=0),
+        )(at, chunks, *earlier)
 
     got = swap_core(full)
-    partial = unpack(full, info[:1], [], [])
-    got, bias_got = lax.optimization_barrier((got, bias_got))
-    g_in, g_conv, g_b_in, g_b_conv = unpack(got, 1 - info[:1], [bias, bias_got], partial)
+    partial = unpack(full, info[:1], [])
+    small = pl.BlockSpec((nbias, LANES), lambda i, at: (0, 0))
+    conv_block = (group, conv_body, LANES)
+    g_conv, g_b_in, g_b_conv = pl.pallas_call(
+        unpack_conv_kernel,
+        grid_spec=pltpu.PrefetchScalarGridSpec(
+            num_scalar_prefetch=1,
+            grid=(steps,),
+            in_specs=[
+                pl.BlockSpec(conv_block, lambda i, at: (i, 0, 0)),
+                pl.BlockSpec(conv_block, lambda i, at: (steps + i, 0, 0)),
+                small,
+                small,
+            ],
+            out_specs=[
+                pl.BlockSpec((NL, group * conv_size, ch), lambda i, at: (0, i, 0)),
+                pl.BlockSpec((ch,), lambda i, at: (0,)),
+                pl.BlockSpec((NL, ch), lambda i, at: (0, 0)),
+            ],
+        ),
+        out_shape=[sds((NL, 2 * ch, ch), F32), sds((ch,), F32), sds((NL, ch), F32)],
+        compiler_params=small_params,
+        cost_estimate=pl.CostEstimate(flops=0, bytes_accessed=10 * 2**20, transcendentals=0),
+    )(info, conv_all, conv_all, bias, bias_got)
+    g_in = unpack(got, 1 - info[:1], [partial])
     return score[0, 0], g_in.reshape(features, ch), g_b_in, g_conv, g_b_conv
 
 

time: 220 us -> 249 us (1.13)
  waiting for transfers between devices: 6.74 us -> 46.5 us
  blocking collectives: 152 us -> 116 us
  between operations: 0.81 us -> 14.2 us
  starting transfers between devices: 15 us -> 21.8 us
  Pallas kernels: 37.1 us -> 42.6 us
    all_to_all x4, blocking collectives: 152 us -> 116 us  [exchange(): return lax.all_to_all(value, PEERS, 0, 0, tiled=True)]
    all_to_all x0 -> x1, waiting for transfers between devices: none -> 18.7 us  [exchange(): return lax.all_to_all(value, PEERS, 0, 0, tiled=True)]
    all_gather x0 -> x1, waiting for transfers between devices: none -> 17.1 us  [per_device(): conv_all = lax.all_gather(chunk[None], ('c',) + PEERS, axis=0, tiled=True)]
    all_to_all x0 -> x1, starting transfers between devices: none -> 5.66 us  [exchange(): return lax.all_to_all(value, PEERS, 0, 0, tiled=True)]
    pallas_call x4 -> x7, Pallas kernels: 15 us -> 20.7 us  [the longest x2 7.16 us: unpack(): pl.pallas_call(unpack_in_kernel, grid_spec=pltpu.PrefetchScalarGridSpec(n...]
    ppermute x2, waiting for transfers between devices: 0.01 us -> 3.46 us  [shift_segment(): lax.ppermute(value, 'tm', [(i, i + steps) for i in range(first, last)])]
    dot_general x1 -> x0, matrix products: 3.04 us -> none  [per_device(): jnp.dot(edges, w_in, preferred_element_type=F32) + b_in]
  transfers between devices with their start and end apart: 10 -> 12, of which waited for: 4 -> 6; matrix products, arithmetic and copies ran while one was open for 4% -> 2% of each run, Pallas kernels for 5% -> 7%
where the time goes in v6:
time: 249 us
  blocking collectives  116 us (47%)
  waiting for transfers between devices  46.5 us (19%)
  Pallas kernels  42.6 us (17%)
  starting transfers between devices  21.8 us (9%)
  between operations  14.2 us (6%)
  matrix products  4.92 us (2%)
    all_to_all x4, blocking collectives, exchange(): return lax.all_to_all(value, PEERS, 0, 0, tiled=True)  116 us
    all_to_all x1, waiting for transfers between devices, exchange(): return lax.all_to_all(value, PEERS, 0, 0, tiled=True)  18.7 us
    all_gather x1, waiting for transfers between devices, per_device(): conv_all = lax.all_gather(chunk[None], ('c',) + PEERS, axis=0, tiled=True)  17.1 us
    pallas_call x1, Pallas kernels, per_device(): pl.pallas_call(functools.partial(step_kernel, dims), out_shape=[sds((8, L...  12.6 us
    ppermute x8, starting transfers between devices, swap_core(): return lax.ppermute(value, 'c', [(0, 1), (1, 0)])  11 us
    pallas_call x3, Pallas kernels, call(): pl.pallas_call(kernel, out_shape=outs, in_specs=specs, out_specs=[pl.Bloc...  7.36 us
    ppermute x8, waiting for transfers between devices, swap_core(): return lax.ppermute(value, 'c', [(0, 1), (1, 0)])  7.18 us
    pallas_call x2, Pallas kernels, unpack(): pl.pallas_call(unpack_in_kernel, grid_spec=pltpu.PrefetchScalarGridSpec(n...  7.16 us
  transfers between devices with their start and end apart: 12, of which 6 were waited for; matrix products, arithmetic and copies ran while one was open for 2% of the time, Pallas kernels for 7%

profile of v6, /device:TPU:1, one launch (start us, length us, event | category | flops | bytes accessed | tf_op | source)
XLA Modules:
  0.0 248.5 jit_solution(10876412950474528217)
XLA Ops:
  7.2 1.5 collective-permute-start.4
  8.7 4.9 %fusion.3 = (bf16[256,512]{1,0:T(8,128)(2,1)S(1)}, f32[256,512]{1,0:T(8,128)}) fusion(f32[512]{0:T(512)} %param.7, bf16[4096,512]{1,0:T(8,128)(2,1)} %param.6, bf16[1,256,4096]{2,1,0:T(8,128)(2,1)} %param.5), kind=kOutput, calls=%fused_computation.5 | convolution fusion | flops 1074003968 | bytes 7079936 | tf_op jit(solution)/shard_map/dot_general | solution.py:454
  13.6 3.8 %collective-permute-start = (bf16[32,512]{1,0:T(8,128)(2,1)S(1)}, bf16[32,512]{1,0:T(8,128)(2,1)S(1)}, u32[]{:S(2)}, u32[]{:S(2)}) collective-permute-start(bf16[32,512]{1,0:T(8,128)(2,1)S(1)} %get-tuple-element.50), channel_id=1, source_target_pairs={{0,1},{1,2},{2,3},{3,4},{4,5},{5,6},{6,7},{7,8},{8,9},{9,10},{10,1... | collective-permute-start | bytes 98312 | tf_op jit(solution)/shard_map/ppermute | solution.py:46
  17.4 1.3 collective-permute-start.1
  18.7 0.1 pad_add_fusion.info
  18.8 0.0 collective-permute-done.before
  18.8 3.5 %collective-permute-done.1.after = bf16[32,512]{1,0:T(8,128)(2,1)S(1)} collective-permute-done((bf16[32,512]{1,0:T(8,128)(2,1)S(1)}, bf16[32,512]{1,0:T(8,128)(2,1)S(1)}, u32[]{:S(2)}, u32[]{:S(2)}) %collective-permute-start.1) | collective-permute-done | bytes 32800 | tf_op jit(solution)/shard_map/ppermute | solution.py:46
  22.3 0.0 copy-done
  22.3 3.9 %shard_map.92 = (bf16[4,320,512]{2,1,0:T(8,128)(2,1)S(1)}, f32[3,320,512]{2,1,0:T(8,128)S(1)}, f32[64,48,128]{2,1,0:T(8,128)S(1)}, bf16[64,48,128]{2,1,0:T(8,128)(2,1)S(1)}, f32[8,512]{1,0:T(8,128)S(1)}) custom-call(s32[3]{0:T(128)S(1)} %pad_add_fusion.info, bf16[32,512]{1,0:T(8,128)(2,1)S(1)} %collective-permute-done.before, ...), custom_call_target="tpu_custom_call" | custom-call | tf_op jit(solution)/shard_map/pallas_call | solution.py:57
  26.2 1.3 collective-permute-start.2
  27.5 0.1 collective-permute-start.3
  27.6 1.8 collective-permute-done.3.sib
  29.4 0.0 collective-permute-done.2.got
  29.4 0.0 collective-permute-done.4.left_got
  29.4 2.0 shard_map.93
  31.4 0.0 copy-start.3
  31.4 28.1 %all_to_all.25.arrived = bf16[64,64,128]{2,1,0:T(8,128)(2,1)S(1)} all-to-all(bf16[64,64,128]{2,1,0:T(8,128)(2,1)S(1)} %shard_map.93), channel_id=1, replica_groups=mesh['x'=4,'c'=2,'tm'=16] {'x','tm'}, dimensions={0} | all-to-all | bytes 2097152 | tf_op jit(solution)/shard_map/all_to_all | solution.py:50
  59.5 1.5 shard_map.94
  61.0 19.0 %all_to_all.26.half_cov = bf16[64,48,128]{2,1,0:T(8,128)(2,1)S(1)} all-to-all(bf16[64,48,128]{2,1,0:T(8,128)(2,1)S(1)} %get-tuple-element.32), channel_id=1, replica_groups=mesh['x'=4,'c'=2,'tm'=16] {'x','tm'}, dimensions={0} | all-to-all | bytes 1572864 | tf_op jit(solution)/shard_map/all_to_all | solution.py:50
  80.0 3.1 %collective-permute-start.5 = (bf16[64,48,128]{2,1,0:T(8,128)(2,1)S(1)}, bf16[64,48,128]{2,1,0:T(8,128)(2,1)S(1)}, u32[]{:S(2)}, u32[]{:S(2)}) collective-permute-start(bf16[64,48,128]{2,1,0:T(8,128)(2,1)S(1)} %all_to_all.26.half_cov), channel_id=1, source_target_pairs={{0,16},{16,0},{1,17},{17,1},{2,18},{18,2},{3,19},{19,3},{4,20},{20... | collective-permute-start | bytes 2359304 | tf_op jit(solution)/shard_map/ppermute | solution.py:40
  83.2 1.9 collective-permute-done.5.other_cov
  85.1 12.6 %shard_map.95 = (f32[8,128]{1,0:T(8,128)S(1)}, bf16[64,112,128]{2,1,0:T(8,128)(2,1)S(1)}, bf16[64,112,128]{2,1,0:T(8,128)(2,1)S(1)}, bf16[256,512]{1,0:T(8,128)(2,1)S(1)}) custom-call(s32[3]{0:T(128)S(1)} %pad_add_fusion.info, bf16[64,48,128]{2,1,0:T(8,128)(2,1)S(1)} %all_to_all.26.half_cov, bf16[64,48,128]{2,1,0:T(8,128)(2,1)S(1)} %collective-permute-done.5.other_cov, ...), custom_call_target="tpu_custom_call" | custom-call | tf_op jit(solution)/shard_map/pallas_call | solution.py:501
  97.7 0.5 collective-permute-start.7
  98.2 3.4 %collective-permute-done.7.got = bf16[64,112,128]{2,1,0:T(8,128)(2,1)S(1)} collective-permute-done((bf16[64,112,128]{2,1,0:T(8,128)(2,1)S(1)}, bf16[64,112,128]{2,1,0:T(8,128)(2,1)S(1)}, u32[]{:S(2)}, u32[]{:S(2)}) %collective-permute-start.7) | collective-permute-done | bytes 1835040 | tf_op jit(solution)/shard_map/ppermute | solution.py:40
  101.6 1.9 shard_map.98
  103.5 5.7 %all-to-all-start.2 = ((bf16[64,112,128]{2,1,0:T(8,128)(2,1)}), bf16[64,112,128]{2,1,0:T(8,128)(2,1)}, u32[]{:S(2)}, u32[]{:S(2)}) async-start(bf16[64,112,128]{2,1,0:T(8,128)(2,1)} %shard_map.98), calls=%async_computation.2 | async-start | bytes 3670016 | tf_op jit(solution)/shard_map/all_to_all | solution.py:50
  109.2 0.0 all-gather.3.cloned.1.call-start
  109.2 0.7 collective-permute-start.6
  109.9 0.0 copy-done.2
  109.9 2.0 shard_map.96.earlier
  111.9 0.0 collective-permute-done.6.dpre_got
  111.9 3.5 %shard_map.97 = bf16[64,128,128]{2,1,0:T(8,128)(2,1)S(1)} custom-call(s32[3]{0:T(128)S(1)} %pad_add_fusion.info, f32[2048,512]{1,0:T(8,128)S(1)} %shard_map.96.earlier, bf16[256,4096]{1,0:T(8,128)(2,1)} %collective-permute-done.4.left_got, bf16[256,512]{1,0:T(8,128)(2,1)S(1)} %collective-permute-done.6.dpre_got), custom_call_target="tpu_custom_call" | custom-call | tf_op jit(solution)/shard_map/pallas_call | solution.py:553
  115.4 18.7 %all-to-all-done.2.arrived = bf16[64,112,128]{2,1,0:T(8,128)(2,1)} async-done(((bf16[64,112,128]{2,1,0:T(8,128)(2,1)}), bf16[64,112,128]{2,1,0:T(8,128)(2,1)}, u32[]{:S(2)}, u32[]{:S(2)}) %all-to-all-start.2) | async-done | bytes 1835040 | tf_op jit(solution)/shard_map/all_to_all | solution.py:50
  134.2 2.4 shard_map.99
  136.6 0.0 all-gather.3.cloned.1.call-update
  136.6 33.4 %all_to_all.27.arrived = bf16[64,128,128]{2,1,0:T(8,128)(2,1)S(1)} all-to-all(bf16[64,128,128]{2,1,0:T(8,128)(2,1)S(1)} %shard_map.97), channel_id=1, replica_groups=mesh['x'=4,'c'=2,'tm'=16] {'x','tm'}, dimensions={0} | all-to-all | bytes 4194304 | tf_op jit(solution)/shard_map/all_to_all | solution.py:50
  170.0 1.0 shard_map.100
  171.1 35.4 %all_to_all.28.chunks = bf16[64,128,128]{2,1,0:T(8,128)(2,1)S(1)} all-to-all(bf16[64,128,128]{2,1,0:T(8,128)(2,1)S(1)} %shard_map.100), channel_id=1, replica_groups=mesh['x'=4,'c'=2,'tm'=16] {'x','tm'}, dimensions={0} | all-to-all | bytes 4194304 | tf_op jit(solution)/shard_map/all_to_all | solution.py:50
  206.5 3.8 %collective-permute-start.8 = (bf16[64,128,128]{2,1,0:T(8,128)(2,1)S(1)}, bf16[64,128,128]{2,1,0:T(8,128)(2,1)S(1)}, u32[]{:S(2)}, u32[]{:S(2)}) collective-permute-start(bf16[64,128,128]{2,1,0:T(8,128)(2,1)S(1)} %all_to_all.28.chunks), channel_id=1, source_target_pairs={{0,16},{16,0},{1,17},{17,1},{2,18},{18,2},{3,19},{19,3},{4,20},{20... | collective-permute-start | bytes 6291464 | tf_op jit(solution)/shard_map/ppermute | solution.py:40
  210.3 0.0 collective-permute-start.9
  210.3 0.5 slice.11
  210.8 3.6 %shard_map.101.refs_0_ = f32[2,2048,512]{2,1,0:T(8,128)} custom-call(s32[1]{0:T(128)} %bitcast.info, bf16[64,128,128]{2,1,0:T(8,128)(2,1)S(1)} %all_to_all.28.chunks), custom_call_target="tpu_custom_call" | custom-call | bytes 6291456 | tf_op jit(solution)/shard_map/pallas_call | solution.py:589
  214.4 0.0 collective-permute-done.8.chunks
  214.4 3.6 %shard_map.102 = f32[2,2048,512]{2,1,0:T(8,128)} custom-call(s32[1]{0:T(128)S(6)} %sub.3.info, bf16[64,128,128]{2,1,0:T(8,128)(2,1)S(1)} %collective-permute-done.8.chunks, f32[2,2048,512]{2,1,0:T(8,128)} %shard_map.101.refs_0_), custom_call_target="tpu_custom_call", output_to_operand_aliasing={{}: (2, {})} | custom-call | bytes 6291456 | tf_op jit(solution)/shard_map/pallas_call | solution.py:589
  218.0 0.0 collective-permute-done.9.bias_got
  218.0 17.1 %all-gather.3.cloned.1.call-done = bf16[12288,128]{1,0:T(8,128)(2,1)} async-done(((bf16[96,128]{1,0:T(8,128)(2,1)}), bf16[12288,128]{1,0:T(8,128)(2,1)}) %all-gather.3.cloned.1.call-update) | async-done | bytes 3145744 | tf_op jit(solution)/shard_map/all_gather | solution.py:573
  235.1 1.9 copy-done.1
  237.0 4.7 %shard_map.103 = (f32[3,1024,512]{2,1,0:T(8,128)}, f32[512]{0:T(512)}, f32[3,512]{1,0:T(4,128)}) custom-call(s32[3]{0:T(128)S(1)} %pad_add_fusion.info, bf16[128,96,128]{2,1,0:T(8,128)(2,1)S(1)} %bitcast.12, bf16[128,96,128]{2,1,0:T(8,128)(2,1)S(1)} %bitcast.13, f32[8,128]{1,0:T(8,128)S(1)} %get-tuple-element.45.bias, ...), custom_call_target="tpu_custom_call" | custom-call | bytes 10485760 | tf_op jit(solution)/shard_map/pallas_call | solution.py:608
  (7 shorter events, 0.0 us)
Async XLA Ops:
  7.2 15.1 %copy-start = (bf16[3,1024,512]{2,1,0:T(8,128)(2,1)S(1)}, bf16[3,1024,512]{2,1,0:T(8,128)(2,1)}, u32[]{:S(2)}) copy-start(bf16[3,1024,512]{2,1,0:T(8,128)(2,1)} %w_hbm.1) | copy-start | bytes 9437188
  7.2 15.1 %copy-start.4 = (f32[3,512]{1,0:T(4,128)S(1)}, f32[3,512]{1,0:T(4,128)}, u32[]{:S(2)}) copy-start(f32[3,512]{1,0:T(4,128)} %b.1) | copy-start | bytes 18436
  7.2 22.3 %collective-permute-start.4 = (bf16[256,4096]{1,0:T(8,128)(2,1)}, bf16[256,4096]{1,0:T(8,128)(2,1)}, u32[]{:S(2)}, u32[]{:S(2)}) collective-permute-start(bf16[256,4096]{1,0:T(8,128)(2,1)} %bitcast.14), channel_id=1, source_target_pairs={{0,16},{16,0},{1,17},{17,1},{2,18},{18,2},{3,19},{19,3},{4,20},{20... | collective-permute-start | bytes 6291464 | tf_op jit(solution)/shard_map/ppermute | solution.py:40
  13.6 5.2 %collective-permute-start = (bf16[32,512]{1,0:T(8,128)(2,1)S(1)}, bf16[32,512]{1,0:T(8,128)(2,1)S(1)}, u32[]{:S(2)}, u32[]{:S(2)}) collective-permute-start(bf16[32,512]{1,0:T(8,128)(2,1)S(1)} %get-tuple-element.50), channel_id=1, source_target_pairs={{0,1},{1,2},{2,3},{3,4},{4,5},{5,6},{6,7},{7,8},{8,9},{9,10},{10,1... | collective-permute-start | bytes 98312 | tf_op jit(solution)/shard_map/ppermute | solution.py:46
  17.4 4.8 %collective-permute-start.1 = (bf16[32,512]{1,0:T(8,128)(2,1)S(1)}, bf16[32,512]{1,0:T(8,128)(2,1)S(1)}, u32[]{:S(2)}, u32[]{:S(2)}) collective-permute-start(bf16[32,512]{1,0:T(8,128)(2,1)S(1)} %get-tuple-element.49), channel_id=1, source_target_pairs={{1,0},{2,1},{3,2},{4,3},{5,4},{6,5},{7,6},{8,7},{9,8},{10,9},{11,1... | collective-permute-start | bytes 98312 | tf_op jit(solution)/shard_map/ppermute | solution.py:46
  26.2 3.2 %collective-permute-start.2 = (bf16[64,48,128]{2,1,0:T(8,128)(2,1)S(1)}, bf16[64,48,128]{2,1,0:T(8,128)(2,1)S(1)}, u32[]{:S(2)}, u32[]{:S(2)}) collective-permute-start(bf16[64,48,128]{2,1,0:T(8,128)(2,1)S(1)} %get-tuple-element.28), channel_id=1, source_target_pairs={{0,16},{16,0},{1,17},{17,1},{2,18},{18,2},{3,19},{19,3},{4,20},{20... | collective-permute-start | bytes 2359304 | tf_op jit(solution)/shard_map/ppermute | solution.py:40
  27.5 1.9 collective-permute-start.3
  31.4 53.7 %copy-start.3 = (f32[256,512]{1,0:T(8,128)S(1)}, f32[256,512]{1,0:T(8,128)}, u32[]{:S(2)}) copy-start(f32[256,512]{1,0:T(8,128)} %get-tuple-element.52.sq0_hbm) | copy-start | bytes 1572868
  80.0 5.1 %collective-permute-start.5 = (bf16[64,48,128]{2,1,0:T(8,128)(2,1)S(1)}, bf16[64,48,128]{2,1,0:T(8,128)(2,1)S(1)}, u32[]{:S(2)}, u32[]{:S(2)}) collective-permute-start(bf16[64,48,128]{2,1,0:T(8,128)(2,1)S(1)} %all_to_all.26.half_cov), channel_id=1, source_target_pairs={{0,16},{16,0},{1,17},{17,1},{2,18},{18,2},{3,19},{19,3},{4,20},{20... | collective-permute-start | bytes 2359304 | tf_op jit(solution)/shard_map/ppermute | solution.py:40
  97.7 3.9 %collective-permute-start.7 = (bf16[64,112,128]{2,1,0:T(8,128)(2,1)S(1)}, bf16[64,112,128]{2,1,0:T(8,128)(2,1)S(1)}, u32[]{:S(2)}, u32[]{:S(2)}) collective-permute-start(bf16[64,112,128]{2,1,0:T(8,128)(2,1)S(1)} %get-tuple-element.40), channel_id=1, source_target_pairs={{0,16},{16,0},{1,17},{17,1},{2,18},{18,2},{3,19},{19,3},{4,20},{20... | collective-permute-start | bytes 5505032 | tf_op jit(solution)/shard_map/ppermute | solution.py:40
  103.5 6.4 %copy-start.2 = (bf16[1,256,4096]{2,1,0:T(8,128)(2,1)S(1)}, bf16[1,256,4096]{2,1,0:T(8,128)(2,1)}, u32[]{:S(2)}) copy-start(bf16[1,256,4096]{2,1,0:T(8,128)(2,1)} %param.5) | copy-start | bytes 6291460
  103.5 30.7 %all-to-all-start.2 = ((bf16[64,112,128]{2,1,0:T(8,128)(2,1)}), bf16[64,112,128]{2,1,0:T(8,128)(2,1)}, u32[]{:S(2)}, u32[]{:S(2)}) async-start(bf16[64,112,128]{2,1,0:T(8,128)(2,1)} %shard_map.98), calls=%async_computation.2 | async-start | bytes 3670016 | tf_op jit(solution)/shard_map/all_to_all | solution.py:50
  109.2 126.0 %all-gather.3.cloned.1.call-start = ((), (), s32[]{:S(2)}) async-start(), calls=%async_computation.5 | async-start | bytes 3170304 | tf_op jit(solution)/shard_map/all_gather | solution.py:573
  109.2 2.7 %collective-permute-start.6 = (bf16[256,512]{1,0:T(8,128)(2,1)S(1)}, bf16[256,512]{1,0:T(8,128)(2,1)S(1)}, u32[]{:S(2)}, u32[]{:S(2)}) collective-permute-start(bf16[256,512]{1,0:T(8,128)(2,1)S(1)} %get-tuple-element.37.dpre), channel_id=1, source_target_pairs={{0,16},{16,0},{1,17},{17,1},{2,18},{18,2},{3,19},{19,3},{4,20},{20... | collective-permute-start | bytes 786440 | tf_op jit(solution)/shard_map/ppermute | solution.py:40
  206.5 7.9 %collective-permute-start.8 = (bf16[64,128,128]{2,1,0:T(8,128)(2,1)S(1)}, bf16[64,128,128]{2,1,0:T(8,128)(2,1)S(1)}, u32[]{:S(2)}, u32[]{:S(2)}) collective-permute-start(bf16[64,128,128]{2,1,0:T(8,128)(2,1)S(1)} %all_to_all.28.chunks), channel_id=1, source_target_pairs={{0,16},{16,0},{1,17},{17,1},{2,18},{18,2},{3,19},{19,3},{4,20},{20... | collective-permute-start | bytes 6291464 | tf_op jit(solution)/shard_map/ppermute | solution.py:40
  210.3 7.7 %collective-permute-start.9 = (f32[8,128]{1,0:T(8,128)S(1)}, f32[8,128]{1,0:T(8,128)S(1)}, u32[]{:S(2)}, u32[]{:S(2)}) collective-permute-start(f32[8,128]{1,0:T(8,128)S(1)} %get-tuple-element.45.bias), channel_id=1, source_target_pairs={{0,16},{16,0},{1,17},{17,1},{2,18},{18,2},{3,19},{19,3},{4,20},{20... | collective-permute-start | bytes 12296 | tf_op jit(solution)/shard_map/ppermute | solution.py:40
  235.1 1.9 copy-start.1
Sparse Core Ops, SparseCore 0:
  136.7 98.3 all-gather.2

commit v7 on v5

--- a/solution.py
+++ b/solution.py
@@ -44,6 +44,36 @@
     count = lax.axis_size("tm")
     first, last = max(0, -steps), min(count, count - steps)
     return lax.ppermute(value, "tm", [(i, i + steps) for i in range(first, last)])
+
+
+def shifts(count):
+    return (0, 1, 3, 2) if count == 4 else tuple(range(count))
+
+
+def spin(value, axis, steps):
+    segments = lax.axis_size("tm")
+    nz = grid_side(segments)
+    ny = segments // nz
+    if axis == "x":
+        n = lax.axis_size("x")
+        return lax.ppermute(value, "x", [(i, (i + steps) % n) for i in range(n)])
+    pairs = []
+    for i in range(segments):
+        y, z = divmod(i, nz)
+        y, z = ((y + steps) % ny, z) if axis == "y" else (y, (z + steps) % nz)
+        pairs.append((i, y * nz + z))
+    return lax.ppermute(value, "tm", pairs)
+
+
+def grid_side(count):
+    side = 1
+    while (side * 2) * (side * 2) <= count:
+        side *= 2
+    return side
+
+
+def along(value, axis, count):
+    return jnp.stack([value] + [spin(value, axis, k) for k in shifts(count)[1:]])
 
 
 def exchange(value):
@@ -379,54 +409,79 @@
     packed[:, at + body :, :] = jnp.broadcast_to(tail[None], (count,) + tail.shape)
 
 
-def sum_kernel(arrived, tails, full, bias):
-    peers = arrived.shape[0]
-
-    def add(p, acc):
-        return acc + arrived[p].astype(F32)
-
-    value = lax.fori_loop(0, peers, add, jnp.zeros(arrived.shape[1:], F32), unroll=4)
-    full[...] = jnp.broadcast_to(value.astype(BF)[None], full.shape)
-
-    @pl.when(pl.program_id(0) == 0)
-    def _():
-        def add_tail(p, acc):
-            return acc + tails[p].astype(F32)
-
-        t = lax.fori_loop(0, peers, add_tail, jnp.zeros(tails.shape[1:], F32))
-        n = t.shape[0] // 2
-        bias[...] = t[:n] + t[n:]
-
-
-def unpack_kernel(sizes, nbiases, info, chunks, *refs):
+def sum_kernel(sizes, arrived, half_a, half_b, bias):
     in_size, conv_size, nb = sizes
+    peers, wide = arrived.shape[:2]
+    nh = nb // 2
+
+    def total_of(at, count):
+        def add(p, acc):
+            return acc + arrived[p, at : at + count, :].astype(F32)
+
+        return lax.fori_loop(0, peers, add, jnp.zeros((count, LANES), F32), unroll=4)
+
+    for side, ref in enumerate((half_a, half_b)):
+        count = nh * in_size
+        ref[:count] = total_of(side * count, count).astype(BF)
+        ch = nh // 2 * conv_size
+        for layer in range(NL):
+            at = nb * in_size + (layer * nh) * conv_size + side * ch
+            ref[count + layer * ch : count + (layer + 1) * ch] = total_of(at, ch).astype(BF)
+    nbias = bias.shape[0]
+    t = total_of(wide - 2 * nbias, 2 * nbias)
+    bias[...] = t[:nbias] + t[nbias:]
+
+
+def unpack_kernel(sizes, nbiases, inner_x, info, chunks, *refs):
+    in_size, conv_size, nb, ny, nz, inner = sizes
+    core, peer, inner_at, z_at = info[0], info[2], info[3], info[4]
     if nbiases:
         bias, bias_got = refs[:2]
         w_in, w_conv, b_in, b_conv = refs[-4:]
     else:
         w_in, w_conv = refs[-2:]
-    count = chunks.shape[0]
-    for j in range(nb):
-        part = chunks[:, j * in_size : (j + 1) * in_size, :].astype(F32)
-        w_in[0, :, j * LANES : (j + 1) * LANES] = part.reshape(count * in_size, LANES)
-    for layer in range(NL):
-        for j in range(nb // 2):
-            at = nb * in_size + (layer * (nb // 2) + j) * conv_size
-            part = chunks[:, at : at + conv_size, :].astype(F32)
-            w_conv[layer, :, j * LANES : (j + 1) * LANES] = part.reshape(count * conv_size, LANES)
+    nh = nb // 2
+    half = nh * LANES
+    ch = nh // 2 * conv_size
+    for a, shift_a in enumerate(shifts(inner)):
+        i = lax.rem(inner_at + inner - shift_a, inner)
+        for b, shift_b in enumerate(shifts(nz)):
+            z = lax.rem(z_at + nz - shift_b, nz)
+            value = chunks[0, a, b].astype(F32)
+            rows = pl.ds(pl.multiple_of(z * in_size, in_size), in_size)
+            left = jnp.concatenate(
+                [value[j * in_size : (j + 1) * in_size] for j in range(nh)], axis=1
+            )
+            crow = pl.ds(pl.multiple_of(z * conv_size, conv_size), conv_size)
+            if inner_x:
+                w_in[0, i, 0, rows, :] = left
+            else:
+                w_in[0, 0, i, rows, :] = left
+            for layer in range(NL):
+                at = nh * in_size + layer * ch
+                part = jnp.concatenate(
+                    [
+                        value[at + j * conv_size : at + (j + 1) * conv_size]
+                        for j in range(nh // 2)
+                    ],
+                    axis=1,
+                )
+                if inner_x:
+                    w_conv[layer, i, 0, crow, :] = part
+                else:
+                    w_conv[layer, 0, i, crow, :] = part
     if nbiases:
 
         @pl.when(pl.program_id(0) == 0)
         def _():
-            swapped = info[0] == 0
+            first = info[5] == 0
             n = NL + 1
-            rows = []
+            parts = []
             for side in range(2):
-                keep = bias_got[...] if side == 0 else bias[...]
-                swap = bias[...] if side == 0 else bias_got[...]
-                value = jnp.where(swapped, keep, swap)
-                rows += [value[j * n : (j + 1) * n] for j in range(nb // 2)]
-            full = jnp.concatenate(rows, axis=1)
+                mine_side = first if side == 0 else jnp.logical_not(first)
+                value = jnp.where(mine_side, bias[...], bias_got[...])
+                parts += [value[j * n : (j + 1) * n] for j in range(nh)]
+            full = jnp.concatenate(parts, axis=1)
             b_in[...] = full[0]
             b_conv[...] = full[1:]
 
@@ -448,12 +503,10 @@
     ext = rows + 2 * HALO
     frames_got = swap_core(frames)
 
-    edges = jnp.concatenate([frames[:HALO], frames[rows - HALO :]], axis=0)
-    edges = jnp.tanh(jnp.dot(edges, w_in, preferred_element_type=F32) + b_in).astype(BF)
-    before = shift_segment(edges[HALO:], 1)
-    after = shift_segment(edges[:HALO], -1)
     squash0 = jnp.tanh(jnp.dot(frames, w_in, preferred_element_type=F32) + b_in)
     own = squash0.astype(BF)
+    before = shift_segment(own[rows - HALO :], 1)
+    after = shift_segment(own[:HALO], -1)
     hid, sq, mine, other, means = call(
         functools.partial(forward_kernel, dims),
         [
@@ -553,54 +606,82 @@
         out_shape=sds((peers, wide, LANES), BF),
         compiler_params=small_params,
     )(info, earlier, frames_got, dpre_got, mine, got)
-    arrived = exchange(packed)
-    block = 32
-    full, bias = pl.pallas_call(
-        sum_kernel,
-        grid=(body // block,),
-        out_shape=[sds((peers, body, LANES), BF), sds((nbias, LANES), F32)],
-        in_specs=[
-            pl.BlockSpec((peers, block, LANES), lambda i: (0, i, 0)),
-            pl.BlockSpec((peers, 2 * nbias, LANES), lambda i: (0, body // (2 * nbias), 0)),
-        ],
-        out_specs=[
-            pl.BlockSpec((peers, block, LANES), lambda i: (0, i, 0)),
-            pl.BlockSpec((nbias, LANES), lambda i: (0, 0)),
-        ],
+    nz = grid_side(segments)
+    ny = segments // nz
+    nx = peers // segments
+    part = nh * in_size + NL * (nh // 2) * conv_size
+    half_a, half_b, bias = pl.pallas_call(
+        functools.partial(sum_kernel, (in_size, conv_size, nb)),
+        in_specs=[vmem],
+        out_specs=[vmem] * 3,
+        out_shape=[sds((part, LANES), BF), sds((part, LANES), BF), sds((nbias, LANES), F32)],
         compiler_params=small_params,
-    )(arrived, arrived)
+    )(exchange(packed))
+    both = along(jnp.stack([half_a, half_b]), "z", nz)
+    plane_a, plane_b = lax.optimization_barrier(
+        (along(both[:, 0], "y", ny), along(both[:, 1], "x", nx))
+    )
+    full_a, full_b = along(plane_a, "x", nx), along(plane_b, "y", ny)
     bias_got = swap_core(bias)
-    full = exchange(full)
-    steps = 8
-    group = peers // steps
-
-    def unpack(chunks, at, biases, earlier):
+    full_a, full_b, bias_got = lax.optimization_barrier((full_a, full_b, bias_got))
+    peer = lax.axis_index("x") * segments + segment
+    place = jnp.stack([lax.axis_index("x"), segment // nz, segment % nz])
+
+    def unpack(chunks, side, inner_x, owner, biases, earlier):
         spare = [sds((ch,), F32), sds((NL, ch), F32)] if biases else []
+        outer, inner = (ny, nx) if inner_x else (nx, ny)
+        outer_at, inner_at = (place[1], place[0]) if inner_x else (place[0], place[1])
+        table = [lax.rem(outer_at + outer - k, outer) for k in shifts(outer)]
+        head = [owner, outer_at, peer, inner_at, place[2], core]
+        info = jnp.stack(head + table).astype(jnp.int32)
+        if inner_x:
+            in_map = lambda i, at: (at[0], 0, at[6 + i], 0, side)
+            conv_map = lambda i, at: (0, 0, at[6 + i], 0, 2 * at[0] + side)
+            xs, ys = nx, 1
+        else:
+            in_map = lambda i, at: (at[0], at[6 + i], 0, 0, side)
+            conv_map = lambda i, at: (0, at[6 + i], 0, 0, 2 * at[0] + side)
+            xs, ys = 1, ny
         return pl.pallas_call(
-            functools.partial(unpack_kernel, (in_size, conv_size, nb), len(biases)),
+            functools.partial(
+                unpack_kernel, (in_size, conv_size, nb, ny, nz, inner), len(biases), inner_x
+            ),
             grid_spec=pltpu.PrefetchScalarGridSpec(
                 num_scalar_prefetch=1,
-                grid=(steps,),
-                in_specs=[pl.BlockSpec((group, body, LANES), lambda i, at: (i, 0, 0))]
+                grid=(outer,),
+                in_specs=[
+                    pl.BlockSpec((1, inner, nz, part, LANES), lambda i, at: (i, 0, 0, 0, 0))
+                ]
                 + [pl.BlockSpec(b.shape, lambda i, at: (0, 0)) for b in biases]
                 + [hbm] * len(earlier),
                 out_specs=[
-                    pl.BlockSpec((1, group * in_size, ch), lambda i, at: (at[0], i, 0)),
-                    pl.BlockSpec((NL, group * conv_size, ch // 2), lambda i, at: (0, i, at[0])),
+                    pl.BlockSpec((1, xs, ys, nz * in_size, ch // 2), in_map),
+                    pl.BlockSpec((NL, xs, ys, nz * conv_size, ch // 4), conv_map),
                 ]
                 + [pl.BlockSpec(b.shape, lambda i, at, n=len(b.shape): (0,) * n) for b in spare],
             ),
-            out_shape=[sds((2, half_features, ch), F32), sds((NL, 2 * ch, ch), F32)] + spare,
+            out_shape=[
+                sds((2, nx, ny, nz * in_size, ch), F32),
+                sds((NL, nx, ny, nz * conv_size, ch), F32),
+            ]
+            + spare,
             input_output_aliases={2 + len(biases) + n: n for n in range(len(earlier))},
             compiler_params=small_params,
-            cost_estimate=pl.CostEstimate(flops=0, bytes_accessed=12 * 2**20, transcendentals=0),
-        )(at, chunks, *biases, *earlier)
-
-    got = swap_core(full)
-    partial = unpack(full, info[:1], [], [])
-    got, bias_got = lax.optimization_barrier((got, bias_got))
-    g_in, g_conv, g_b_in, g_b_conv = unpack(got, 1 - info[:1], [bias, bias_got], partial)
-    return score[0, 0], g_in.reshape(features, ch), g_b_in, g_conv, g_b_conv
+            cost_estimate=pl.CostEstimate(flops=0, bytes_accessed=6 * 2**20, transcendentals=0),
+        )(info, chunks, *biases, *earlier)
+
+    got_a, got_b = swap_core(full_a), swap_core(full_b)
+    partial = unpack(full_a, 0, False, core, [], [])
+    partial = unpack(full_b, 1, True, core, [], partial)
+    partial = unpack(got_a, 0, False, 1 - core, [], partial)
+    g_in, g_conv, g_b_in, g_b_conv = unpack(got_b, 1, True, 1 - core, [bias, bias_got], partial)
+    return (
+        score[0, 0],
+        g_in.reshape(features, ch),
+        g_b_in,
+        g_conv.reshape(NL, 2 * ch, ch),
+        g_b_conv,
+    )
 
 
 def solution(mesh):

time: 220 us -> 227 us (1.032)
  blocking collectives: 152 us -> 98.6 us
  starting transfers between devices: 15 us -> 53.6 us
  waiting for transfers between devices: 6.74 us -> 21.1 us
  Pallas kernels: 37.1 us -> 43.9 us
    all_to_all x4 -> x3, blocking collectives: 152 us -> 98.6 us  [exchange(): return lax.all_to_all(value, PEERS, 0, 0, tiled=True)]
    ppermute x0 -> x15, starting transfers between devices: none -> 21.8 us  [the longest x6 11.2 us: spin(): return lax.ppermute(value, 'x', [(i, (i + steps) % n) for i in range(n)])]
    ppermute x8 -> x9, starting transfers between devices: 9.46 us -> 26.9 us  [swap_core(): return lax.ppermute(value, 'c', [(0, 1), (1, 0)])]
    ppermute x0 -> x15, waiting for transfers between devices: none -> 12.2 us  [the longest x9 11.4 us: spin(): return lax.ppermute(value, 'tm', pairs)]
    pallas_call x3 -> x5, Pallas kernels: 11.2 us -> 18 us  [the longest x4 16.8 us: unpack(): pl.pallas_call(functools.partial(unpack_kernel, (in_size, conv_size, nb,...]
    ppermute x2, waiting for transfers between devices: 0.01 us -> 3.46 us  [shift_segment(): lax.ppermute(value, 'tm', [(i, i + steps) for i in range(first, last)])]
    dot_general x1 -> x0, matrix products: 3.04 us -> none  [per_device(): jnp.dot(edges, w_in, preferred_element_type=F32) + b_in]
    ppermute x8 -> x9, waiting for transfers between devices: 6.74 us -> 5.43 us  [swap_core(): return lax.ppermute(value, 'c', [(0, 1), (1, 0)])]
  transfers between devices with their start and end apart: 10 -> 26, of which waited for: 4 -> 10; matrix products, arithmetic and copies ran while one was open for 4% -> 3% of each run, Pallas kernels for 5% -> 8%
where the time goes in v7:
time: 227 us; the launch traced here: 226 us
  blocking collectives  98.6 us (43%)
  starting transfers between devices  53.6 us (24%)
  Pallas kernels  43.9 us (19%)
  waiting for transfers between devices  21.1 us (9%)
  matrix products  5.05 us (2%)
    all_to_all x3, blocking collectives, exchange(): return lax.all_to_all(value, PEERS, 0, 0, tiled=True)  98.6 us
    ppermute x9, starting transfers between devices, swap_core(): return lax.ppermute(value, 'c', [(0, 1), (1, 0)])  26.9 us
    pallas_call x4, Pallas kernels, unpack(): pl.pallas_call(functools.partial(unpack_kernel, (in_size, conv_size, nb,...  16.8 us
    pallas_call x1, Pallas kernels, per_device(): pl.pallas_call(functools.partial(step_kernel, dims), out_shape=[sds((8, L...  12.6 us
    ppermute x9, waiting for transfers between devices, spin(): return lax.ppermute(value, 'tm', pairs)  11.4 us
    ppermute x6, starting transfers between devices, spin(): return lax.ppermute(value, 'x', [(i, (i + steps) % n) for i in range(n)])  11.2 us
    ppermute x9, starting transfers between devices, spin(): return lax.ppermute(value, 'tm', pairs)  10.7 us
    pallas_call x3, Pallas kernels, call(): pl.pallas_call(kernel, out_shape=outs, in_specs=specs, out_specs=[pl.Bloc...  7.36 us
  transfers between devices with their start and end apart: 26, of which 10 were waited for; matrix products, arithmetic and copies ran while one was open for 3% of the time, Pallas kernels for 8%

profile of v7, /device:TPU:1, one launch (start us, length us, event | category | flops | bytes accessed | tf_op | source)
XLA Modules:
  0.0 226.2 jit_solution(6573572133504599040)
XLA Ops:
  0.6 1.5 collective-permute-start.4
  2.1 5.1 %fusion.4 = (bf16[256,512]{1,0:T(8,128)(2,1)S(1)}, f32[256,512]{1,0:T(8,128)}) fusion(f32[512]{0:T(512)} %param.7, bf16[4096,512]{1,0:T(8,128)(2,1)} %param.6, bf16[1,256,4096]{2,1,0:T(8,128)(2,1)} %param.5), kind=kOutput, calls=%fused_computation.16 | convolution fusion | flops 1074003968 | bytes 7079936 | tf_op jit(solution)/shard_map/dot_general | solution.py:506
  7.2 3.6 %collective-permute-start = (bf16[32,512]{1,0:T(8,128)(2,1)S(1)}, bf16[32,512]{1,0:T(8,128)(2,1)S(1)}, u32[]{:S(2)}, u32[]{:S(2)}) collective-permute-start(bf16[32,512]{1,0:T(8,128)(2,1)S(1)} %get-tuple-element.70), channel_id=1, source_target_pairs={{0,1},{1,2},{2,3},{3,4},{4,5},{5,6},{6,7},{7,8},{8,9},{9,10},{10,1... | collective-permute-start | bytes 98312 | tf_op jit(solution)/shard_map/ppermute | solution.py:46
  10.8 1.3 collective-permute-start.1
  12.2 3.5 %collective-permute-done.1.after = bf16[32,512]{1,0:T(8,128)(2,1)S(1)} collective-permute-done((bf16[32,512]{1,0:T(8,128)(2,1)S(1)}, bf16[32,512]{1,0:T(8,128)(2,1)S(1)}, u32[]{:S(2)}, u32[]{:S(2)}) %collective-permute-start.1) | collective-permute-done | bytes 32800 | tf_op jit(solution)/shard_map/ppermute | solution.py:46
  15.7 3.9 %shard_map.92 = (bf16[4,320,512]{2,1,0:T(8,128)(2,1)S(1)}, f32[3,320,512]{2,1,0:T(8,128)S(1)}, f32[64,48,128]{2,1,0:T(8,128)S(1)}, bf16[64,48,128]{2,1,0:T(8,128)(2,1)S(1)}, f32[8,512]{1,0:T(8,128)S(1)}) custom-call(s32[3]{0:T(128)S(1)} %pad_add_fusion.info, bf16[32,512]{1,0:T(8,128)(2,1)S(1)} %collective-permute-done.before, ...), custom_call_target="tpu_custom_call" | custom-call | tf_op jit(solution)/shard_map/pallas_call | solution.py:87
  19.6 1.3 collective-permute-start.2
  21.1 1.8 collective-permute-done.3.sib
  22.9 2.0 shard_map.93
  24.9 28.0 %all_to_all.15.arrived = bf16[64,64,128]{2,1,0:T(8,128)(2,1)S(1)} all-to-all(bf16[64,64,128]{2,1,0:T(8,128)(2,1)S(1)} %shard_map.93), channel_id=1, replica_groups=mesh['x'=4,'c'=2,'tm'=16] {'x','tm'}, dimensions={0} | all-to-all | bytes 2097152 | tf_op jit(solution)/shard_map/all_to_all | solution.py:80
  52.9 1.5 shard_map.94
  54.4 19.0 %all_to_all.16.half_cov = bf16[64,48,128]{2,1,0:T(8,128)(2,1)S(1)} all-to-all(bf16[64,48,128]{2,1,0:T(8,128)(2,1)S(1)} %get-tuple-element.42), channel_id=1, replica_groups=mesh['x'=4,'c'=2,'tm'=16] {'x','tm'}, dimensions={0} | all-to-all | bytes 1572864 | tf_op jit(solution)/shard_map/all_to_all | solution.py:80
  73.4 3.1 %collective-permute-start.5 = (bf16[64,48,128]{2,1,0:T(8,128)(2,1)S(1)}, bf16[64,48,128]{2,1,0:T(8,128)(2,1)S(1)}, u32[]{:S(2)}, u32[]{:S(2)}) collective-permute-start(bf16[64,48,128]{2,1,0:T(8,128)(2,1)S(1)} %all_to_all.16.half_cov), channel_id=1, source_target_pairs={{0,16},{16,0},{1,17},{17,1},{2,18},{18,2},{3,19},{19,3},{4,20},{20... | collective-permute-start | bytes 2359304 | tf_op jit(solution)/shard_map/ppermute | solution.py:40
  76.5 1.9 collective-permute-done.5.other_cov
  78.4 12.6 %shard_map.95 = (f32[8,128]{1,0:T(8,128)S(1)}, bf16[64,112,128]{2,1,0:T(8,128)(2,1)S(1)}, bf16[64,112,128]{2,1,0:T(8,128)(2,1)S(1)}, bf16[256,512]{1,0:T(8,128)(2,1)S(1)}) custom-call(s32[3]{0:T(128)S(1)} %pad_add_fusion.info, bf16[64,48,128]{2,1,0:T(8,128)(2,1)S(1)} %all_to_all.16.half_cov, bf16[64,48,128]{2,1,0:T(8,128)(2,1)S(1)} %collective-permute-done.5.other_cov, ...), custom_call_target="tpu_custom_call" | custom-call | tf_op jit(solution)/shard_map/pallas_call | solution.py:555
  91.1 0.5 collective-permute-start.7
  91.7 2.0 shard_map.96.earlier
  93.7 1.7 collective-permute-done.6.dpre_got
  95.3 3.9 %shard_map.97 = bf16[64,240,128]{2,1,0:T(8,128)(2,1)S(1)} custom-call(s32[3]{0:T(128)S(1)} %pad_add_fusion.info, f32[2048,512]{1,0:T(8,128)S(1)} %shard_map.96.earlier, bf16[256,4096]{1,0:T(8,128)(2,1)} %collective-permute-done.4.left_got, bf16[256,512]{1,0:T(8,128)(2,1)S(1)} %collective-permute-done.6.dpre_got, ...), custom_call_target="tpu_custom_call" | custom-call | tf_op jit(solution)/shard_map/pallas_call | solution.py:598
  99.2 51.6 %all_to_all.17.arrived = bf16[64,240,128]{2,1,0:T(8,128)(2,1)S(1)} all-to-all(bf16[64,240,128]{2,1,0:T(8,128)(2,1)S(1)} %shard_map.97), channel_id=1, replica_groups=mesh['x'=4,'c'=2,'tm'=16] {'x','tm'}, dimensions={0} | all-to-all | bytes 7864320 | tf_op jit(solution)/shard_map/all_to_all | solution.py:80
  150.8 1.3 shard_map.98
  152.1 0.8 collective-permute-start.8
  152.9 2.0 collective-permute-start.9
  154.9 1.0 collective-permute-start.10
  155.9 0.5 collective-permute-done.8
  156.4 3.2 %collective-permute-done.10 = bf16[2,112,128]{2,1,0:T(8,128)(2,1)S(1)} collective-permute-done((bf16[2,112,128]{2,1,0:T(8,128)(2,1)S(1)}, bf16[2,112,128]{2,1,0:T(8,128)(2,1)S(1)}, u32[]{:S(2)}, u32[]{:S(2)}) %collective-permute-start.10) | collective-permute-done | bytes 57376 | tf_op jit(solution)/shard_map/ppermute | solution.py:65
  159.7 0.6 collective-permute-start.14
  160.3 2.2 collective-permute-start.15
  162.4 0.6 collective-permute-start.16
  163.1 0.7 collective-permute-start.11
  163.8 2.0 collective-permute-start.12
  165.7 1.2 collective-permute-start.13
  167.0 0.8 collective-permute-done.16
  167.9 3.0 %collective-permute-done.13 = bf16[4,112,128]{2,1,0:T(8,128)(2,1)S(1)} collective-permute-done((bf16[4,112,128]{2,1,0:T(8,128)(2,1)S(1)}, bf16[4,112,128]{2,1,0:T(8,128)(2,1)S(1)}, u32[]{:S(2)}, u32[]{:S(2)}) %collective-permute-start.13) | collective-permute-done | bytes 114720 | tf_op jit(solution)/shard_map/ppermute | solution.py:65
  171.2 2.6 %collective-permute-start.21 = (bf16[4,4,112,128]{3,2,1,0:T(8,128)(2,1)S(1)}, bf16[4,4,112,128]{3,2,1,0:T(8,128)(2,1)S(1)}, u32[]{:S(2)}, u32[]{:S(2)}) collective-permute-start(bf16[4,4,112,128]{3,2,1,0:T(8,128)(2,1)S(1)} %pad_maximum_fusion.3), channel_id=1, source_target_pairs={{0,12},{1,13},{2,14},{3,15},{4,0},{5,1},{6,2},{7,3},{8,4},{9,5},{1... | collective-permute-start | bytes 1376264 | tf_op jit(solution)/shard_map/ppermute | solution.py:65
  173.8 0.3 collective-permute-start.22
  174.0 0.9 collective-permute-start.17
  174.9 1.8 collective-permute-start.18
  176.7 4.6 %collective-permute-done.20 = bf16[4,4,112,128]{3,2,1,0:T(8,128)(2,1)S(1)} collective-permute-done((bf16[4,4,112,128]{3,2,1,0:T(8,128)(2,1)S(1)}, bf16[4,4,112,128]{3,2,1,0:T(8,128)(2,1)S(1)}, u32[]{:S(2)}, u32[]{:S(2)}) %collective-permute-start.20) | collective-permute-done | bytes 458784 | tf_op jit(solution)/shard_map/ppermute | solution.py:65
  181.2 5.1 %collective-permute-start.19 = (bf16[4,4,112,128]{3,2,1,0:T(8,128)(2,1)S(1)}, bf16[4,4,112,128]{3,2,1,0:T(8,128)(2,1)S(1)}, u32[]{:S(2)}, u32[]{:S(2)}) collective-permute-start(bf16[4,4,112,128]{3,2,1,0:T(8,128)(2,1)S(1)} %pad_maximum_fusion.2), channel_id=1, source_target_pairs={{0,64},{32,96},{64,0},{96,32},{1,65},{33,97},{65,1},{97,33},{2,66}... | collective-permute-start | bytes 1376264 | tf_op jit(solution)/shard_map/ppermute | solution.py:59
  186.4 13.1 %collective-permute-start.23 = (f32[8,128]{1,0:T(8,128)S(1)}, f32[8,128]{1,0:T(8,128)S(1)}, u32[]{:S(2)}, u32[]{:S(2)}) collective-permute-start(f32[8,128]{1,0:T(8,128)S(1)} %get-tuple-element.55.refs_0_), channel_id=1, source_target_pairs={{0,16},{16,0},{1,17},{17,1},{2,18},{18,2},{3,19},{19,3},{4,20},{20... | collective-permute-start | bytes 12296 | tf_op jit(solution)/shard_map/ppermute | solution.py:40
  199.8 1.5 pad_maximum_fusion.chunks
  201.2 7.1 %collective-permute-start.25 = (bf16[4,4,4,112,128]{4,3,2,1,0:T(8,128)(2,1)}, bf16[4,4,4,112,128]{4,3,2,1,0:T(8,128)(2,1)}, u32[]{:S(2)}, u32[]{:S(2)}) collective-permute-start(bf16[4,4,4,112,128]{4,3,2,1,0:T(8,128)(2,1)} %pad_maximum_fusion.chunks), channel_id=1, source_target_pairs={{0,16},{16,0},{1,17},{17,1},{2,18},{18,2},{3,19},{19,3},{4,20},{20... | collective-permute-start | bytes 5505032 | tf_op jit(solution)/shard_map/ppermute | solution.py:40
  208.7 0.5 slice.17
  209.2 4.6 %shard_map.99 = (f32[2,4,4,128,512]{4,3,2,1,0:T(8,128)}, f32[3,4,4,64,512]{4,3,2,1,0:T(8,128)}) custom-call(s32[10]{0:T(128)S(1)} %stack.202.info, bf16[4,4,4,112,128]{4,3,2,1,0:T(8,128)(2,1)} %pad_maximum_fusion.chunks), custom_call_target="tpu_custom_call" | custom-call | bytes 6291456 | tf_op jit(solution)/shard_map/pallas_call | solution.py:645
  213.8 2.9 %shard_map.100 = (f32[2,4,4,128,512]{4,3,2,1,0:T(8,128)}, f32[3,4,4,64,512]{4,3,2,1,0:T(8,128)}) custom-call(s32[10]{0:T(128)S(1)} %stack.201.info, bf16[4,4,4,112,128]{4,3,2,1,0:T(8,128)(2,1)S(1)} %pad_maximum_fusion.1.chunks, f32[2,4,4,128,512]{4,3,2,1,0:T(8,128)} %get-tuple-element.59.refs_0_, ...), custom_call_target="tpu_custom_call", output_to_operand_aliasing={{0}: (2, {}), {1}: (3, {})} | custom-call | bytes 6291456 | tf_op jit(solution)/shard_map/pallas_call | solution.py:645
  216.7 4.6 %shard_map.101 = (f32[2,4,4,128,512]{4,3,2,1,0:T(8,128)}, f32[3,4,4,64,512]{4,3,2,1,0:T(8,128)}) custom-call(s32[10]{0:T(128)S(1)} %stack.200.info, bf16[4,4,4,112,128]{4,3,2,1,0:T(8,128)(2,1)} %collective-permute-done.25.chunks, f32[2,4,4,128,512]{4,3,2,1,0:T(8,128)} %get-tuple-element.61.refs_0_, ...), custom_call_target="tpu_custom_call", output_to_operand_aliasing={{0}: (2, {}), {1}: (3, {})} | custom-call | bytes 6291456 | tf_op jit(solution)/shard_map/pallas_call | solution.py:645
  221.4 4.6 %shard_map.102 = (f32[2,4,4,128,512]{4,3,2,1,0:T(8,128)}, f32[3,4,4,64,512]{4,3,2,1,0:T(8,128)}, f32[512]{0:T(512)}, f32[3,512]{1,0:T(4,128)}) custom-call(s32[10]{0:T(128)S(1)} %stack.169.info, bf16[4,4,4,112,128]{4,3,2,1,0:T(8,128)(2,1)} %collective-permute-done.24.chunks, ...), custom_call_target="tpu_custom_call", output_to_operand_aliasing={{0}: (4, {}), {1}: (5, {})} | custom-call | bytes 6291456 | tf_op jit(solution)/shard_map/pallas_call | solution.py:645
  (41 shorter events, 1.4 us)
Async XLA Ops:
  0.6 15.0 %copy-start.3 = (f32[3,512]{1,0:T(4,128)S(1)}, f32[3,512]{1,0:T(4,128)}, u32[]{:S(2)}) copy-start(f32[3,512]{1,0:T(4,128)} %b.1) | copy-start | bytes 18436
  0.6 22.3 %collective-permute-start.4 = (bf16[256,4096]{1,0:T(8,128)(2,1)}, bf16[256,4096]{1,0:T(8,128)(2,1)}, u32[]{:S(2)}, u32[]{:S(2)}) collective-permute-start(bf16[256,4096]{1,0:T(8,128)(2,1)} %bitcast.59), channel_id=1, source_target_pairs={{0,16},{16,0},{1,17},{17,1},{2,18},{18,2},{3,19},{19,3},{4,20},{20... | collective-permute-start | bytes 6291464 | tf_op jit(solution)/shard_map/ppermute | solution.py:40
  2.1 13.5 %copy-start = (bf16[3,1024,512]{2,1,0:T(8,128)(2,1)S(1)}, bf16[3,1024,512]{2,1,0:T(8,128)(2,1)}, u32[]{:S(2)}) copy-start(bf16[3,1024,512]{2,1,0:T(8,128)(2,1)} %w_hbm.1) | copy-start | bytes 9437188
  7.2 5.0 %collective-permute-start = (bf16[32,512]{1,0:T(8,128)(2,1)S(1)}, bf16[32,512]{1,0:T(8,128)(2,1)S(1)}, u32[]{:S(2)}, u32[]{:S(2)}) collective-permute-start(bf16[32,512]{1,0:T(8,128)(2,1)S(1)} %get-tuple-element.70), channel_id=1, source_target_pairs={{0,1},{1,2},{2,3},{3,4},{4,5},{5,6},{6,7},{7,8},{8,9},{9,10},{10,1... | collective-permute-start | bytes 98312 | tf_op jit(solution)/shard_map/ppermute | solution.py:46
  10.8 4.8 %collective-permute-start.1 = (bf16[32,512]{1,0:T(8,128)(2,1)S(1)}, bf16[32,512]{1,0:T(8,128)(2,1)S(1)}, u32[]{:S(2)}, u32[]{:S(2)}) collective-permute-start(bf16[32,512]{1,0:T(8,128)(2,1)S(1)} %get-tuple-element.69), channel_id=1, source_target_pairs={{1,0},{2,1},{3,2},{4,3},{5,4},{6,5},{7,6},{8,7},{9,8},{10,9},{11,1... | collective-permute-start | bytes 98312 | tf_op jit(solution)/shard_map/ppermute | solution.py:46
  19.6 3.3 %collective-permute-start.2 = (bf16[64,48,128]{2,1,0:T(8,128)(2,1)S(1)}, bf16[64,48,128]{2,1,0:T(8,128)(2,1)S(1)}, u32[]{:S(2)}, u32[]{:S(2)}) collective-permute-start(bf16[64,48,128]{2,1,0:T(8,128)(2,1)S(1)} %get-tuple-element.38), channel_id=1, source_target_pairs={{0,16},{16,0},{1,17},{17,1},{2,18},{18,2},{3,19},{19,3},{4,20},{20... | collective-permute-start | bytes 2359304 | tf_op jit(solution)/shard_map/ppermute | solution.py:40
  21.0 1.9 collective-permute-start.3
  52.9 25.5 %copy-start.2 = (f32[256,512]{1,0:T(8,128)S(1)}, f32[256,512]{1,0:T(8,128)}, u32[]{:S(2)}) copy-start(f32[256,512]{1,0:T(8,128)} %get-tuple-element.78.sq0_hbm) | copy-start | bytes 1572868
  73.4 5.1 %collective-permute-start.5 = (bf16[64,48,128]{2,1,0:T(8,128)(2,1)S(1)}, bf16[64,48,128]{2,1,0:T(8,128)(2,1)S(1)}, u32[]{:S(2)}, u32[]{:S(2)}) collective-permute-start(bf16[64,48,128]{2,1,0:T(8,128)(2,1)S(1)} %all_to_all.16.half_cov), channel_id=1, source_target_pairs={{0,16},{16,0},{1,17},{17,1},{2,18},{18,2},{3,19},{19,3},{4,20},{20... | collective-permute-start | bytes 2359304 | tf_op jit(solution)/shard_map/ppermute | solution.py:40
  78.4 13.2 %copy-start.1 = (bf16[1,256,4096]{2,1,0:T(8,128)(2,1)S(1)}, bf16[1,256,4096]{2,1,0:T(8,128)(2,1)}, u32[]{:S(2)}) copy-start(bf16[1,256,4096]{2,1,0:T(8,128)(2,1)} %param.5) | copy-start | bytes 6291460
  91.1 4.2 %collective-permute-start.7 = (bf16[64,112,128]{2,1,0:T(8,128)(2,1)S(1)}, bf16[64,112,128]{2,1,0:T(8,128)(2,1)S(1)}, u32[]{:S(2)}, u32[]{:S(2)}) collective-permute-start(bf16[64,112,128]{2,1,0:T(8,128)(2,1)S(1)} %get-tuple-element.50), channel_id=1, source_target_pairs={{0,16},{16,0},{1,17},{17,1},{2,18},{18,2},{3,19},{19,3},{4,20},{20... | collective-permute-start | bytes 5505032 | tf_op jit(solution)/shard_map/ppermute | solution.py:40
  91.5 3.8 %collective-permute-start.6 = (bf16[256,512]{1,0:T(8,128)(2,1)S(1)}, bf16[256,512]{1,0:T(8,128)(2,1)S(1)}, u32[]{:S(2)}, u32[]{:S(2)}) collective-permute-start(bf16[256,512]{1,0:T(8,128)(2,1)S(1)} %get-tuple-element.47.dpre), channel_id=1, source_target_pairs={{0,16},{16,0},{1,17},{17,1},{2,18},{18,2},{3,19},{19,3},{4,20},{20... | collective-permute-start | bytes 786440 | tf_op jit(solution)/shard_map/ppermute | solution.py:40
  152.1 4.3 %collective-permute-start.8 = (bf16[2,112,128]{2,1,0:T(8,128)(2,1)S(1)}, bf16[2,112,128]{2,1,0:T(8,128)(2,1)S(1)}, u32[]{:S(2)}, u32[]{:S(2)}) collective-permute-start(bf16[2,112,128]{2,1,0:T(8,128)(2,1)S(1)} %get-tuple-element.76), channel_id=1, source_target_pairs={{0,1},{1,2},{2,3},{3,0},{4,5},{5,6},{6,7},{7,4},{8,9},{9,10},{10,1... | collective-permute-start | bytes 172040 | tf_op jit(solution)/shard_map/ppermute | solution.py:65
  152.9 3.5 %collective-permute-start.9 = (bf16[2,112,128]{2,1,0:T(8,128)(2,1)S(1)}, bf16[2,112,128]{2,1,0:T(8,128)(2,1)S(1)}, u32[]{:S(2)}, u32[]{:S(2)}) collective-permute-start(bf16[2,112,128]{2,1,0:T(8,128)(2,1)S(1)} %get-tuple-element.76), channel_id=1, source_target_pairs={{0,3},{1,0},{2,1},{3,2},{4,7},{5,4},{6,5},{7,6},{8,11},{9,8},{10,9... | collective-permute-start | bytes 172040 | tf_op jit(solution)/shard_map/ppermute | solution.py:65
  154.9 4.7 %collective-permute-start.10 = (bf16[2,112,128]{2,1,0:T(8,128)(2,1)S(1)}, bf16[2,112,128]{2,1,0:T(8,128)(2,1)S(1)}, u32[]{:S(2)}, u32[]{:S(2)}) collective-permute-start(bf16[2,112,128]{2,1,0:T(8,128)(2,1)S(1)} %get-tuple-element.76), channel_id=1, source_target_pairs={{0,2},{1,3},{2,0},{3,1},{4,6},{5,7},{6,4},{7,5},{8,10},{9,11},{10,... | collective-permute-start | bytes 172040 | tf_op jit(solution)/shard_map/ppermute | solution.py:65
  159.7 6.1 %collective-permute-start.14 = (bf16[4,112,128]{2,1,0:T(8,128)(2,1)S(1)}, bf16[4,112,128]{2,1,0:T(8,128)(2,1)S(1)}, u32[]{:S(2)}, u32[]{:S(2)}) collective-permute-start(bf16[4,112,128]{2,1,0:T(8,128)(2,1)S(1)} %get-tuple-element.73), channel_id=1, source_target_pairs={{0,32},{32,64},{64,96},{96,0},{1,33},{33,65},{65,97},{97,1},{2,34}... | collective-permute-start | bytes 344072 | tf_op jit(solution)/shard_map/ppermute | solution.py:59
  160.3 6.7 %collective-permute-start.15 = (bf16[4,112,128]{2,1,0:T(8,128)(2,1)S(1)}, bf16[4,112,128]{2,1,0:T(8,128)(2,1)S(1)}, u32[]{:S(2)}, u32[]{:S(2)}) collective-permute-start(bf16[4,112,128]{2,1,0:T(8,128)(2,1)S(1)} %get-tuple-element.73), channel_id=1, source_target_pairs={{0,96},{32,0},{64,32},{96,64},{1,97},{33,1},{65,33},{97,65},{2,98}... | collective-permute-start | bytes 344072 | tf_op jit(solution)/shard_map/ppermute | solution.py:59
  162.4 5.3 %collective-permute-start.16 = (bf16[4,112,128]{2,1,0:T(8,128)(2,1)S(1)}, bf16[4,112,128]{2,1,0:T(8,128)(2,1)S(1)}, u32[]{:S(2)}, u32[]{:S(2)}) collective-permute-start(bf16[4,112,128]{2,1,0:T(8,128)(2,1)S(1)} %get-tuple-element.73), channel_id=1, source_target_pairs={{0,64},{32,96},{64,0},{96,32},{1,65},{33,97},{65,1},{97,33},{2,66}... | collective-permute-start | bytes 344072 | tf_op jit(solution)/shard_map/ppermute | solution.py:59
  163.1 4.9 %collective-permute-start.11 = (bf16[4,112,128]{2,1,0:T(8,128)(2,1)S(1)}, bf16[4,112,128]{2,1,0:T(8,128)(2,1)S(1)}, u32[]{:S(2)}, u32[]{:S(2)}) collective-permute-start(bf16[4,112,128]{2,1,0:T(8,128)(2,1)S(1)} %get-tuple-element.72), channel_id=1, source_target_pairs={{0,4},{1,5},{2,6},{3,7},{4,8},{5,9},{6,10},{7,11},{8,12},{9,13},{1... | collective-permute-start | bytes 344072 | tf_op jit(solution)/shard_map/ppermute | solution.py:65
  163.8 4.2 %collective-permute-start.12 = (bf16[4,112,128]{2,1,0:T(8,128)(2,1)S(1)}, bf16[4,112,128]{2,1,0:T(8,128)(2,1)S(1)}, u32[]{:S(2)}, u32[]{:S(2)}) collective-permute-start(bf16[4,112,128]{2,1,0:T(8,128)(2,1)S(1)} %get-tuple-element.72), channel_id=1, source_target_pairs={{0,12},{1,13},{2,14},{3,15},{4,0},{5,1},{6,2},{7,3},{8,4},{9,5},{1... | collective-permute-start | bytes 344072 | tf_op jit(solution)/shard_map/ppermute | solution.py:65
  165.7 5.2 %collective-permute-start.13 = (bf16[4,112,128]{2,1,0:T(8,128)(2,1)S(1)}, bf16[4,112,128]{2,1,0:T(8,128)(2,1)S(1)}, u32[]{:S(2)}, u32[]{:S(2)}) collective-permute-start(bf16[4,112,128]{2,1,0:T(8,128)(2,1)S(1)} %get-tuple-element.72), channel_id=1, source_target_pairs={{0,8},{1,9},{2,10},{3,11},{4,12},{5,13},{6,14},{7,15},{8,0},{9,1},... | collective-permute-start | bytes 344072 | tf_op jit(solution)/shard_map/ppermute | solution.py:65
  171.0 10.2 %collective-permute-start.20 = (bf16[4,4,112,128]{3,2,1,0:T(8,128)(2,1)S(1)}, bf16[4,4,112,128]{3,2,1,0:T(8,128)(2,1)S(1)}, u32[]{:S(2)}, u32[]{:S(2)}) collective-permute-start(bf16[4,4,112,128]{3,2,1,0:T(8,128)(2,1)S(1)} %pad_maximum_fusion.3), channel_id=1, source_target_pairs={{0,4},{1,5},{2,6},{3,7},{4,8},{5,9},{6,10},{7,11},{8,12},{9,13},{1... | collective-permute-start | bytes 1376264 | tf_op jit(solution)/shard_map/ppermute | solution.py:65
  171.2 15.2 %collective-permute-start.21 = (bf16[4,4,112,128]{3,2,1,0:T(8,128)(2,1)S(1)}, bf16[4,4,112,128]{3,2,1,0:T(8,128)(2,1)S(1)}, u32[]{:S(2)}, u32[]{:S(2)}) collective-permute-start(bf16[4,4,112,128]{3,2,1,0:T(8,128)(2,1)S(1)} %pad_maximum_fusion.3), channel_id=1, source_target_pairs={{0,12},{1,13},{2,14},{3,15},{4,0},{5,1},{6,2},{7,3},{8,4},{9,5},{1... | collective-permute-start | bytes 1376264 | tf_op jit(solution)/shard_map/ppermute | solution.py:65
  173.8 25.7 %collective-permute-start.22 = (bf16[4,4,112,128]{3,2,1,0:T(8,128)(2,1)S(1)}, bf16[4,4,112,128]{3,2,1,0:T(8,128)(2,1)S(1)}, u32[]{:S(2)}, u32[]{:S(2)}) collective-permute-start(bf16[4,4,112,128]{3,2,1,0:T(8,128)(2,1)S(1)} %pad_maximum_fusion.3), channel_id=1, source_target_pairs={{0,8},{1,9},{2,10},{3,11},{4,12},{5,13},{6,14},{7,15},{8,0},{9,1},... | collective-permute-start | bytes 1376264 | tf_op jit(solution)/shard_map/ppermute | solution.py:65
  174.0 25.7 %collective-permute-start.17 = (bf16[4,4,112,128]{3,2,1,0:T(8,128)(2,1)S(1)}, bf16[4,4,112,128]{3,2,1,0:T(8,128)(2,1)S(1)}, u32[]{:S(2)}, u32[]{:S(2)}) collective-permute-start(bf16[4,4,112,128]{3,2,1,0:T(8,128)(2,1)S(1)} %pad_maximum_fusion.2), channel_id=1, source_target_pairs={{0,32},{32,64},{64,96},{96,0},{1,33},{33,65},{65,97},{97,1},{2,34}... | collective-permute-start | bytes 1376264 | tf_op jit(solution)/shard_map/ppermute | solution.py:59
  174.9 24.9 %collective-permute-start.18 = (bf16[4,4,112,128]{3,2,1,0:T(8,128)(2,1)S(1)}, bf16[4,4,112,128]{3,2,1,0:T(8,128)(2,1)S(1)}, u32[]{:S(2)}, u32[]{:S(2)}) collective-permute-start(bf16[4,4,112,128]{3,2,1,0:T(8,128)(2,1)S(1)} %pad_maximum_fusion.2), channel_id=1, source_target_pairs={{0,96},{32,0},{64,32},{96,64},{1,97},{33,1},{65,33},{97,65},{2,98}... | collective-permute-start | bytes 1376264 | tf_op jit(solution)/shard_map/ppermute | solution.py:59
  181.2 18.5 %collective-permute-start.19 = (bf16[4,4,112,128]{3,2,1,0:T(8,128)(2,1)S(1)}, bf16[4,4,112,128]{3,2,1,0:T(8,128)(2,1)S(1)}, u32[]{:S(2)}, u32[]{:S(2)}) collective-permute-start(bf16[4,4,112,128]{3,2,1,0:T(8,128)(2,1)S(1)} %pad_maximum_fusion.2), channel_id=1, source_target_pairs={{0,64},{32,96},{64,0},{96,32},{1,65},{33,97},{65,1},{97,33},{2,66}... | collective-permute-start | bytes 1376264 | tf_op jit(solution)/shard_map/ppermute | solution.py:59
  186.4 14.8 %collective-permute-start.23 = (f32[8,128]{1,0:T(8,128)S(1)}, f32[8,128]{1,0:T(8,128)S(1)}, u32[]{:S(2)}, u32[]{:S(2)}) collective-permute-start(f32[8,128]{1,0:T(8,128)S(1)} %get-tuple-element.55.refs_0_), channel_id=1, source_target_pairs={{0,16},{16,0},{1,17},{17,1},{2,18},{18,2},{3,19},{19,3},{4,20},{20... | collective-permute-start | bytes 12296 | tf_op jit(solution)/shard_map/ppermute | solution.py:40
  201.2 15.5 %collective-permute-start.25 = (bf16[4,4,4,112,128]{4,3,2,1,0:T(8,128)(2,1)}, bf16[4,4,4,112,128]{4,3,2,1,0:T(8,128)(2,1)}, u32[]{:S(2)}, u32[]{:S(2)}) collective-permute-start(bf16[4,4,4,112,128]{4,3,2,1,0:T(8,128)(2,1)} %pad_maximum_fusion.chunks), channel_id=1, source_target_pairs={{0,16},{16,0},{1,17},{17,1},{2,18},{18,2},{3,19},{19,3},{4,20},{20... | collective-permute-start | bytes 5505032 | tf_op jit(solution)/shard_map/ppermute | solution.py:40
  208.3 13.0 %collective-permute-start.24 = (bf16[4,4,4,112,128]{4,3,2,1,0:T(8,128)(2,1)S(1)}, bf16[4,4,4,112,128]{4,3,2,1,0:T(8,128)(2,1)}, u32[]{:S(2)}, u32[]{:S(2)}) collective-permute-start(bf16[4,4,4,112,128]{4,3,2,1,0:T(8,128)(2,1)S(1)} %pad_maximum_fusion.1.chunks), channel_id=1, source_target_pairs={{0,16},{16,0},{1,17},{17,1},{2,18},{18,2},{3,19},{19,3},{4,20},{20... | collective-permute-start | bytes 5505032 | tf_op jit(solution)/shard_map/ppermute | solution.py:40

commit v8 on v7

--- a/solution.py
+++ b/solution.py
@@ -432,49 +432,35 @@
     bias[...] = t[:nbias] + t[nbias:]
 
 
-def unpack_kernel(sizes, nbiases, inner_x, info, chunks, *refs):
-    in_size, conv_size, nb, ny, nz, inner = sizes
-    core, peer, inner_at, z_at = info[0], info[2], info[3], info[4]
+def unpack_kernel(sizes, nbiases, info, left, right, *refs):
+    in_size, conv_size, nb, nz = sizes
+    z_at = info[1]
     if nbiases:
         bias, bias_got = refs[:2]
         w_in, w_conv, b_in, b_conv = refs[-4:]
     else:
         w_in, w_conv = refs[-2:]
     nh = nb // 2
-    half = nh * LANES
-    ch = nh // 2 * conv_size
-    for a, shift_a in enumerate(shifts(inner)):
-        i = lax.rem(inner_at + inner - shift_a, inner)
-        for b, shift_b in enumerate(shifts(nz)):
-            z = lax.rem(z_at + nz - shift_b, nz)
-            value = chunks[0, a, b].astype(F32)
-            rows = pl.ds(pl.multiple_of(z * in_size, in_size), in_size)
-            left = jnp.concatenate(
-                [value[j * in_size : (j + 1) * in_size] for j in range(nh)], axis=1
-            )
-            crow = pl.ds(pl.multiple_of(z * conv_size, conv_size), conv_size)
-            if inner_x:
-                w_in[0, i, 0, rows, :] = left
-            else:
-                w_in[0, 0, i, rows, :] = left
+    for b, shift in enumerate(shifts(nz)):
+        z = lax.rem(z_at + nz - shift, nz)
+        rows = pl.ds(pl.multiple_of(z * in_size, in_size), in_size)
+        conv_rows = pl.ds(pl.multiple_of(z * conv_size, conv_size), conv_size)
+        for side, ref in enumerate((left, right)):
+            value = ref[0, 0, 0, b].astype(F32)
+            for j in range(nh):
+                col = (side * nh + j) * LANES
+                w_in[0, 0, rows, col : col + LANES] = value[j * in_size : (j + 1) * in_size]
             for layer in range(NL):
-                at = nh * in_size + layer * ch
-                part = jnp.concatenate(
-                    [
-                        value[at + j * conv_size : at + (j + 1) * conv_size]
-                        for j in range(nh // 2)
-                    ],
-                    axis=1,
-                )
-                if inner_x:
-                    w_conv[layer, i, 0, crow, :] = part
-                else:
-                    w_conv[layer, 0, i, crow, :] = part
+                for j in range(nh // 2):
+                    at = nh * in_size + (layer * (nh // 2) + j) * conv_size
+                    col = (side * (nh // 2) + j) * LANES
+                    part = value[at : at + conv_size]
+                    w_conv[layer, 0, conv_rows, col : col + LANES] = part
     if nbiases:
 
         @pl.when(pl.program_id(0) == 0)
         def _():
-            first = info[5] == 0
+            first = info[0] == 1
             n = NL + 1
             parts = []
             for side in range(2):
@@ -621,60 +607,60 @@
     plane_a, plane_b = lax.optimization_barrier(
         (along(both[:, 0], "y", ny), along(both[:, 1], "x", nx))
     )
-    full_a, full_b = along(plane_a, "x", nx), along(plane_b, "y", ny)
-    bias_got = swap_core(bias)
-    full_a, full_b, bias_got = lax.optimization_barrier((full_a, full_b, bias_got))
-    peer = lax.axis_index("x") * segments + segment
-    place = jnp.stack([lax.axis_index("x"), segment // nz, segment % nz])
-
-    def unpack(chunks, side, inner_x, owner, biases, earlier):
+    full = jnp.stack([along(plane_a, "x", nx), along(plane_b, "y", ny)])
+    full, bias = lax.optimization_barrier((full, bias))
+    places = nx * ny
+
+    def slots(at, count):
+        steps_back = lax.rem(at + count - jnp.arange(count), count)
+        return steps_back ^ (steps_back >> 1)
+
+    x_slots = slots(lax.axis_index("x"), nx)
+    y_slots = slots(segment // nz, ny)
+    tables = [jnp.repeat(x_slots, ny), jnp.tile(y_slots, nx)]
+
+    def unpack(chunks, owner, biases, earlier):
         spare = [sds((ch,), F32), sds((NL, ch), F32)] if biases else []
-        outer, inner = (ny, nx) if inner_x else (nx, ny)
-        outer_at, inner_at = (place[1], place[0]) if inner_x else (place[0], place[1])
-        table = [lax.rem(outer_at + outer - k, outer) for k in shifts(outer)]
-        head = [owner, outer_at, peer, inner_at, place[2], core]
-        info = jnp.stack(head + table).astype(jnp.int32)
-        if inner_x:
-            in_map = lambda i, at: (at[0], 0, at[6 + i], 0, side)
-            conv_map = lambda i, at: (0, 0, at[6 + i], 0, 2 * at[0] + side)
-            xs, ys = nx, 1
-        else:
-            in_map = lambda i, at: (at[0], at[6 + i], 0, 0, side)
-            conv_map = lambda i, at: (0, at[6 + i], 0, 0, 2 * at[0] + side)
-            xs, ys = 1, ny
+        info = jnp.concatenate([jnp.stack([owner, segment % nz])] + tables).astype(jnp.int32)
+        block = (1, 1, 1, nz, part, LANES)
         return pl.pallas_call(
-            functools.partial(
-                unpack_kernel, (in_size, conv_size, nb, ny, nz, inner), len(biases), inner_x
-            ),
+            functools.partial(unpack_kernel, (in_size, conv_size, nb, nz), len(biases)),
             grid_spec=pltpu.PrefetchScalarGridSpec(
                 num_scalar_prefetch=1,
-                grid=(outer,),
+                grid=(places,),
                 in_specs=[
-                    pl.BlockSpec((1, inner, nz, part, LANES), lambda i, at: (i, 0, 0, 0, 0))
+                    pl.BlockSpec(
+                        block, lambda i, at: (0, at[2 + i], at[2 + places + i], 0, 0, 0)
+                    ),
+                    pl.BlockSpec(
+                        block, lambda i, at: (1, at[2 + places + i], at[2 + i], 0, 0, 0)
+                    ),
                 ]
                 + [pl.BlockSpec(b.shape, lambda i, at: (0, 0)) for b in biases]
                 + [hbm] * len(earlier),
                 out_specs=[
-                    pl.BlockSpec((1, xs, ys, nz * in_size, ch // 2), in_map),
-                    pl.BlockSpec((NL, xs, ys, nz * conv_size, ch // 4), conv_map),
+                    pl.BlockSpec((1, 1, nz * in_size, ch), lambda i, at: (at[0], i, 0, 0)),
+                    pl.BlockSpec(
+                        (NL, 1, nz * conv_size, ch // 2), lambda i, at: (0, i, 0, at[0])
+                    ),
                 ]
                 + [pl.BlockSpec(b.shape, lambda i, at, n=len(b.shape): (0,) * n) for b in spare],
             ),
             out_shape=[
-                sds((2, nx, ny, nz * in_size, ch), F32),
-                sds((NL, nx, ny, nz * conv_size, ch), F32),
+                sds((2, places, nz * in_size, ch), F32),
+                sds((NL, places, nz * conv_size, ch), F32),
             ]
             + spare,
-            input_output_aliases={2 + len(biases) + n: n for n in range(len(earlier))},
+            input_output_aliases={3 + len(biases) + n: n for n in range(len(earlier))},
             compiler_params=small_params,
-            cost_estimate=pl.CostEstimate(flops=0, bytes_accessed=6 * 2**20, transcendentals=0),
-        )(info, chunks, *biases, *earlier)
-
-    got_a, got_b = swap_core(full_a), swap_core(full_b)
-    partial = unpack(full_a, 0, False, core, [], [])
-    partial = unpack(full_b, 1, True, core, [], partial)
-    partial = unpack(got_a, 0, False, 1 - core, [], partial)
-    g_in, g_conv, g_b_in, g_b_conv = unpack(got_b, 1, True, 1 - core, [bias, bias_got], partial)
+            cost_estimate=pl.CostEstimate(flops=0, bytes_accessed=12 * 2**20, transcendentals=0),
+        )(info, chunks, chunks, *biases, *earlier)
+
+    got = swap_core(full)
+    bias_got = swap_core(bias)
+    partial = unpack(full, core, [], [])
+    got, bias_got = lax.optimization_barrier((got, bias_got))
+    g_in, g_conv, g_b_in, g_b_conv = unpack(got, 1 - core, [bias, bias_got], partial)
     return (
         score[0, 0],
         g_in.reshape(features, ch),

time: 227 us -> 229 us (level)
  starting transfers between devices: 53.6 us -> 39.4 us
  waiting for transfers between devices: 21.1 us -> 27.3 us
  Pallas kernels: 43.9 us -> 49.9 us
  blocking collectives: 98.6 us -> 102 us
    ppermute x6, waiting for transfers between devices: 0.79 us -> 11.4 us  [spin(): return lax.ppermute(value, 'x', [(i, (i + steps) % n) for i in range(n)])]
    ppermute x9 -> x8, starting transfers between devices: 26.9 us -> 18.5 us  [swap_core(): return lax.ppermute(value, 'c', [(0, 1), (1, 0)])]
    ppermute x6, starting transfers between devices: 11.2 us -> 4.56 us  [spin(): return lax.ppermute(value, 'x', [(i, (i + steps) % n) for i in range(n)])]
    pallas_call x4 -> x2, Pallas kernels: 16.8 us -> 22.8 us  [unpack(): pl.pallas_call(functools.partial(unpack_kernel, (in_size, conv_size, nb,...]
    all_to_all x3, blocking collectives: 98.6 us -> 102 us  [exchange(): return lax.all_to_all(value, PEERS, 0, 0, tiled=True)]
    another operation x0 -> x3, other arithmetic: none -> 2.56 us  [per_device(): full = jnp.stack([along(plane_a, 'x', nx), along(plane_b, 'y', ny)])]
    ppermute x2, waiting for transfers between devices: 3.46 us -> 0.92 us  [shift_segment(): lax.ppermute(value, 'tm', [(i, i + steps) for i in range(first, last)])]
    ppermute x9 -> x8, waiting for transfers between devices: 5.43 us -> 5.42 us  [swap_core(): return lax.ppermute(value, 'c', [(0, 1), (1, 0)])]
  transfers between devices with their start and end apart: 26 -> 25, of which waited for: 10 -> 12; matrix products, arithmetic and copies ran while one was open for 3% -> 3% of each run, Pallas kernels for 8% -> 8%
where the time goes in v8:
time: 229 us; the launch traced here: 228 us
  blocking collectives  102 us (45%)
  Pallas kernels  49.9 us (22%)
  starting transfers between devices  39.4 us (17%)
  waiting for transfers between devices  27.3 us (12%)
  matrix products  5.05 us (2%)
  other arithmetic  2.9 us (1%)
    all_to_all x3, blocking collectives, exchange(): return lax.all_to_all(value, PEERS, 0, 0, tiled=True)  102 us
    pallas_call x2, Pallas kernels, unpack(): pl.pallas_call(functools.partial(unpack_kernel, (in_size, conv_size, nb,...  22.8 us
    ppermute x8, starting transfers between devices, swap_core(): return lax.ppermute(value, 'c', [(0, 1), (1, 0)])  18.5 us
    pallas_call x1, Pallas kernels, per_device(): pl.pallas_call(functools.partial(step_kernel, dims), out_shape=[sds((8, L...  12.7 us
    ppermute x6, waiting for transfers between devices, spin(): return lax.ppermute(value, 'x', [(i, (i + steps) % n) for i in range(n)])  11.4 us
    ppermute x9, starting transfers between devices, spin(): return lax.ppermute(value, 'tm', pairs)  10.8 us
    ppermute x9, waiting for transfers between devices, spin(): return lax.ppermute(value, 'tm', pairs)  9.61 us
    pallas_call x3, Pallas kernels, call(): pl.pallas_call(kernel, out_shape=outs, in_specs=specs, out_specs=[pl.Bloc...  7.35 us
  transfers between devices with their start and end apart: 25, of which 12 were waited for; matrix products, arithmetic and copies ran while one was open for 3% of the time, Pallas kernels for 8%

profile of v8, /device:TPU:1, one launch (start us, length us, event | category | flops | bytes accessed | tf_op | source)
XLA Modules:
  0.0 228.0 jit_solution(11559952270216217644)
XLA Ops:
  0.6 1.5 collective-permute-start.4
  2.1 5.1 %fusion.6 = (bf16[256,512]{1,0:T(8,128)(2,1)S(1)}, f32[256,512]{1,0:T(8,128)}) fusion(f32[512]{0:T(512)} %param.7, bf16[4096,512]{1,0:T(8,128)(2,1)} %param.6, bf16[1,256,4096]{2,1,0:T(8,128)(2,1)} %param.5), kind=kOutput, calls=%fused_computation.27 | convolution fusion | flops 1074003968 | bytes 7079936 | tf_op jit(solution)/shard_map/dot_general | solution.py:492
  7.2 1.3 collective-permute-start.1
  8.5 4.3 %collective-permute-start = (bf16[32,512]{1,0:T(8,128)(2,1)S(1)}, bf16[32,512]{1,0:T(8,128)(2,1)S(1)}, u32[]{:S(2)}, u32[]{:S(2)}) collective-permute-start(bf16[32,512]{1,0:T(8,128)(2,1)S(1)} %get-tuple-element.64), channel_id=1, source_target_pairs={{0,1},{1,2},{2,3},{3,4},{4,5},{5,6},{6,7},{7,8},{8,9},{9,10},{10,1... | collective-permute-start | bytes 98312 | tf_op jit(solution)/shard_map/ppermute | solution.py:46
  12.8 0.9 collective-permute-done.before
  13.8 3.9 %shard_map.92 = (bf16[4,320,512]{2,1,0:T(8,128)(2,1)S(1)}, f32[3,320,512]{2,1,0:T(8,128)S(1)}, f32[64,48,128]{2,1,0:T(8,128)S(1)}, bf16[64,48,128]{2,1,0:T(8,128)(2,1)S(1)}, f32[8,512]{1,0:T(8,128)S(1)}) custom-call(s32[3]{0:T(128)S(1)} %pad_add_fusion.info, bf16[32,512]{1,0:T(8,128)(2,1)S(1)} %collective-permute-done.before, ...), custom_call_target="tpu_custom_call" | custom-call | tf_op jit(solution)/shard_map/pallas_call | solution.py:87
  17.7 1.0 collective-permute-start.2
  18.8 1.8 collective-permute-done.3.sib
  20.6 2.0 shard_map.93
  22.6 31.0 %all_to_all.15.arrived = bf16[64,64,128]{2,1,0:T(8,128)(2,1)S(1)} all-to-all(bf16[64,64,128]{2,1,0:T(8,128)(2,1)S(1)} %shard_map.93), channel_id=1, replica_groups=mesh['x'=4,'c'=2,'tm'=16] {'x','tm'}, dimensions={0} | all-to-all | bytes 2097152 | tf_op jit(solution)/shard_map/all_to_all | solution.py:80
  53.6 1.5 shard_map.94
  55.0 19.0 %all_to_all.16.half_cov = bf16[64,48,128]{2,1,0:T(8,128)(2,1)S(1)} all-to-all(bf16[64,48,128]{2,1,0:T(8,128)(2,1)S(1)} %get-tuple-element.39), channel_id=1, replica_groups=mesh['x'=4,'c'=2,'tm'=16] {'x','tm'}, dimensions={0} | all-to-all | bytes 1572864 | tf_op jit(solution)/shard_map/all_to_all | solution.py:80
  74.0 3.1 %collective-permute-start.5 = (bf16[64,48,128]{2,1,0:T(8,128)(2,1)S(1)}, bf16[64,48,128]{2,1,0:T(8,128)(2,1)S(1)}, u32[]{:S(2)}, u32[]{:S(2)}) collective-permute-start(bf16[64,48,128]{2,1,0:T(8,128)(2,1)S(1)} %all_to_all.16.half_cov), channel_id=1, source_target_pairs={{0,16},{16,0},{1,17},{17,1},{2,18},{18,2},{3,19},{19,3},{4,20},{20... | collective-permute-start | bytes 2359304 | tf_op jit(solution)/shard_map/ppermute | solution.py:40
  77.2 1.9 collective-permute-done.5.other_cov
  79.1 12.7 %shard_map.95 = (f32[8,128]{1,0:T(8,128)S(1)}, bf16[64,112,128]{2,1,0:T(8,128)(2,1)S(1)}, bf16[64,112,128]{2,1,0:T(8,128)(2,1)S(1)}, bf16[256,512]{1,0:T(8,128)(2,1)S(1)}) custom-call(s32[3]{0:T(128)S(1)} %pad_add_fusion.info, bf16[64,48,128]{2,1,0:T(8,128)(2,1)S(1)} %all_to_all.16.half_cov, bf16[64,48,128]{2,1,0:T(8,128)(2,1)S(1)} %collective-permute-done.5.other_cov, ...), custom_call_target="tpu_custom_call" | custom-call | tf_op jit(solution)/shard_map/pallas_call | solution.py:541
  91.8 0.4 collective-permute-start.7
  92.2 0.1 collective-permute-start.6
  92.4 2.0 shard_map.96.earlier
  94.4 1.7 collective-permute-done.6.dpre_got
  96.0 3.9 %shard_map.97 = bf16[64,240,128]{2,1,0:T(8,128)(2,1)S(1)} custom-call(s32[3]{0:T(128)S(1)} %pad_add_fusion.info, f32[2048,512]{1,0:T(8,128)S(1)} %shard_map.96.earlier, bf16[256,4096]{1,0:T(8,128)(2,1)} %collective-permute-done.4.left_got, bf16[256,512]{1,0:T(8,128)(2,1)S(1)} %collective-permute-done.6.dpre_got, ...), custom_call_target="tpu_custom_call" | custom-call | tf_op jit(solution)/shard_map/pallas_call | solution.py:584
  99.9 51.6 %all_to_all.17.arrived = bf16[64,240,128]{2,1,0:T(8,128)(2,1)S(1)} all-to-all(bf16[64,240,128]{2,1,0:T(8,128)(2,1)S(1)} %shard_map.97), channel_id=1, replica_groups=mesh['x'=4,'c'=2,'tm'=16] {'x','tm'}, dimensions={0} | all-to-all | bytes 7864320 | tf_op jit(solution)/shard_map/all_to_all | solution.py:80
  151.5 1.3 shard_map.98
  152.8 1.6 collective-permute-start.9
  154.4 2.1 collective-permute-start.10
  156.6 2.7 %collective-permute-done.8 = bf16[2,112,128]{2,1,0:T(8,128)(2,1)S(1)} collective-permute-done((bf16[2,112,128]{2,1,0:T(8,128)(2,1)S(1)}, bf16[2,112,128]{2,1,0:T(8,128)(2,1)S(1)}, u32[]{:S(2)}, u32[]{:S(2)}) %collective-permute-start.8) | collective-permute-done | bytes 57376 | tf_op jit(solution)/shard_map/ppermute | solution.py:65
  159.4 1.1 collective-permute-start.13
  160.5 3.0 %collective-permute-start.12 = (bf16[4,112,128]{2,1,0:T(8,128)(2,1)S(1)}, bf16[4,112,128]{2,1,0:T(8,128)(2,1)S(1)}, u32[]{:S(2)}, u32[]{:S(2)}) collective-permute-start(bf16[4,112,128]{2,1,0:T(8,128)(2,1)S(1)} %get-tuple-element.66), channel_id=1, source_target_pairs={{0,12},{1,13},{2,14},{3,15},{4,0},{5,1},{6,2},{7,3},{8,4},{9,5},{1... | collective-permute-start | bytes 344072 | tf_op jit(solution)/shard_map/ppermute | solution.py:65
  163.5 1.5 collective-permute-start.16
  165.0 1.2 collective-permute-start.15
  166.2 0.2 collective-permute-start.14
  166.5 3.2 %collective-permute-done.11 = bf16[4,112,128]{2,1,0:T(8,128)(2,1)S(1)} collective-permute-done((bf16[4,112,128]{2,1,0:T(8,128)(2,1)S(1)}, bf16[4,112,128]{2,1,0:T(8,128)(2,1)S(1)}, u32[]{:S(2)}, u32[]{:S(2)}) %collective-permute-start.11) | collective-permute-done | bytes 114720 | tf_op jit(solution)/shard_map/ppermute | solution.py:65
  169.8 1.6 collective-permute-done.14
  171.5 1.2 collective-permute-start.18
  172.7 0.3 collective-permute-start.17
  173.1 2.0 collective-permute-start.22
  175.1 0.9 collective-permute-start.21
  176.0 4.5 %collective-permute-done.19 = bf16[4,4,112,128]{3,2,1,0:T(8,128)(2,1)S(1)} collective-permute-done((bf16[4,4,112,128]{3,2,1,0:T(8,128)(2,1)S(1)}, bf16[4,4,112,128]{3,2,1,0:T(8,128)(2,1)S(1)}, u32[]{:S(2)}, u32[]{:S(2)}) %collective-permute-start.19) | collective-permute-done | bytes 458784 | tf_op jit(solution)/shard_map/ppermute | solution.py:59
  180.5 2.7 %collective-permute-done.18 = bf16[4,4,112,128]{3,2,1,0:T(8,128)(2,1)S(1)} collective-permute-done((bf16[4,4,112,128]{3,2,1,0:T(8,128)(2,1)S(1)}, bf16[4,4,112,128]{3,2,1,0:T(8,128)(2,1)S(1)}, u32[]{:S(2)}, u32[]{:S(2)}) %collective-permute-start.18) | collective-permute-done | bytes 458784 | tf_op jit(solution)/shard_map/ppermute | solution.py:59
  183.2 2.6 %collective-permute-done.17 = bf16[4,4,112,128]{3,2,1,0:T(8,128)(2,1)S(1)} collective-permute-done((bf16[4,4,112,128]{3,2,1,0:T(8,128)(2,1)S(1)}, bf16[4,4,112,128]{3,2,1,0:T(8,128)(2,1)S(1)}, u32[]{:S(2)}, u32[]{:S(2)}) %collective-permute-start.17) | collective-permute-done | bytes 458784 | tf_op jit(solution)/shard_map/ppermute | solution.py:59
  185.8 0.2 maximum_bitcast_fusion
  186.0 2.1 collective-permute-done.21
  188.1 1.6 collective-permute-done.20
  189.7 0.2 maximum_bitcast_fusion.1
  189.9 2.1 pad_maximum_fusion.left.right
  192.0 12.2 %collective-permute-start.23 = (bf16[2,4,4,4,112,128]{5,4,3,2,1,0:T(8,128)(2,1)}, bf16[2,4,4,4,112,128]{5,4,3,2,1,0:T(8,128)(2,1)}, u32[]{:S(2)}, u32[]{:S(2)}) collective-permute-start(bf16[2,4,4,4,112,128]{5,4,3,2,1,0:T(8,128)(2,1)} %pad_maximum_fusion.left.right), channel_id=1, source_target_pairs={{0,16},{16,0},{1,17},{17,1},{2,18},{18,2},{3,19},{19,3},{4,20},{20... | collective-permute-start | bytes 11010056 | tf_op jit(solution)/shard_map/ppermute | solution.py:40
  204.6 0.5 slice.17
  205.1 11.4 %shard_map.99 = (f32[2,16,128,512]{3,2,1,0:T(8,128)}, f32[3,16,64,512]{3,2,1,0:T(8,128)}) custom-call(s32[34]{0:T(128)S(1)} %get-tuple-element.71.info, bf16[2,4,4,4,112,128]{5,4,3,2,1,0:T(8,128)(2,1)} %pad_maximum_fusion.left.right, bf16[2,4,4,4,112,128]{5,4,3,2,1,0:T(8,128)(2,1)} %pad_maximum_fusion.left.right), custom_call_target="tpu_custom_call" | custom-call | bytes 12582912 | tf_op jit(solution)/shard_map/pallas_call | solution.py:626
  216.4 11.4 %shard_map.100 = (f32[2,16,128,512]{3,2,1,0:T(8,128)}, f32[3,16,64,512]{3,2,1,0:T(8,128)}, f32[512]{0:T(512)}, f32[3,512]{1,0:T(4,128)}) custom-call(s32[34]{0:T(128)S(1)} %get-tuple-element.72.info, bf16[2,4,4,4,112,128]{5,4,3,2,1,0:T(8,128)(2,1)} %collective-permute-done.23.left.right, ...), custom_call_target="tpu_custom_call", output_to_operand_aliasing={{0}: (5, {}), {1}: (6, {})} | custom-call | bytes 12582912 | tf_op jit(solution)/shard_map/pallas_call | solution.py:626
  (41 shorter events, 0.9 us)
Async XLA Ops:
  0.6 13.1 %copy-start.3 = (f32[3,512]{1,0:T(4,128)S(1)}, f32[3,512]{1,0:T(4,128)}, u32[]{:S(2)}) copy-start(f32[3,512]{1,0:T(4,128)} %b.1) | copy-start | bytes 18436
  0.6 20.0 %collective-permute-start.4 = (bf16[256,4096]{1,0:T(8,128)(2,1)}, bf16[256,4096]{1,0:T(8,128)(2,1)}, u32[]{:S(2)}, u32[]{:S(2)}) collective-permute-start(bf16[256,4096]{1,0:T(8,128)(2,1)} %bitcast.53), channel_id=1, source_target_pairs={{0,16},{16,0},{1,17},{17,1},{2,18},{18,2},{3,19},{19,3},{4,20},{20... | collective-permute-start | bytes 6291464 | tf_op jit(solution)/shard_map/ppermute | solution.py:40
  2.1 11.6 %copy-start = (bf16[3,1024,512]{2,1,0:T(8,128)(2,1)S(1)}, bf16[3,1024,512]{2,1,0:T(8,128)(2,1)}, u32[]{:S(2)}) copy-start(bf16[3,1024,512]{2,1,0:T(8,128)(2,1)} %w_hbm.1) | copy-start | bytes 9437188
  7.2 5.6 %collective-permute-start.1 = (bf16[32,512]{1,0:T(8,128)(2,1)S(1)}, bf16[32,512]{1,0:T(8,128)(2,1)S(1)}, u32[]{:S(2)}, u32[]{:S(2)}) collective-permute-start(bf16[32,512]{1,0:T(8,128)(2,1)S(1)} %get-tuple-element.63), channel_id=1, source_target_pairs={{1,0},{2,1},{3,2},{4,3},{5,4},{6,5},{7,6},{8,7},{9,8},{10,9},{11,1... | collective-permute-start | bytes 98312 | tf_op jit(solution)/shard_map/ppermute | solution.py:46
  8.5 5.3 %collective-permute-start = (bf16[32,512]{1,0:T(8,128)(2,1)S(1)}, bf16[32,512]{1,0:T(8,128)(2,1)S(1)}, u32[]{:S(2)}, u32[]{:S(2)}) collective-permute-start(bf16[32,512]{1,0:T(8,128)(2,1)S(1)} %get-tuple-element.64), channel_id=1, source_target_pairs={{0,1},{1,2},{2,3},{3,4},{4,5},{5,6},{6,7},{7,8},{8,9},{9,10},{10,1... | collective-permute-start | bytes 98312 | tf_op jit(solution)/shard_map/ppermute | solution.py:46
  17.7 2.9 %collective-permute-start.2 = (bf16[64,48,128]{2,1,0:T(8,128)(2,1)S(1)}, bf16[64,48,128]{2,1,0:T(8,128)(2,1)S(1)}, u32[]{:S(2)}, u32[]{:S(2)}) collective-permute-start(bf16[64,48,128]{2,1,0:T(8,128)(2,1)S(1)} %get-tuple-element.35), channel_id=1, source_target_pairs={{0,16},{16,0},{1,17},{17,1},{2,18},{18,2},{3,19},{19,3},{4,20},{20... | collective-permute-start | bytes 2359304 | tf_op jit(solution)/shard_map/ppermute | solution.py:40
  18.7 1.9 collective-permute-start.3
  22.6 56.5 %copy-start.2 = (f32[256,512]{1,0:T(8,128)S(1)}, f32[256,512]{1,0:T(8,128)}, u32[]{:S(2)}) copy-start(f32[256,512]{1,0:T(8,128)} %get-tuple-element.74.sq0_hbm) | copy-start | bytes 1572868
  74.0 5.1 %collective-permute-start.5 = (bf16[64,48,128]{2,1,0:T(8,128)(2,1)S(1)}, bf16[64,48,128]{2,1,0:T(8,128)(2,1)S(1)}, u32[]{:S(2)}, u32[]{:S(2)}) collective-permute-start(bf16[64,48,128]{2,1,0:T(8,128)(2,1)S(1)} %all_to_all.16.half_cov), channel_id=1, source_target_pairs={{0,16},{16,0},{1,17},{17,1},{2,18},{18,2},{3,19},{19,3},{4,20},{20... | collective-permute-start | bytes 2359304 | tf_op jit(solution)/shard_map/ppermute | solution.py:40
  79.1 13.3 %copy-start.1 = (bf16[1,256,4096]{2,1,0:T(8,128)(2,1)S(1)}, bf16[1,256,4096]{2,1,0:T(8,128)(2,1)}, u32[]{:S(2)}) copy-start(bf16[1,256,4096]{2,1,0:T(8,128)(2,1)} %param.5) | copy-start | bytes 6291460
  91.8 4.2 %collective-permute-start.7 = (bf16[64,112,128]{2,1,0:T(8,128)(2,1)S(1)}, bf16[64,112,128]{2,1,0:T(8,128)(2,1)S(1)}, u32[]{:S(2)}, u32[]{:S(2)}) collective-permute-start(bf16[64,112,128]{2,1,0:T(8,128)(2,1)S(1)} %get-tuple-element.47), channel_id=1, source_target_pairs={{0,16},{16,0},{1,17},{17,1},{2,18},{18,2},{3,19},{19,3},{4,20},{20... | collective-permute-start | bytes 5505032 | tf_op jit(solution)/shard_map/ppermute | solution.py:40
  92.2 3.8 %collective-permute-start.6 = (bf16[256,512]{1,0:T(8,128)(2,1)S(1)}, bf16[256,512]{1,0:T(8,128)(2,1)S(1)}, u32[]{:S(2)}, u32[]{:S(2)}) collective-permute-start(bf16[256,512]{1,0:T(8,128)(2,1)S(1)} %get-tuple-element.44.dpre), channel_id=1, source_target_pairs={{0,16},{16,0},{1,17},{17,1},{2,18},{18,2},{3,19},{19,3},{4,20},{20... | collective-permute-start | bytes 786440 | tf_op jit(solution)/shard_map/ppermute | solution.py:40
  152.8 3.8 %collective-permute-start.9 = (bf16[2,112,128]{2,1,0:T(8,128)(2,1)S(1)}, bf16[2,112,128]{2,1,0:T(8,128)(2,1)S(1)}, u32[]{:S(2)}, u32[]{:S(2)}) collective-permute-start(bf16[2,112,128]{2,1,0:T(8,128)(2,1)S(1)} %get-tuple-element.70), channel_id=1, source_target_pairs={{0,3},{1,0},{2,1},{3,2},{4,7},{5,4},{6,5},{7,6},{8,11},{9,8},{10,9... | collective-permute-start | bytes 172040 | tf_op jit(solution)/shard_map/ppermute | solution.py:65
  154.4 4.9 %collective-permute-start.8 = (bf16[2,112,128]{2,1,0:T(8,128)(2,1)S(1)}, bf16[2,112,128]{2,1,0:T(8,128)(2,1)S(1)}, u32[]{:S(2)}, u32[]{:S(2)}) collective-permute-start(bf16[2,112,128]{2,1,0:T(8,128)(2,1)S(1)} %get-tuple-element.70), channel_id=1, source_target_pairs={{0,1},{1,2},{2,3},{3,0},{4,5},{5,6},{6,7},{7,4},{8,9},{9,10},{10,1... | collective-permute-start | bytes 172040 | tf_op jit(solution)/shard_map/ppermute | solution.py:65
  154.4 4.9 %collective-permute-start.10 = (bf16[2,112,128]{2,1,0:T(8,128)(2,1)S(1)}, bf16[2,112,128]{2,1,0:T(8,128)(2,1)S(1)}, u32[]{:S(2)}, u32[]{:S(2)}) collective-permute-start(bf16[2,112,128]{2,1,0:T(8,128)(2,1)S(1)} %get-tuple-element.70), channel_id=1, source_target_pairs={{0,2},{1,3},{2,0},{3,1},{4,6},{5,7},{6,4},{7,5},{8,10},{9,11},{10,... | collective-permute-start | bytes 172040 | tf_op jit(solution)/shard_map/ppermute | solution.py:65
  159.4 6.8 %collective-permute-start.13 = (bf16[4,112,128]{2,1,0:T(8,128)(2,1)S(1)}, bf16[4,112,128]{2,1,0:T(8,128)(2,1)S(1)}, u32[]{:S(2)}, u32[]{:S(2)}) collective-permute-start(bf16[4,112,128]{2,1,0:T(8,128)(2,1)S(1)} %get-tuple-element.66), channel_id=1, source_target_pairs={{0,8},{1,9},{2,10},{3,11},{4,12},{5,13},{6,14},{7,15},{8,0},{9,1},... | collective-permute-start | bytes 344072 | tf_op jit(solution)/shard_map/ppermute | solution.py:65
  160.5 6.0 %collective-permute-start.12 = (bf16[4,112,128]{2,1,0:T(8,128)(2,1)S(1)}, bf16[4,112,128]{2,1,0:T(8,128)(2,1)S(1)}, u32[]{:S(2)}, u32[]{:S(2)}) collective-permute-start(bf16[4,112,128]{2,1,0:T(8,128)(2,1)S(1)} %get-tuple-element.66), channel_id=1, source_target_pairs={{0,12},{1,13},{2,14},{3,15},{4,0},{5,1},{6,2},{7,3},{8,4},{9,5},{1... | collective-permute-start | bytes 344072 | tf_op jit(solution)/shard_map/ppermute | solution.py:65
  163.5 6.2 %collective-permute-start.11 = (bf16[4,112,128]{2,1,0:T(8,128)(2,1)S(1)}, bf16[4,112,128]{2,1,0:T(8,128)(2,1)S(1)}, u32[]{:S(2)}, u32[]{:S(2)}) collective-permute-start(bf16[4,112,128]{2,1,0:T(8,128)(2,1)S(1)} %get-tuple-element.66), channel_id=1, source_target_pairs={{0,4},{1,5},{2,6},{3,7},{4,8},{5,9},{6,10},{7,11},{8,12},{9,13},{1... | collective-permute-start | bytes 344072 | tf_op jit(solution)/shard_map/ppermute | solution.py:65
  163.5 6.3 %collective-permute-start.16 = (bf16[4,112,128]{2,1,0:T(8,128)(2,1)S(1)}, bf16[4,112,128]{2,1,0:T(8,128)(2,1)S(1)}, u32[]{:S(2)}, u32[]{:S(2)}) collective-permute-start(bf16[4,112,128]{2,1,0:T(8,128)(2,1)S(1)} %get-tuple-element.67), channel_id=1, source_target_pairs={{0,64},{32,96},{64,0},{96,32},{1,65},{33,97},{65,1},{97,33},{2,66}... | collective-permute-start | bytes 344072 | tf_op jit(solution)/shard_map/ppermute | solution.py:59
  165.0 4.8 %collective-permute-start.15 = (bf16[4,112,128]{2,1,0:T(8,128)(2,1)S(1)}, bf16[4,112,128]{2,1,0:T(8,128)(2,1)S(1)}, u32[]{:S(2)}, u32[]{:S(2)}) collective-permute-start(bf16[4,112,128]{2,1,0:T(8,128)(2,1)S(1)} %get-tuple-element.67), channel_id=1, source_target_pairs={{0,96},{32,0},{64,32},{96,64},{1,97},{33,1},{65,33},{97,65},{2,98}... | collective-permute-start | bytes 344072 | tf_op jit(solution)/shard_map/ppermute | solution.py:59
  166.2 5.1 %collective-permute-start.14 = (bf16[4,112,128]{2,1,0:T(8,128)(2,1)S(1)}, bf16[4,112,128]{2,1,0:T(8,128)(2,1)S(1)}, u32[]{:S(2)}, u32[]{:S(2)}) collective-permute-start(bf16[4,112,128]{2,1,0:T(8,128)(2,1)S(1)} %get-tuple-element.67), channel_id=1, source_target_pairs={{0,32},{32,64},{64,96},{96,0},{1,33},{33,65},{65,97},{97,1},{2,34}... | collective-permute-start | bytes 344072 | tf_op jit(solution)/shard_map/ppermute | solution.py:59
  171.4 9.0 %collective-permute-start.19 = (bf16[4,4,112,128]{3,2,1,0:T(8,128)(2,1)S(1)}, bf16[4,4,112,128]{3,2,1,0:T(8,128)(2,1)S(1)}, u32[]{:S(2)}, u32[]{:S(2)}) collective-permute-start(bf16[4,4,112,128]{3,2,1,0:T(8,128)(2,1)S(1)} %pad_maximum_fusion.1), channel_id=1, source_target_pairs={{0,64},{32,96},{64,0},{96,32},{1,65},{33,97},{65,1},{97,33},{2,66}... | collective-permute-start | bytes 1376264 | tf_op jit(solution)/shard_map/ppermute | solution.py:59
  171.5 11.6 %collective-permute-start.18 = (bf16[4,4,112,128]{3,2,1,0:T(8,128)(2,1)S(1)}, bf16[4,4,112,128]{3,2,1,0:T(8,128)(2,1)S(1)}, u32[]{:S(2)}, u32[]{:S(2)}) collective-permute-start(bf16[4,4,112,128]{3,2,1,0:T(8,128)(2,1)S(1)} %pad_maximum_fusion.1), channel_id=1, source_target_pairs={{0,96},{32,0},{64,32},{96,64},{1,97},{33,1},{65,33},{97,65},{2,98}... | collective-permute-start | bytes 1376264 | tf_op jit(solution)/shard_map/ppermute | solution.py:59
  172.7 13.0 %collective-permute-start.17 = (bf16[4,4,112,128]{3,2,1,0:T(8,128)(2,1)S(1)}, bf16[4,4,112,128]{3,2,1,0:T(8,128)(2,1)S(1)}, u32[]{:S(2)}, u32[]{:S(2)}) collective-permute-start(bf16[4,4,112,128]{3,2,1,0:T(8,128)(2,1)S(1)} %pad_maximum_fusion.1), channel_id=1, source_target_pairs={{0,32},{32,64},{64,96},{96,0},{1,33},{33,65},{65,97},{97,1},{2,34}... | collective-permute-start | bytes 1376264 | tf_op jit(solution)/shard_map/ppermute | solution.py:59
  173.1 13.0 %collective-permute-start.22 = (bf16[4,4,112,128]{3,2,1,0:T(8,128)(2,1)S(1)}, bf16[4,4,112,128]{3,2,1,0:T(8,128)(2,1)S(1)}, u32[]{:S(2)}, u32[]{:S(2)}) collective-permute-start(bf16[4,4,112,128]{3,2,1,0:T(8,128)(2,1)S(1)} %pad_maximum_fusion.2), channel_id=1, source_target_pairs={{0,8},{1,9},{2,10},{3,11},{4,12},{5,13},{6,14},{7,15},{8,0},{9,1},... | collective-permute-start | bytes 1376264 | tf_op jit(solution)/shard_map/ppermute | solution.py:65
  175.1 13.0 %collective-permute-start.21 = (bf16[4,4,112,128]{3,2,1,0:T(8,128)(2,1)S(1)}, bf16[4,4,112,128]{3,2,1,0:T(8,128)(2,1)S(1)}, u32[]{:S(2)}, u32[]{:S(2)}) collective-permute-start(bf16[4,4,112,128]{3,2,1,0:T(8,128)(2,1)S(1)} %pad_maximum_fusion.2), channel_id=1, source_target_pairs={{0,12},{1,13},{2,14},{3,15},{4,0},{5,1},{6,2},{7,3},{8,4},{9,5},{1... | collective-permute-start | bytes 1376264 | tf_op jit(solution)/shard_map/ppermute | solution.py:65
  180.5 9.2 %collective-permute-start.20 = (bf16[4,4,112,128]{3,2,1,0:T(8,128)(2,1)S(1)}, bf16[4,4,112,128]{3,2,1,0:T(8,128)(2,1)S(1)}, u32[]{:S(2)}, u32[]{:S(2)}) collective-permute-start(bf16[4,4,112,128]{3,2,1,0:T(8,128)(2,1)S(1)} %pad_maximum_fusion.2), channel_id=1, source_target_pairs={{0,4},{1,5},{2,6},{3,7},{4,8},{5,9},{6,10},{7,11},{8,12},{9,13},{1... | collective-permute-start | bytes 1376264 | tf_op jit(solution)/shard_map/ppermute | solution.py:65
  192.0 24.4 %collective-permute-start.23 = (bf16[2,4,4,4,112,128]{5,4,3,2,1,0:T(8,128)(2,1)}, bf16[2,4,4,4,112,128]{5,4,3,2,1,0:T(8,128)(2,1)}, u32[]{:S(2)}, u32[]{:S(2)}) collective-permute-start(bf16[2,4,4,4,112,128]{5,4,3,2,1,0:T(8,128)(2,1)} %pad_maximum_fusion.left.right), channel_id=1, source_target_pairs={{0,16},{16,0},{1,17},{17,1},{2,18},{18,2},{3,19},{19,3},{4,20},{20... | collective-permute-start | bytes 11010056 | tf_op jit(solution)/shard_map/ppermute | solution.py:40
  204.4 12.0 %collective-permute-start.24 = (f32[8,128]{1,0:T(8,128)S(1)}, f32[8,128]{1,0:T(8,128)S(1)}, u32[]{:S(2)}, u32[]{:S(2)}) collective-permute-start(f32[8,128]{1,0:T(8,128)S(1)} %get-tuple-element.54.refs_0_), channel_id=1, source_target_pairs={{0,16},{16,0},{1,17},{17,1},{2,18},{18,2},{3,19},{19,3},{4,20},{20... | collective-permute-start | bytes 12296 | tf_op jit(solution)/shard_map/ppermute | solution.py:40

commit v9 on v8

--- a/solution.py
+++ b/solution.py
@@ -433,29 +433,31 @@
 
 
 def unpack_kernel(sizes, nbiases, info, left, right, *refs):
-    in_size, conv_size, nb, nz = sizes
-    z_at = info[1]
+    in_size, conv_size, nb, ny, nz = sizes
+    z_at, y_at = info[1], info[2]
     if nbiases:
         bias, bias_got = refs[:2]
         w_in, w_conv, b_in, b_conv = refs[-4:]
     else:
         w_in, w_conv = refs[-2:]
     nh = nb // 2
-    for b, shift in enumerate(shifts(nz)):
-        z = lax.rem(z_at + nz - shift, nz)
-        rows = pl.ds(pl.multiple_of(z * in_size, in_size), in_size)
-        conv_rows = pl.ds(pl.multiple_of(z * conv_size, conv_size), conv_size)
-        for side, ref in enumerate((left, right)):
-            value = ref[0, 0, 0, b].astype(F32)
-            for j in range(nh):
-                col = (side * nh + j) * LANES
-                w_in[0, 0, rows, col : col + LANES] = value[j * in_size : (j + 1) * in_size]
-            for layer in range(NL):
-                for j in range(nh // 2):
-                    at = nh * in_size + (layer * (nh // 2) + j) * conv_size
-                    col = (side * (nh // 2) + j) * LANES
-                    part = value[at : at + conv_size]
-                    w_conv[layer, 0, conv_rows, col : col + LANES] = part
+    for a, shift_a in enumerate(shifts(ny)):
+        y = lax.rem(y_at + ny - shift_a, ny)
+        for b, shift_b in enumerate(shifts(nz)):
+            z = lax.rem(z_at + nz - shift_b, nz)
+            rows = pl.ds(pl.multiple_of(z * in_size, in_size), in_size)
+            conv_rows = pl.ds(pl.multiple_of(z * conv_size, conv_size), conv_size)
+            for side, value in enumerate((left[0, 0, a, b], right[0, a, 0, b])):
+                value = value.astype(F32)
+                for j in range(nh):
+                    col = (side * nh + j) * LANES
+                    w_in[0, y, rows, col : col + LANES] = value[j * in_size : (j + 1) * in_size]
+                for layer in range(NL):
+                    for j in range(nh // 2):
+                        at = nh * in_size + (layer * (nh // 2) + j) * conv_size
+                        col = (side * (nh // 2) + j) * LANES
+                        part = value[at : at + conv_size]
+                        w_conv[layer, y, conv_rows, col : col + LANES] = part
     if nbiases:
 
         @pl.when(pl.program_id(0) == 0)
@@ -615,33 +617,32 @@
         steps_back = lax.rem(at + count - jnp.arange(count), count)
         return steps_back ^ (steps_back >> 1)
 
-    x_slots = slots(lax.axis_index("x"), nx)
-    y_slots = slots(segment // nz, ny)
-    tables = [jnp.repeat(x_slots, ny), jnp.tile(y_slots, nx)]
+    table = slots(lax.axis_index("x"), nx)
 
     def unpack(chunks, owner, biases, earlier):
         spare = [sds((ch,), F32), sds((NL, ch), F32)] if biases else []
-        info = jnp.concatenate([jnp.stack([owner, segment % nz])] + tables).astype(jnp.int32)
-        block = (1, 1, 1, nz, part, LANES)
+        info = jnp.concatenate(
+            [jnp.stack([owner, segment % nz, segment // nz]), table]
+        ).astype(jnp.int32)
         return pl.pallas_call(
-            functools.partial(unpack_kernel, (in_size, conv_size, nb, nz), len(biases)),
+            functools.partial(unpack_kernel, (in_size, conv_size, nb, ny, nz), len(biases)),
             grid_spec=pltpu.PrefetchScalarGridSpec(
                 num_scalar_prefetch=1,
-                grid=(places,),
+                grid=(nx,),
                 in_specs=[
                     pl.BlockSpec(
-                        block, lambda i, at: (0, at[2 + i], at[2 + places + i], 0, 0, 0)
+                        (1, 1, ny, nz, part, LANES), lambda i, at: (0, at[3 + i], 0, 0, 0, 0)
                     ),
                     pl.BlockSpec(
-                        block, lambda i, at: (1, at[2 + places + i], at[2 + i], 0, 0, 0)
+                        (1, ny, 1, nz, part, LANES), lambda i, at: (1, 0, at[3 + i], 0, 0, 0)
                     ),
                 ]
                 + [pl.BlockSpec(b.shape, lambda i, at: (0, 0)) for b in biases]
                 + [hbm] * len(earlier),
                 out_specs=[
-                    pl.BlockSpec((1, 1, nz * in_size, ch), lambda i, at: (at[0], i, 0, 0)),
+                    pl.BlockSpec((1, ny, nz * in_size, ch), lambda i, at: (at[0], i, 0, 0)),
                     pl.BlockSpec(
-                        (NL, 1, nz * conv_size, ch // 2), lambda i, at: (0, i, 0, at[0])
+                        (NL, ny, nz * conv_size, ch // 2), lambda i, at: (0, i, 0, at[0])
                     ),
                 ]
                 + [pl.BlockSpec(b.shape, lambda i, at, n=len(b.shape): (0,) * n) for b in spare],

time: 229 us -> 218 us (0.952)
  Pallas kernels: 49.9 us -> 39.2 us
    pallas_call x2, Pallas kernels: 22.8 us -> 12.1 us  [unpack(): pl.pallas_call(functools.partial(unpack_kernel, (in_size, conv_size, nb,...]
  transfers between devices with their start and end apart: 25 -> 25, of which waited for: 12 -> 12; matrix products, arithmetic and copies ran while one was open for 3% -> 3% of each run, Pallas kernels for 8% -> 6%
where the time goes in v9:
time: 218 us; the launch traced here: 217 us
  blocking collectives  102 us (47%)
  starting transfers between devices  39.5 us (18%)
  Pallas kernels  39.2 us (18%)
  waiting for transfers between devices  27.3 us (13%)
  matrix products  5.05 us (2%)
  other arithmetic  2.88 us (1%)
    all_to_all x3, blocking collectives, exchange(): return lax.all_to_all(value, PEERS, 0, 0, tiled=True)  102 us
    ppermute x8, starting transfers between devices, swap_core(): return lax.ppermute(value, 'c', [(0, 1), (1, 0)])  18.5 us
    pallas_call x1, Pallas kernels, per_device(): pl.pallas_call(functools.partial(step_kernel, dims), out_shape=[sds((8, L...  12.7 us
    pallas_call x2, Pallas kernels, unpack(): pl.pallas_call(functools.partial(unpack_kernel, (in_size, conv_size, nb,...  12.1 us
    ppermute x6, waiting for transfers between devices, spin(): return lax.ppermute(value, 'x', [(i, (i + steps) % n) for i in range(n)])  11.4 us
    ppermute x9, starting transfers between devices, spin(): return lax.ppermute(value, 'tm', pairs)  10.8 us
    ppermute x9, waiting for transfers between devices, spin(): return lax.ppermute(value, 'tm', pairs)  9.61 us
    pallas_call x3, Pallas kernels, call(): pl.pallas_call(kernel, out_shape=outs, in_specs=specs, out_specs=[pl.Bloc...  7.35 us
  transfers between devices with their start and end apart: 25, of which 12 were waited for; matrix products, arithmetic and copies ran while one was open for 3% of the time, Pallas kernels for 6%

profile of v9, /device:TPU:1, one launch (start us, length us, event | category | flops | bytes accessed | tf_op | source)
XLA Modules:
  0.0 217.1 jit_solution(13742132681291415141)
XLA Ops:
  0.6 1.5 collective-permute-start.4
  2.1 5.1 %fusion.5 = (bf16[256,512]{1,0:T(8,128)(2,1)S(1)}, f32[256,512]{1,0:T(8,128)}) fusion(f32[512]{0:T(512)} %param.7, bf16[4096,512]{1,0:T(8,128)(2,1)} %param.6, bf16[1,256,4096]{2,1,0:T(8,128)(2,1)} %param.5), kind=kOutput, calls=%fused_computation.23 | convolution fusion | flops 1074003968 | bytes 7079936 | tf_op jit(solution)/shard_map/dot_general | solution.py:494
  7.2 1.3 collective-permute-start.1
  8.5 4.3 %collective-permute-start = (bf16[32,512]{1,0:T(8,128)(2,1)S(1)}, bf16[32,512]{1,0:T(8,128)(2,1)S(1)}, u32[]{:S(2)}, u32[]{:S(2)}) collective-permute-start(bf16[32,512]{1,0:T(8,128)(2,1)S(1)} %get-tuple-element.64), channel_id=1, source_target_pairs={{0,1},{1,2},{2,3},{3,4},{4,5},{5,6},{6,7},{7,8},{8,9},{9,10},{10,1... | collective-permute-start | bytes 98312 | tf_op jit(solution)/shard_map/ppermute | solution.py:46
  12.8 0.9 collective-permute-done.before
  13.8 3.9 %shard_map.92 = (bf16[4,320,512]{2,1,0:T(8,128)(2,1)S(1)}, f32[3,320,512]{2,1,0:T(8,128)S(1)}, f32[64,48,128]{2,1,0:T(8,128)S(1)}, bf16[64,48,128]{2,1,0:T(8,128)(2,1)S(1)}, f32[8,512]{1,0:T(8,128)S(1)}) custom-call(s32[3]{0:T(128)S(1)} %pad_add_fusion.info, bf16[32,512]{1,0:T(8,128)(2,1)S(1)} %collective-permute-done.before, ...), custom_call_target="tpu_custom_call" | custom-call | tf_op jit(solution)/shard_map/pallas_call | solution.py:87
  17.7 1.0 collective-permute-start.2
  18.8 1.8 collective-permute-done.3.sib
  20.6 2.0 shard_map.93
  22.6 31.0 %all_to_all.15.arrived = bf16[64,64,128]{2,1,0:T(8,128)(2,1)S(1)} all-to-all(bf16[64,64,128]{2,1,0:T(8,128)(2,1)S(1)} %shard_map.93), channel_id=1, replica_groups=mesh['x'=4,'c'=2,'tm'=16] {'x','tm'}, dimensions={0} | all-to-all | bytes 2097152 | tf_op jit(solution)/shard_map/all_to_all | solution.py:80
  53.6 1.5 shard_map.94
  55.0 19.0 %all_to_all.16.half_cov = bf16[64,48,128]{2,1,0:T(8,128)(2,1)S(1)} all-to-all(bf16[64,48,128]{2,1,0:T(8,128)(2,1)S(1)} %get-tuple-element.39), channel_id=1, replica_groups=mesh['x'=4,'c'=2,'tm'=16] {'x','tm'}, dimensions={0} | all-to-all | bytes 1572864 | tf_op jit(solution)/shard_map/all_to_all | solution.py:80
  74.0 3.1 %collective-permute-start.5 = (bf16[64,48,128]{2,1,0:T(8,128)(2,1)S(1)}, bf16[64,48,128]{2,1,0:T(8,128)(2,1)S(1)}, u32[]{:S(2)}, u32[]{:S(2)}) collective-permute-start(bf16[64,48,128]{2,1,0:T(8,128)(2,1)S(1)} %all_to_all.16.half_cov), channel_id=1, source_target_pairs={{0,16},{16,0},{1,17},{17,1},{2,18},{18,2},{3,19},{19,3},{4,20},{20... | collective-permute-start | bytes 2359304 | tf_op jit(solution)/shard_map/ppermute | solution.py:40
  77.2 1.9 collective-permute-done.5.other_cov
  79.1 12.7 %shard_map.95 = (f32[8,128]{1,0:T(8,128)S(1)}, bf16[64,112,128]{2,1,0:T(8,128)(2,1)S(1)}, bf16[64,112,128]{2,1,0:T(8,128)(2,1)S(1)}, bf16[256,512]{1,0:T(8,128)(2,1)S(1)}) custom-call(s32[3]{0:T(128)S(1)} %pad_add_fusion.info, bf16[64,48,128]{2,1,0:T(8,128)(2,1)S(1)} %all_to_all.16.half_cov, bf16[64,48,128]{2,1,0:T(8,128)(2,1)S(1)} %collective-permute-done.5.other_cov, ...), custom_call_target="tpu_custom_call" | custom-call | tf_op jit(solution)/shard_map/pallas_call | solution.py:543
  91.8 0.4 collective-permute-start.7
  92.2 0.1 collective-permute-start.6
  92.4 2.0 shard_map.96.earlier
  94.4 1.7 collective-permute-done.6.dpre_got
  96.0 3.9 %shard_map.97 = bf16[64,240,128]{2,1,0:T(8,128)(2,1)S(1)} custom-call(s32[3]{0:T(128)S(1)} %pad_add_fusion.info, f32[2048,512]{1,0:T(8,128)S(1)} %shard_map.96.earlier, bf16[256,4096]{1,0:T(8,128)(2,1)} %collective-permute-done.4.left_got, bf16[256,512]{1,0:T(8,128)(2,1)S(1)} %collective-permute-done.6.dpre_got, ...), custom_call_target="tpu_custom_call" | custom-call | tf_op jit(solution)/shard_map/pallas_call | solution.py:586
  99.9 51.6 %all_to_all.17.arrived = bf16[64,240,128]{2,1,0:T(8,128)(2,1)S(1)} all-to-all(bf16[64,240,128]{2,1,0:T(8,128)(2,1)S(1)} %shard_map.97), channel_id=1, replica_groups=mesh['x'=4,'c'=2,'tm'=16] {'x','tm'}, dimensions={0} | all-to-all | bytes 7864320 | tf_op jit(solution)/shard_map/all_to_all | solution.py:80
  151.5 1.3 shard_map.98
  152.8 1.6 collective-permute-start.9
  154.4 2.1 collective-permute-start.10
  156.6 2.7 %collective-permute-done.8 = bf16[2,112,128]{2,1,0:T(8,128)(2,1)S(1)} collective-permute-done((bf16[2,112,128]{2,1,0:T(8,128)(2,1)S(1)}, bf16[2,112,128]{2,1,0:T(8,128)(2,1)S(1)}, u32[]{:S(2)}, u32[]{:S(2)}) %collective-permute-start.8) | collective-permute-done | bytes 57376 | tf_op jit(solution)/shard_map/ppermute | solution.py:65
  159.4 1.1 collective-permute-start.13
  160.5 3.0 %collective-permute-start.12 = (bf16[4,112,128]{2,1,0:T(8,128)(2,1)S(1)}, bf16[4,112,128]{2,1,0:T(8,128)(2,1)S(1)}, u32[]{:S(2)}, u32[]{:S(2)}) collective-permute-start(bf16[4,112,128]{2,1,0:T(8,128)(2,1)S(1)} %get-tuple-element.66), channel_id=1, source_target_pairs={{0,12},{1,13},{2,14},{3,15},{4,0},{5,1},{6,2},{7,3},{8,4},{9,5},{1... | collective-permute-start | bytes 344072 | tf_op jit(solution)/shard_map/ppermute | solution.py:65
  163.5 1.5 collective-permute-start.16
  165.0 1.2 collective-permute-start.15
  166.2 0.2 collective-permute-start.14
  166.5 3.2 %collective-permute-done.11 = bf16[4,112,128]{2,1,0:T(8,128)(2,1)S(1)} collective-permute-done((bf16[4,112,128]{2,1,0:T(8,128)(2,1)S(1)}, bf16[4,112,128]{2,1,0:T(8,128)(2,1)S(1)}, u32[]{:S(2)}, u32[]{:S(2)}) %collective-permute-start.11) | collective-permute-done | bytes 114720 | tf_op jit(solution)/shard_map/ppermute | solution.py:65
  169.8 1.6 collective-permute-done.14
  171.5 1.2 collective-permute-start.18
  172.7 0.3 collective-permute-start.17
  173.1 2.0 collective-permute-start.22
  175.1 0.9 collective-permute-start.21
  176.0 4.5 %collective-permute-done.19 = bf16[4,4,112,128]{3,2,1,0:T(8,128)(2,1)S(1)} collective-permute-done((bf16[4,4,112,128]{3,2,1,0:T(8,128)(2,1)S(1)}, bf16[4,4,112,128]{3,2,1,0:T(8,128)(2,1)S(1)}, u32[]{:S(2)}, u32[]{:S(2)}) %collective-permute-start.19) | collective-permute-done | bytes 458784 | tf_op jit(solution)/shard_map/ppermute | solution.py:59
  180.5 2.7 %collective-permute-done.18 = bf16[4,4,112,128]{3,2,1,0:T(8,128)(2,1)S(1)} collective-permute-done((bf16[4,4,112,128]{3,2,1,0:T(8,128)(2,1)S(1)}, bf16[4,4,112,128]{3,2,1,0:T(8,128)(2,1)S(1)}, u32[]{:S(2)}, u32[]{:S(2)}) %collective-permute-start.18) | collective-permute-done | bytes 458784 | tf_op jit(solution)/shard_map/ppermute | solution.py:59
  183.2 2.6 %collective-permute-done.17 = bf16[4,4,112,128]{3,2,1,0:T(8,128)(2,1)S(1)} collective-permute-done((bf16[4,4,112,128]{3,2,1,0:T(8,128)(2,1)S(1)}, bf16[4,4,112,128]{3,2,1,0:T(8,128)(2,1)S(1)}, u32[]{:S(2)}, u32[]{:S(2)}) %collective-permute-start.17) | collective-permute-done | bytes 458784 | tf_op jit(solution)/shard_map/ppermute | solution.py:59
  185.8 0.2 maximum_bitcast_fusion
  186.0 2.1 collective-permute-done.21
  188.1 1.6 collective-permute-done.20
  189.7 0.2 maximum_bitcast_fusion.1
  189.9 2.1 pad_maximum_fusion.left.right
  192.0 12.2 %collective-permute-start.23 = (bf16[2,4,4,4,112,128]{5,4,3,2,1,0:T(8,128)(2,1)}, bf16[2,4,4,4,112,128]{5,4,3,2,1,0:T(8,128)(2,1)}, u32[]{:S(2)}, u32[]{:S(2)}) collective-permute-start(bf16[2,4,4,4,112,128]{5,4,3,2,1,0:T(8,128)(2,1)} %pad_maximum_fusion.left.right), channel_id=1, source_target_pairs={{0,16},{16,0},{1,17},{17,1},{2,18},{18,2},{3,19},{19,3},{4,20},{20... | collective-permute-start | bytes 11010056 | tf_op jit(solution)/shard_map/ppermute | solution.py:40
  204.3 0.5 slice.17
  204.9 6.0 %shard_map.99 = (f32[2,16,128,512]{3,2,1,0:T(8,128)}, f32[3,16,64,512]{3,2,1,0:T(8,128)}) custom-call(s32[7]{0:T(128)S(1)} %get-tuple-element.71.info, bf16[2,4,4,4,112,128]{5,4,3,2,1,0:T(8,128)(2,1)} %pad_maximum_fusion.left.right, bf16[2,4,4,4,112,128]{5,4,3,2,1,0:T(8,128)(2,1)} %pad_maximum_fusion.left.right), custom_call_target="tpu_custom_call" | custom-call | bytes 12582912 | tf_op jit(solution)/shard_map/pallas_call | solution.py:627
  210.9 6.1 %shard_map.100 = (f32[2,16,128,512]{3,2,1,0:T(8,128)}, f32[3,16,64,512]{3,2,1,0:T(8,128)}, f32[512]{0:T(512)}, f32[3,512]{1,0:T(4,128)}) custom-call(s32[7]{0:T(128)S(1)} %get-tuple-element.72.info, bf16[2,4,4,4,112,128]{5,4,3,2,1,0:T(8,128)(2,1)} %collective-permute-done.23.left.right, ...), custom_call_target="tpu_custom_call", output_to_operand_aliasing={{0}: (5, {}), {1}: (6, {})} | custom-call | bytes 12582912 | tf_op jit(solution)/shard_map/pallas_call | solution.py:627
  (36 shorter events, 0.7 us)
Async XLA Ops:
  0.6 13.1 %copy-start.3 = (f32[3,512]{1,0:T(4,128)S(1)}, f32[3,512]{1,0:T(4,128)}, u32[]{:S(2)}) copy-start(f32[3,512]{1,0:T(4,128)} %b.1) | copy-start | bytes 18436
  0.6 20.0 %collective-permute-start.4 = (bf16[256,4096]{1,0:T(8,128)(2,1)}, bf16[256,4096]{1,0:T(8,128)(2,1)}, u32[]{:S(2)}, u32[]{:S(2)}) collective-permute-start(bf16[256,4096]{1,0:T(8,128)(2,1)} %bitcast.54), channel_id=1, source_target_pairs={{0,16},{16,0},{1,17},{17,1},{2,18},{18,2},{3,19},{19,3},{4,20},{20... | collective-permute-start | bytes 6291464 | tf_op jit(solution)/shard_map/ppermute | solution.py:40
  2.1 11.6 %copy-start = (bf16[3,1024,512]{2,1,0:T(8,128)(2,1)S(1)}, bf16[3,1024,512]{2,1,0:T(8,128)(2,1)}, u32[]{:S(2)}) copy-start(bf16[3,1024,512]{2,1,0:T(8,128)(2,1)} %w_hbm.1) | copy-start | bytes 9437188
  7.2 5.6 %collective-permute-start.1 = (bf16[32,512]{1,0:T(8,128)(2,1)S(1)}, bf16[32,512]{1,0:T(8,128)(2,1)S(1)}, u32[]{:S(2)}, u32[]{:S(2)}) collective-permute-start(bf16[32,512]{1,0:T(8,128)(2,1)S(1)} %get-tuple-element.63), channel_id=1, source_target_pairs={{1,0},{2,1},{3,2},{4,3},{5,4},{6,5},{7,6},{8,7},{9,8},{10,9},{11,1... | collective-permute-start | bytes 98312 | tf_op jit(solution)/shard_map/ppermute | solution.py:46
  8.5 5.3 %collective-permute-start = (bf16[32,512]{1,0:T(8,128)(2,1)S(1)}, bf16[32,512]{1,0:T(8,128)(2,1)S(1)}, u32[]{:S(2)}, u32[]{:S(2)}) collective-permute-start(bf16[32,512]{1,0:T(8,128)(2,1)S(1)} %get-tuple-element.64), channel_id=1, source_target_pairs={{0,1},{1,2},{2,3},{3,4},{4,5},{5,6},{6,7},{7,8},{8,9},{9,10},{10,1... | collective-permute-start | bytes 98312 | tf_op jit(solution)/shard_map/ppermute | solution.py:46
  17.7 2.9 %collective-permute-start.2 = (bf16[64,48,128]{2,1,0:T(8,128)(2,1)S(1)}, bf16[64,48,128]{2,1,0:T(8,128)(2,1)S(1)}, u32[]{:S(2)}, u32[]{:S(2)}) collective-permute-start(bf16[64,48,128]{2,1,0:T(8,128)(2,1)S(1)} %get-tuple-element.35), channel_id=1, source_target_pairs={{0,16},{16,0},{1,17},{17,1},{2,18},{18,2},{3,19},{19,3},{4,20},{20... | collective-permute-start | bytes 2359304 | tf_op jit(solution)/shard_map/ppermute | solution.py:40
  18.7 1.9 collective-permute-start.3
  22.6 56.5 %copy-start.2 = (f32[256,512]{1,0:T(8,128)S(1)}, f32[256,512]{1,0:T(8,128)}, u32[]{:S(2)}) copy-start(f32[256,512]{1,0:T(8,128)} %get-tuple-element.74.sq0_hbm) | copy-start | bytes 1572868
  74.0 5.1 %collective-permute-start.5 = (bf16[64,48,128]{2,1,0:T(8,128)(2,1)S(1)}, bf16[64,48,128]{2,1,0:T(8,128)(2,1)S(1)}, u32[]{:S(2)}, u32[]{:S(2)}) collective-permute-start(bf16[64,48,128]{2,1,0:T(8,128)(2,1)S(1)} %all_to_all.16.half_cov), channel_id=1, source_target_pairs={{0,16},{16,0},{1,17},{17,1},{2,18},{18,2},{3,19},{19,3},{4,20},{20... | collective-permute-start | bytes 2359304 | tf_op jit(solution)/shard_map/ppermute | solution.py:40
  79.1 13.3 %copy-start.1 = (bf16[1,256,4096]{2,1,0:T(8,128)(2,1)S(1)}, bf16[1,256,4096]{2,1,0:T(8,128)(2,1)}, u32[]{:S(2)}) copy-start(bf16[1,256,4096]{2,1,0:T(8,128)(2,1)} %param.5) | copy-start | bytes 6291460
  91.8 4.2 %collective-permute-start.7 = (bf16[64,112,128]{2,1,0:T(8,128)(2,1)S(1)}, bf16[64,112,128]{2,1,0:T(8,128)(2,1)S(1)}, u32[]{:S(2)}, u32[]{:S(2)}) collective-permute-start(bf16[64,112,128]{2,1,0:T(8,128)(2,1)S(1)} %get-tuple-element.47), channel_id=1, source_target_pairs={{0,16},{16,0},{1,17},{17,1},{2,18},{18,2},{3,19},{19,3},{4,20},{20... | collective-permute-start | bytes 5505032 | tf_op jit(solution)/shard_map/ppermute | solution.py:40
  92.2 3.8 %collective-permute-start.6 = (bf16[256,512]{1,0:T(8,128)(2,1)S(1)}, bf16[256,512]{1,0:T(8,128)(2,1)S(1)}, u32[]{:S(2)}, u32[]{:S(2)}) collective-permute-start(bf16[256,512]{1,0:T(8,128)(2,1)S(1)} %get-tuple-element.44.dpre), channel_id=1, source_target_pairs={{0,16},{16,0},{1,17},{17,1},{2,18},{18,2},{3,19},{19,3},{4,20},{20... | collective-permute-start | bytes 786440 | tf_op jit(solution)/shard_map/ppermute | solution.py:40
  152.8 3.8 %collective-permute-start.9 = (bf16[2,112,128]{2,1,0:T(8,128)(2,1)S(1)}, bf16[2,112,128]{2,1,0:T(8,128)(2,1)S(1)}, u32[]{:S(2)}, u32[]{:S(2)}) collective-permute-start(bf16[2,112,128]{2,1,0:T(8,128)(2,1)S(1)} %get-tuple-element.70), channel_id=1, source_target_pairs={{0,3},{1,0},{2,1},{3,2},{4,7},{5,4},{6,5},{7,6},{8,11},{9,8},{10,9... | collective-permute-start | bytes 172040 | tf_op jit(solution)/shard_map/ppermute | solution.py:65
  154.4 4.9 %collective-permute-start.8 = (bf16[2,112,128]{2,1,0:T(8,128)(2,1)S(1)}, bf16[2,112,128]{2,1,0:T(8,128)(2,1)S(1)}, u32[]{:S(2)}, u32[]{:S(2)}) collective-permute-start(bf16[2,112,128]{2,1,0:T(8,128)(2,1)S(1)} %get-tuple-element.70), channel_id=1, source_target_pairs={{0,1},{1,2},{2,3},{3,0},{4,5},{5,6},{6,7},{7,4},{8,9},{9,10},{10,1... | collective-permute-start | bytes 172040 | tf_op jit(solution)/shard_map/ppermute | solution.py:65
  154.4 4.9 %collective-permute-start.10 = (bf16[2,112,128]{2,1,0:T(8,128)(2,1)S(1)}, bf16[2,112,128]{2,1,0:T(8,128)(2,1)S(1)}, u32[]{:S(2)}, u32[]{:S(2)}) collective-permute-start(bf16[2,112,128]{2,1,0:T(8,128)(2,1)S(1)} %get-tuple-element.70), channel_id=1, source_target_pairs={{0,2},{1,3},{2,0},{3,1},{4,6},{5,7},{6,4},{7,5},{8,10},{9,11},{10,... | collective-permute-start | bytes 172040 | tf_op jit(solution)/shard_map/ppermute | solution.py:65
  159.4 6.8 %collective-permute-start.13 = (bf16[4,112,128]{2,1,0:T(8,128)(2,1)S(1)}, bf16[4,112,128]{2,1,0:T(8,128)(2,1)S(1)}, u32[]{:S(2)}, u32[]{:S(2)}) collective-permute-start(bf16[4,112,128]{2,1,0:T(8,128)(2,1)S(1)} %get-tuple-element.66), channel_id=1, source_target_pairs={{0,8},{1,9},{2,10},{3,11},{4,12},{5,13},{6,14},{7,15},{8,0},{9,1},... | collective-permute-start | bytes 344072 | tf_op jit(solution)/shard_map/ppermute | solution.py:65
  160.5 6.0 %collective-permute-start.12 = (bf16[4,112,128]{2,1,0:T(8,128)(2,1)S(1)}, bf16[4,112,128]{2,1,0:T(8,128)(2,1)S(1)}, u32[]{:S(2)}, u32[]{:S(2)}) collective-permute-start(bf16[4,112,128]{2,1,0:T(8,128)(2,1)S(1)} %get-tuple-element.66), channel_id=1, source_target_pairs={{0,12},{1,13},{2,14},{3,15},{4,0},{5,1},{6,2},{7,3},{8,4},{9,5},{1... | collective-permute-start | bytes 344072 | tf_op jit(solution)/shard_map/ppermute | solution.py:65
  163.5 6.2 %collective-permute-start.11 = (bf16[4,112,128]{2,1,0:T(8,128)(2,1)S(1)}, bf16[4,112,128]{2,1,0:T(8,128)(2,1)S(1)}, u32[]{:S(2)}, u32[]{:S(2)}) collective-permute-start(bf16[4,112,128]{2,1,0:T(8,128)(2,1)S(1)} %get-tuple-element.66), channel_id=1, source_target_pairs={{0,4},{1,5},{2,6},{3,7},{4,8},{5,9},{6,10},{7,11},{8,12},{9,13},{1... | collective-permute-start | bytes 344072 | tf_op jit(solution)/shard_map/ppermute | solution.py:65
  163.5 6.3 %collective-permute-start.16 = (bf16[4,112,128]{2,1,0:T(8,128)(2,1)S(1)}, bf16[4,112,128]{2,1,0:T(8,128)(2,1)S(1)}, u32[]{:S(2)}, u32[]{:S(2)}) collective-permute-start(bf16[4,112,128]{2,1,0:T(8,128)(2,1)S(1)} %get-tuple-element.67), channel_id=1, source_target_pairs={{0,64},{32,96},{64,0},{96,32},{1,65},{33,97},{65,1},{97,33},{2,66}... | collective-permute-start | bytes 344072 | tf_op jit(solution)/shard_map/ppermute | solution.py:59
  165.0 4.8 %collective-permute-start.15 = (bf16[4,112,128]{2,1,0:T(8,128)(2,1)S(1)}, bf16[4,112,128]{2,1,0:T(8,128)(2,1)S(1)}, u32[]{:S(2)}, u32[]{:S(2)}) collective-permute-start(bf16[4,112,128]{2,1,0:T(8,128)(2,1)S(1)} %get-tuple-element.67), channel_id=1, source_target_pairs={{0,96},{32,0},{64,32},{96,64},{1,97},{33,1},{65,33},{97,65},{2,98}... | collective-permute-start | bytes 344072 | tf_op jit(solution)/shard_map/ppermute | solution.py:59
  166.2 5.1 %collective-permute-start.14 = (bf16[4,112,128]{2,1,0:T(8,128)(2,1)S(1)}, bf16[4,112,128]{2,1,0:T(8,128)(2,1)S(1)}, u32[]{:S(2)}, u32[]{:S(2)}) collective-permute-start(bf16[4,112,128]{2,1,0:T(8,128)(2,1)S(1)} %get-tuple-element.67), channel_id=1, source_target_pairs={{0,32},{32,64},{64,96},{96,0},{1,33},{33,65},{65,97},{97,1},{2,34}... | collective-permute-start | bytes 344072 | tf_op jit(solution)/shard_map/ppermute | solution.py:59
  171.4 9.0 %collective-permute-start.19 = (bf16[4,4,112,128]{3,2,1,0:T(8,128)(2,1)S(1)}, bf16[4,4,112,128]{3,2,1,0:T(8,128)(2,1)S(1)}, u32[]{:S(2)}, u32[]{:S(2)}) collective-permute-start(bf16[4,4,112,128]{3,2,1,0:T(8,128)(2,1)S(1)} %pad_maximum_fusion.1), channel_id=1, source_target_pairs={{0,64},{32,96},{64,0},{96,32},{1,65},{33,97},{65,1},{97,33},{2,66}... | collective-permute-start | bytes 1376264 | tf_op jit(solution)/shard_map/ppermute | solution.py:59
  171.5 11.6 %collective-permute-start.18 = (bf16[4,4,112,128]{3,2,1,0:T(8,128)(2,1)S(1)}, bf16[4,4,112,128]{3,2,1,0:T(8,128)(2,1)S(1)}, u32[]{:S(2)}, u32[]{:S(2)}) collective-permute-start(bf16[4,4,112,128]{3,2,1,0:T(8,128)(2,1)S(1)} %pad_maximum_fusion.1), channel_id=1, source_target_pairs={{0,96},{32,0},{64,32},{96,64},{1,97},{33,1},{65,33},{97,65},{2,98}... | collective-permute-start | bytes 1376264 | tf_op jit(solution)/shard_map/ppermute | solution.py:59
  172.7 13.0 %collective-permute-start.17 = (bf16[4,4,112,128]{3,2,1,0:T(8,128)(2,1)S(1)}, bf16[4,4,112,128]{3,2,1,0:T(8,128)(2,1)S(1)}, u32[]{:S(2)}, u32[]{:S(2)}) collective-permute-start(bf16[4,4,112,128]{3,2,1,0:T(8,128)(2,1)S(1)} %pad_maximum_fusion.1), channel_id=1, source_target_pairs={{0,32},{32,64},{64,96},{96,0},{1,33},{33,65},{65,97},{97,1},{2,34}... | collective-permute-start | bytes 1376264 | tf_op jit(solution)/shard_map/ppermute | solution.py:59
  173.1 13.0 %collective-permute-start.22 = (bf16[4,4,112,128]{3,2,1,0:T(8,128)(2,1)S(1)}, bf16[4,4,112,128]{3,2,1,0:T(8,128)(2,1)S(1)}, u32[]{:S(2)}, u32[]{:S(2)}) collective-permute-start(bf16[4,4,112,128]{3,2,1,0:T(8,128)(2,1)S(1)} %pad_maximum_fusion.2), channel_id=1, source_target_pairs={{0,8},{1,9},{2,10},{3,11},{4,12},{5,13},{6,14},{7,15},{8,0},{9,1},... | collective-permute-start | bytes 1376264 | tf_op jit(solution)/shard_map/ppermute | solution.py:65
  175.1 13.0 %collective-permute-start.21 = (bf16[4,4,112,128]{3,2,1,0:T(8,128)(2,1)S(1)}, bf16[4,4,112,128]{3,2,1,0:T(8,128)(2,1)S(1)}, u32[]{:S(2)}, u32[]{:S(2)}) collective-permute-start(bf16[4,4,112,128]{3,2,1,0:T(8,128)(2,1)S(1)} %pad_maximum_fusion.2), channel_id=1, source_target_pairs={{0,12},{1,13},{2,14},{3,15},{4,0},{5,1},{6,2},{7,3},{8,4},{9,5},{1... | collective-permute-start | bytes 1376264 | tf_op jit(solution)/shard_map/ppermute | solution.py:65
  180.5 9.2 %collective-permute-start.20 = (bf16[4,4,112,128]{3,2,1,0:T(8,128)(2,1)S(1)}, bf16[4,4,112,128]{3,2,1,0:T(8,128)(2,1)S(1)}, u32[]{:S(2)}, u32[]{:S(2)}) collective-permute-start(bf16[4,4,112,128]{3,2,1,0:T(8,128)(2,1)S(1)} %pad_maximum_fusion.2), channel_id=1, source_target_pairs={{0,4},{1,5},{2,6},{3,7},{4,8},{5,9},{6,10},{7,11},{8,12},{9,13},{1... | collective-permute-start | bytes 1376264 | tf_op jit(solution)/shard_map/ppermute | solution.py:65
  192.0 18.9 %collective-permute-start.23 = (bf16[2,4,4,4,112,128]{5,4,3,2,1,0:T(8,128)(2,1)}, bf16[2,4,4,4,112,128]{5,4,3,2,1,0:T(8,128)(2,1)}, u32[]{:S(2)}, u32[]{:S(2)}) collective-permute-start(bf16[2,4,4,4,112,128]{5,4,3,2,1,0:T(8,128)(2,1)} %pad_maximum_fusion.left.right), channel_id=1, source_target_pairs={{0,16},{16,0},{1,17},{17,1},{2,18},{18,2},{3,19},{19,3},{4,20},{20... | collective-permute-start | bytes 11010056 | tf_op jit(solution)/shard_map/ppermute | solution.py:40
  204.2 6.7 %collective-permute-start.24 = (f32[8,128]{1,0:T(8,128)S(1)}, f32[8,128]{1,0:T(8,128)S(1)}, u32[]{:S(2)}, u32[]{:S(2)}) collective-permute-start(f32[8,128]{1,0:T(8,128)S(1)} %get-tuple-element.54.refs_0_), channel_id=1, source_target_pairs={{0,16},{16,0},{1,17},{17,1},{2,18},{18,2},{3,19},{19,3},{4,20},{20... | collective-permute-start | bytes 12296 | tf_op jit(solution)/shard_map/ppermute | solution.py:40
